TPU v7x, 128 devices: a whole 4x4x4 slice. The times are simulated.
128 devices in a mesh: dp: 8 (over x, core), tensor: 16 (over y, z).
Axes of the slice: x: 4, y: 4, z: 4, core: 2. Of those that a mesh axis runs over, the one named last changes fastest.
Arguments:
- hidden_input: bfloat16 [512, 8192], P('dp', 'tensor'), may hold values from -6 to 6
- query_projection_weight: bfloat16 [8192, 8192], P(None, 'tensor'), may hold values from -0.0625 to 0.0625
- key_projection_weight: bfloat16 [8192, 1024], P(None, 'tensor'), may hold values from -0.0625 to 0.0625
- value_projection_weight: bfloat16 [8192, 1024], P(None, 'tensor'), may hold values from -0.0625 to 0.0625
- adapter_down_maps: bfloat16 [512, 24, 8192], P(('dp', 'tensor')), may hold values from -0.0625 to 0.0625
- adapter_up_maps: bfloat16 [512, 8, 10240], P(('dp', 'tensor')), may hold values from -2 to 2
- key_cache_blocks: bfloat16 [16, 256, 512, 128], P('tensor', 'dp'), may hold values from -240 to 240
- value_cache_blocks: bfloat16 [16, 256, 512, 128], P('tensor', 'dp'), may hold values from -6 to 6
- filled: int32 [512], P('dp'), may hold values from 5 to 512, as said below
- positions: int32 [512], P('dp'), may hold values from 512 to 1023
- requests: int32 [8, 63], P('dp'), may hold values from 0 to 511, as said below
- session_request_slot: int32 [512], P('dp'), may hold values from 0 to 62, as said below
Outputs:
- attended: bfloat16 [512, 8192], P('dp', 'tensor')
- new_keys: bfloat16 [512, 1024], P('dp', 'tensor')
- fresh_values: bfloat16 [512, 1024], P('dp', 'tensor')
Inputs may be any that keep to these rules, and one draw needn't show every extreme that they name: Slots below filled hold a session's keys and values, the 4 sinks first; at least one session uses all 512 slots. `requests`: A row lists 63 different adapters of one session group, no two on one device; adapter a lies on device a // 4 of dp+tensor. `session_request_slot`: every entry of a group's list is used; entry 0 by 2 sessions of the group, every other entry by 1.
All inputs are finite; a program needn't handle non-finite values.
Results may differ from a plain program's by a relative error of at most 0.012.
The roundings to bfloat16 on the way count: a program that leaves them out, or rounds other values in their place, can miss the bound.
Values may be sent and summed in bfloat16 or wider, within the bound.
No kernel may reach another device: no remote copies, remote signals or barrier semaphores. Data moves between devices by JAX's collectives and lax.ppermute only.
A program may use at most 128 MiB of HBM per device.

v0:
```python
import math

import jax
import jax.numpy as jnp
from jax import lax
from jax.sharding import PartitionSpec as P

HEAD_SIZE = 128
ADAPTER_RANK = 8
RCAP = 1


THETA = 500000.0


def from_partner(block, axis, apart):
    count = lax.axis_size(axis)
    route = []
    for low in range(count):
        high = low | 1 << apart
        if high != low and high < count:
            route += [(low, high), (high, low)]
    return lax.ppermute(block, axis, route)


def apply_rotation(vector, positions_in):
    head_width = vector.shape[-1]
    half_width = head_width // 2
    frequency = THETA ** (-2.0 * jnp.arange(half_width, dtype=jnp.float32) / head_width)
    phase_angle = positions_in.astype(jnp.float32)[:, None, None] * frequency[None, None, :]
    cosine = jnp.cos(phase_angle)
    sine_part = jnp.sin(phase_angle)
    lower_half = vector[..., :half_width]
    upper_half = vector[..., half_width:]
    return jnp.concatenate(
        [
            lower_half * cosine - upper_half * sine_part,
            upper_half * cosine + lower_half * sine_part,
        ],
        axis=-1,
    )


def attend_block(query_rot, key_new, value_new, key_rows, value_rows, length):
    score_scale = 1.0 / math.sqrt(query_rot.shape[-1])
    scores = (
        jnp.einsum("sgd,scd->sgc", query_rot, key_rows, preferred_element_type=jnp.float32)
        * score_scale
    )
    own_score = (
        jnp.einsum("sgd,sd->sg", query_rot, key_new, preferred_element_type=jnp.float32)
        * score_scale
    )
    valid_slot = (jnp.arange(key_rows.shape[1])[None, :] < length[:, None])[:, None, :]
    top_score = jnp.maximum(jnp.max(jnp.where(valid_slot, scores, -jnp.inf), axis=-1), own_score)
    weights = jnp.where(valid_slot, jnp.exp(scores - top_score[..., None]), 0.0)
    own_weight = jnp.exp(own_score - top_score)
    denominator = jnp.sum(weights, axis=-1) + own_weight
    attention_output = jnp.einsum(
        "sgc,scd->sgd", weights.astype(jnp.bfloat16), value_rows, preferred_element_type=jnp.float32
    )
    own_rounded_state = lax.optimization_barrier(own_weight.astype(jnp.bfloat16)).astype(
        jnp.float32
    )
    attention_output = (
        attention_output + own_rounded_state[..., None] * value_new.astype(jnp.float32)[:, None, :]
    )
    return (attention_output / denominator[..., None]).astype(jnp.bfloat16)


def local(
    hidden_input,
    query_projection_weight,
    key_projection_weight,
    value_projection_weight,
    adapter_down_maps,
    adapter_up_maps,
    key_cache_blocks,
    value_cache_blocks,
    filled,
    positions,
    requests,
    session_request_slot,
):
    tensor_group_size = lax.axis_size("tensor")
    all_size = lax.axis_size(("dp", "tensor"))
    tensor_index = lax.axis_index("tensor")
    sessions = hidden_input.shape[0]
    feature_columns = hidden_input.shape[1]
    query_columns = query_projection_weight.shape[1]
    key_value_columns = key_projection_weight.shape[1]
    merged_cols = query_columns + 2 * key_value_columns
    pair_size = HEAD_SIZE // key_value_columns
    parity = tensor_index % pair_size
    holding_count = adapter_down_maps.shape[0]
    request_count = requests.shape[1]
    columns = lax.all_gather(hidden_input, "tensor", axis=1, tiled=True)
    base_query = jnp.dot(columns, query_projection_weight, preferred_element_type=jnp.float32)
    base_key = jnp.dot(columns, key_projection_weight, preferred_element_type=jnp.float32)
    base_value = jnp.dot(columns, value_projection_weight, preferred_element_type=jnp.float32)
    wanted = requests[0]
    slot_match = session_request_slot[:, None] == jnp.arange(request_count)[None, :]
    adapter_index = jnp.sum(jnp.where(slot_match, wanted[None, :], 0), axis=1)
    owner_dev = adapter_index // holding_count
    req_owner = wanted // holding_count
    req_local = wanted % holding_count
    earlier = jnp.arange(request_count)[None, :] < jnp.arange(request_count)[:, None]
    req_rank = jnp.sum(earlier & (req_owner[:, None] == req_owner[None, :]), axis=1)
    target = (jnp.arange(all_size)[:, None, None] == req_owner[None, None, :]) & (
        jnp.arange(RCAP)[None, :, None] == req_rank[None, None, :]
    )
    asked_table = jnp.sum(jnp.where(target, req_local[None, None, :] + 1, 0), axis=2) - 1
    down_table = (
        adapter_down_maps.reshape(
            holding_count, 3 * ADAPTER_RANK, tensor_group_size, feature_columns
        )
        .transpose(0, 2, 1, 3)
        .reshape(holding_count * tensor_group_size, 3 * ADAPTER_RANK, feature_columns)
    )
    query_total = query_columns * tensor_group_size
    key_value_total = key_value_columns * tensor_group_size
    query_up_map = adapter_up_maps[:, :, :query_total].reshape(
        holding_count, ADAPTER_RANK, tensor_group_size, query_columns
    )
    key_up_map = adapter_up_maps[:, :, query_total : query_total + key_value_total].reshape(
        holding_count, ADAPTER_RANK, tensor_group_size, key_value_columns
    )
    value_up_map = adapter_up_maps[:, :, query_total + key_value_total :].reshape(
        holding_count, ADAPTER_RANK, tensor_group_size, key_value_columns
    )
    up_table = (
        jnp.concatenate([query_up_map, key_up_map, value_up_map], axis=3)
        .transpose(0, 2, 1, 3)
        .reshape(holding_count * tensor_group_size, ADAPTER_RANK, merged_cols)
    )
    asked = lax.all_to_all(asked_table, ("dp", "tensor"), split_axis=0, concat_axis=0, tiled=True)
    source_tensor = (jnp.arange(asked.shape[0]) % tensor_group_size)[:, None]
    row_index = jnp.maximum(asked, 0) * tensor_group_size + source_tensor
    present = (asked >= 0)[..., None, None]
    down_pieces = jnp.where(present, jnp.take(down_table, row_index, axis=0), 0)
    up_pieces = jnp.where(present, jnp.take(up_table, row_index, axis=0), 0)
    down_got = lax.all_to_all(
        down_pieces, ("dp", "tensor"), split_axis=0, concat_axis=0, tiled=True
    )
    up_got = lax.all_to_all(up_pieces, ("dp", "tensor"), split_axis=0, concat_axis=0, tiled=True)
    sess_rank = jnp.sum(jnp.where(slot_match, req_rank[None, :], 0), axis=1)
    piece_index = owner_dev * RCAP + sess_rank
    down_chosen = jnp.take(
        down_got.reshape(all_size * RCAP, 3 * ADAPTER_RANK, feature_columns), piece_index, axis=0
    )
    up_chosen = jnp.take(
        up_got.reshape(all_size * RCAP, ADAPTER_RANK, merged_cols), piece_index, axis=0
    )
    partial_coords = jnp.einsum(
        "sf,srf->sr", hidden_input, down_chosen, preferred_element_type=jnp.float32
    )
    mesh_coordinates = lax.psum(partial_coords, "tensor").astype(jnp.bfloat16)
    low_query = jnp.einsum(
        "sr,src->sc",
        mesh_coordinates[:, :ADAPTER_RANK],
        up_chosen[:, :, :query_columns],
        preferred_element_type=jnp.float32,
    )
    low_key = jnp.einsum(
        "sr,src->sc",
        mesh_coordinates[:, ADAPTER_RANK : 2 * ADAPTER_RANK],
        up_chosen[:, :, query_columns : query_columns + key_value_columns],
        preferred_element_type=jnp.float32,
    )
    low_value = jnp.einsum(
        "sr,src->sc",
        mesh_coordinates[:, 2 * ADAPTER_RANK :],
        up_chosen[:, :, query_columns + key_value_columns :],
        preferred_element_type=jnp.float32,
    )
    query_full = base_query + low_query
    key_part = base_key + low_key
    value_part = base_value + low_value
    paired = query_full.reshape(sessions // 2, 2, query_columns)
    mine_rows = lax.dynamic_index_in_dim(paired, parity, 1, keepdims=False)
    given_rows = lax.dynamic_index_in_dim(paired, 1 - parity, 1, keepdims=False)
    partner_query, partner_key, partner_value = from_partner(
        (given_rows, key_part, value_part), "tensor", 0
    )
    lower_first = parity == 0
    group_query = jnp.where(
        lower_first,
        jnp.concatenate([mine_rows, partner_query], axis=1),
        jnp.concatenate([partner_query, mine_rows], axis=1),
    )
    key_full = jnp.where(
        lower_first,
        jnp.concatenate([key_part, partner_key], axis=1),
        jnp.concatenate([partner_key, key_part], axis=1),
    )
    value_full = jnp.where(
        lower_first,
        jnp.concatenate([value_part, partner_value], axis=1),
        jnp.concatenate([partner_value, value_part], axis=1),
    )
    key_round = (
        apply_rotation(key_full.reshape(sessions, 1, HEAD_SIZE), positions)
        .reshape(sessions, HEAD_SIZE)
        .astype(jnp.bfloat16)
    )
    new_keys = lax.dynamic_slice_in_dim(key_round, parity * key_value_columns, key_value_columns, 1)
    fresh_values = value_part.astype(jnp.bfloat16)
    value_round = value_full.astype(jnp.bfloat16)
    mine_count = sessions // pair_size
    positions_mine = lax.dynamic_index_in_dim(
        positions.reshape(mine_count, pair_size), parity, 1, keepdims=False
    )
    filled_mine = lax.dynamic_index_in_dim(
        filled.reshape(mine_count, pair_size), parity, 1, keepdims=False
    )
    key_mine = lax.dynamic_index_in_dim(
        key_round.reshape(mine_count, pair_size, HEAD_SIZE), parity, 1, keepdims=False
    )
    value_mine = lax.dynamic_index_in_dim(
        value_round.reshape(mine_count, pair_size, HEAD_SIZE), parity, 1, keepdims=False
    )
    heads_group = group_query.shape[1] // HEAD_SIZE
    query_rot = apply_rotation(
        group_query.reshape(mine_count, heads_group, HEAD_SIZE), positions_mine
    ).astype(jnp.bfloat16)
    attended_mine = attend_block(
        query_rot, key_mine, value_mine, key_cache_blocks[0], value_cache_blocks[0], filled_mine
    ).reshape(mine_count, heads_group * HEAD_SIZE)
    own_cols = lax.dynamic_slice_in_dim(attended_mine, parity * query_columns, query_columns, 1)
    give_cols = lax.dynamic_slice_in_dim(
        attended_mine, (1 - parity) * query_columns, query_columns, 1
    )
    back_cols = from_partner(give_cols, "tensor", 0)
    attended = jnp.where(
        parity == 0,
        jnp.stack([own_cols, back_cols], axis=1),
        jnp.stack([back_cols, own_cols], axis=1),
    ).reshape(sessions, query_columns)
    return (attended, new_keys, fresh_values)


def solution(mesh):
    return jax.shard_map(
        local,
        mesh=mesh,
        in_specs=(
            P("dp", "tensor"),
            P(None, "tensor"),
            P(None, "tensor"),
            P(None, "tensor"),
            P(("dp", "tensor"), None, None),
            P(("dp", "tensor"), None, None),
            P("tensor", "dp", None, None),
            P("tensor", "dp", None, None),
            P("dp"),
            P("dp"),
            P("dp", None),
            P("dp"),
        ),
        out_specs=(P("dp", "tensor"), P("dp", "tensor"), P("dp", "tensor")),
        check_vma=False,
    )
```

profile of v0, /device:TPU:0, one launch (start us, length us, event | category | flops | bytes accessed | tf_op | source)
XLA Modules:
  0.0 222.6 jit_solution(10677071832448935430)
XLA Ops:
  9.9 11.1 %all-to-all-start = ((s32[128,1,1]{2,1,0:T(1,128)}), s32[128,1,1]{2,1,0:T(1,128)S(1)}, u32[]{:S(2)}, u32[]{:S(2)}) async-start(s32[128,1,1]{2,1,0:T(1,128)} %copy.61), calls=%async_computation | async-start | bytes 131072 | tf_op jit(solution)/shard_map/all_to_all | solution.py:136
  21.0 0.9 fusion.63
  22.4 8.0 %all-to-all-done = s32[128,1,1]{2,1,0:T(1,128)S(1)} async-done(((s32[128,1,1]{2,1,0:T(1,128)}), s32[128,1,1]{2,1,0:T(1,128)S(1)}, u32[]{:S(2)}, u32[]{:S(2)}) %all-to-all-start) | async-done | bytes 544 | tf_op jit(solution)/shard_map/all_to_all | solution.py:136
  30.4 4.7 %and_reduce_fusion = (pred[128]{0:T(512)(128)(4,1)S(1)}, s32[128,1,1]{2,1,0:T(1,128)S(1)}, pred[128]{0:T(512)(128)(4,1)S(1)}) fusion(s32[128,1,1]{2,1,0:T(1,128)S(1)} %all-to-all-done), kind=kLoop, calls=%fused_computation.36 | loop fusion | flops 2048 | bytes 1280 | tf_op jit(solution)/shard_map/jit(_take)/and | solution.py:140
  35.1 2.4 %reduce.4 = s32[128]{0:T(128)S(1)} reduce(s32[128,1,1]{2,1,0:T(1,128)S(1)} %get-tuple-element.6, s32[]{:T(128)} %constant.148.clone.1), dimensions={1,2}, to_apply=%select_n.258.reduce_sub_computation | reduce | bytes 1028 | tf_op jit(solution)/shard_map/jit(_take)/jit(_where)/select_n | solution.py:140
  37.5 0.8 gather_fusion.2
  38.3 1.6 fusion.9
  39.9 5.8 %all-to-all-start.2 = ((bf16[128,1,8,640]{3,2,1,0:T(8,128)(2,1)}), bf16[128,1,8,640]{3,2,1,0:T(8,128)(2,1)}, u32[]{:S(2)}, u32[]{:S(2)}) async-start(bf16[128,1,8,640]{3,2,1,0:T(8,128)(2,1)} %fusion.9), calls=%async_computation.2 | async-start | bytes 2621440 | tf_op jit(solution)/shard_map/all_to_all | solution.py:145
  46.4 0.9 copy.62
  47.3 2.4 %gather_fusion = bf16[128,24,512]{2,1,0:T(8,128)(2,1)} fusion(bf16[64,24,512]{2,1,0:T(8,128)(2,1)S(1)} %bitcast.118, s32[1024]{0:T(1024)S(1)} %pad_clamp_fusion.1), kind=kCustom, calls=%fused_computation | custom fusion | bytes 6291968 | tf_op jit(solution)/shard_map/jit(_take)/gather | solution.py:140
  49.7 3.5 %fusion.5 = bf16[128,1,24,512]{3,2,1,0:T(8,128)(2,1)} fusion(bf16[128,24,512]{2,1,0:T(8,128)(2,1)} %gather_fusion, pred[128]{0:T(512)(128)(4,1)S(1)} %get-tuple-element.5, pred[128]{0:T(512)(128)(4,1)S(1)} %get-tuple-element.15), kind=kLoop, calls=%fused_computation.10 | loop fusion | flops 3145728 | bytes 6291712 | tf_op jit(solution)/shard_map/jit(_where)/select_n | solution.py:140
  53.2 13.9 %all-to-all-done.2 = bf16[128,1,8,640]{3,2,1,0:T(8,128)(2,1)} async-done(((bf16[128,1,8,640]{3,2,1,0:T(8,128)(2,1)}), bf16[128,1,8,640]{3,2,1,0:T(8,128)(2,1)}, u32[]{:S(2)}, u32[]{:S(2)}) %all-to-all-start.2) | async-done | bytes 1310752 | tf_op jit(solution)/shard_map/all_to_all | solution.py:145
  67.1 5.9 %all-to-all-start.1 = ((bf16[128,1,24,512]{3,2,1,0:T(8,128)(2,1)}), bf16[128,1,24,512]{3,2,1,0:T(8,128)(2,1)}, u32[]{:S(2)}, u32[]{:S(2)}) async-start(bf16[128,1,24,512]{3,2,1,0:T(8,128)(2,1)} %fusion.5), calls=%async_computation.1 | async-start | bytes 6291456 | tf_op jit(solution)/shard_map/all_to_all | solution.py:142
  74.9 2.0 gather_fusion.3
  77.1 36.7 %all-to-all-done.1 = bf16[128,1,24,512]{3,2,1,0:T(8,128)(2,1)} async-done(((bf16[128,1,24,512]{3,2,1,0:T(8,128)(2,1)}), bf16[128,1,24,512]{3,2,1,0:T(8,128)(2,1)}, u32[]{:S(2)}, u32[]{:S(2)}) %all-to-all-start.1) | async-done | bytes 3145760 | tf_op jit(solution)/shard_map/all_to_all | solution.py:142
  113.8 3.7 %gather_fusion.1 = bf16[64,24,512]{2,1,0:T(8,128)(2,1)} fusion(bf16[128,24,512]{2,1,0:T(8,128)(2,1)} %bitcast.7, s32[1024]{0:T(1024)S(1)} %pad_clamp_fusion), kind=kCustom, calls=%fused_computation.1 | custom fusion | bytes 3145984 | tf_op jit(solution)/shard_map/jit(_take)/gather | solution.py:148
  117.5 2.1 fusion.6
  119.6 71.3 %psum.7 = bf16[64,24]{1,0:T(8,128)(2,1)S(1)} all-reduce(f32[64,24]{1,0:T(8,128)S(1)} %bitcast.136), channel_id=1, replica_groups=mesh['dp'=8,'tensor'=16] {'tensor'}, use_global_device_ids=true, to_apply=%region_4.5 | all-reduce | flops 1536 | bytes 9216 | tf_op jit(solution)/shard_map/psum | solution.py:157
  191.3 1.7 convolution_add_fusion.1
  193.9 2.1 collective-permute-start.1
  196.3 4.9 %convolution_add_fusion = f32[64,512]{1,0:T(8,128)S(1)} fusion(bf16[64,8192]{1,0:T(8,128)(2,1)S(1)} %copy-done.1, bf16[8192,512]{1,0:T(8,128)(2,1)} %param.13, f32[64,1,512]{2,1,0:T(1,128)S(1)} %fusion.23), kind=kOutput, calls=%fused_computation.20 | convolution fusion | flops 536903680 | bytes 9699328 | tf_op jit(solution)/shard_map/dot_general | solution.py:98
  202.1 3.7 %collective-permute-done = f32[32,512]{1,0:T(8,128)S(1)} collective-permute-done((f32[32,512]{1,0:T(8,128)S(1)}, f32[32,512]{1,0:T(8,128)S(1)}, u32[]{:S(2)}, u32[]{:S(2)}) %collective-permute-start) | collective-permute-done | bytes 65568 | tf_op jit(solution)/shard_map/ppermute | solution.py:23
  206.2 3.6 %select_reduce_fusion = (f32[32,8]{1,0:T(8,128)S(1)}, f32[32,8,512]{2,1,0:T(8,128)S(1)}) fusion(pred[32,512]{1,0:T(8,128)(4,1)S(1)} %iota_compare_fusion, bf16[1,32,512,128]{3,2,1,0:T(8,128)(2,1)} %param.18, bf16[32,8,64]{2,1,0:T(8,128)(2,1)S(1)} %get-tuple-element.10, bf16[32,8,64]{2,1,0:T(8,128)(2,1)S(1)} %get-tuple-element.9), kind=kOutput, calls=%fused_computation.30 | convolution fusion | flops 34078464 | bytes 4801536 | tf_op jit(solution)/shard_map/sgd,scd->sgc/dot_general | solution.py:47
  211.8 3.2 %collective-permute-done.3 = bf16[32,512]{1,0:T(8,128)(2,1)S(1)} collective-permute-done((bf16[32,512]{1,0:T(8,128)(2,1)S(1)}, bf16[32,512]{1,0:T(8,128)(2,1)S(1)}, u32[]{:S(2)}, u32[]{:S(2)}) %collective-permute-start.3) | collective-permute-done | bytes 32800 | tf_op jit(solution)/shard_map/ppermute | solution.py:23
  (91 shorter events, 10.9 us)
Async XLA Ops:
  7.2 184.2 %copy-start = (bf16[8192,64]{0,1:T(8,128)(2,1)S(1)}, bf16[8192,64]{0,1:T(8,128)(2,1)}, u32[]{:S(2)}) copy-start(bf16[8192,64]{0,1:T(8,128)(2,1)} %param.15) | copy-start | bytes 3145732
  7.2 15.1 %slice-start = ((bf16[4,8,10240]{2,1,0:T(8,128)(2,1)}), bf16[4,8,8192]{2,1,0:T(8,128)(2,1)S(1)}, s32[]{:S(2)}) async-start(bf16[4,8,10240]{2,1,0:T(8,128)(2,1)} %param.17), calls=%async_computation.4 | async-start | bytes 1048576 | tf_op jit(solution)/shard_map/slice | solution.py:122
  9.9 20.6 %all-to-all-start = ((s32[128,1,1]{2,1,0:T(1,128)}), s32[128,1,1]{2,1,0:T(1,128)S(1)}, u32[]{:S(2)}, u32[]{:S(2)}) async-start(s32[128,1,1]{2,1,0:T(1,128)} %copy.61), calls=%async_computation | async-start | bytes 131072 | tf_op jit(solution)/shard_map/all_to_all | solution.py:136
  39.9 5.8 %copy-start.3 = (bf16[4,24,8192]{2,1,0:T(8,128)(2,1)S(1)}, bf16[4,24,8192]{2,1,0:T(8,128)(2,1)}, u32[]{:S(2)}) copy-start(bf16[4,24,8192]{2,1,0:T(8,128)(2,1)} %param.16) | copy-start | bytes 4718596
  39.9 27.2 %all-to-all-start.2 = ((bf16[128,1,8,640]{3,2,1,0:T(8,128)(2,1)}), bf16[128,1,8,640]{3,2,1,0:T(8,128)(2,1)}, u32[]{:S(2)}, u32[]{:S(2)}) async-start(bf16[128,1,8,640]{3,2,1,0:T(8,128)(2,1)} %fusion.9), calls=%async_computation.2 | async-start | bytes 2621440 | tf_op jit(solution)/shard_map/all_to_all | solution.py:145
  53.2 20.6 %copy-start.7 = (s32[64]{0:T(128)S(1)}, s32[64]{0:T(128)}, u32[]{:S(2)}) copy-start(s32[64]{0:T(128)} %param.21) | copy-start | bytes 772
  53.2 20.7 %copy-start.8 = (s32[64]{0:T(128)S(1)}, s32[64]{0:T(128)}, u32[]{:S(2)}) copy-start(s32[64]{0:T(128)} %param.20) | copy-start | bytes 772
  53.2 21.2 %copy-start.9 = (s32[1,63]{1,0:T(1,128)S(1)}, s32[1,63]{1,0:T(1,128)}, u32[]{:S(2)}) copy-start(s32[1,63]{1,0:T(1,128)} %param.22) | copy-start | bytes 760
  53.2 21.2 %copy-start.10 = (s32[64]{0:T(128)S(1)}, s32[64]{0:T(128)}, u32[]{:S(2)}) copy-start(s32[64]{0:T(128)} %param.23) | copy-start | bytes 772
  67.1 46.7 %all-to-all-start.1 = ((bf16[128,1,24,512]{3,2,1,0:T(8,128)(2,1)}), bf16[128,1,24,512]{3,2,1,0:T(8,128)(2,1)}, u32[]{:S(2)}, u32[]{:S(2)}) async-start(bf16[128,1,24,512]{3,2,1,0:T(8,128)(2,1)} %fusion.5), calls=%async_computation.1 | async-start | bytes 6291456 | tf_op jit(solution)/shard_map/all_to_all | solution.py:142
  73.0 118.3 %all-gather.2.cloned.1.call-start = ((), (), s32[]{:S(2)}) async-start(), calls=%async_computation.3 | async-start | bytes 1114112 | tf_op jit(solution)/shard_map/all_gather | solution.py:97
  113.8 3.7 %copy-start.6 = (bf16[64,512]{1,0:T(8,128)(2,1)S(1)}, bf16[64,512]{1,0:T(8,128)(2,1)}, u32[]{:S(2)}) copy-start(bf16[64,512]{1,0:T(8,128)(2,1)} %param.12) | copy-start | bytes 196612
  119.6 73.8 %copy-start.4 = (bf16[8192,64]{0,1:T(8,128)(2,1)S(1)}, bf16[8192,64]{0,1:T(8,128)(2,1)}, u32[]{:S(2)}) copy-start(bf16[8192,64]{0,1:T(8,128)(2,1)} %param.14) | copy-start | bytes 3145732
  191.3 2.1 copy-start.1
  193.1 3.2 %copy-start.5 = (bf16[64,64]{1,0:T(8,128)(2,1)}, bf16[64,64]{1,0:T(8,128)(2,1)S(1)}, u32[]{:S(2)}) copy-start(bf16[64,64]{1,0:T(8,128)(2,1)S(1)} %convolution_add_fusion.1) | copy-start | bytes 24580
  193.1 8.4 %collective-permute-start.2 = (bf16[64,64]{1,0:T(8,128)(2,1)S(1)}, bf16[64,64]{1,0:T(8,128)(2,1)S(1)}, u32[]{:S(2)}, u32[]{:S(2)}) collective-permute-start(bf16[64,64]{1,0:T(8,128)(2,1)S(1)} %convolution_add_fusion.1), channel_id=1, source_target_pairs={{0,1},{1,0},{2,3},{3,2},{4,5},{5,4},{6,7},{7,6},{8,9},{9,8},{10,11... | collective-permute-start | bytes 24584 | tf_op jit(solution)/shard_map/ppermute | solution.py:23
  193.9 7.8 %collective-permute-start.1 = (f32[64,64]{1,0:T(8,128)S(1)}, f32[64,64]{1,0:T(8,128)S(1)}, u32[]{:S(2)}, u32[]{:S(2)}) collective-permute-start(f32[64,64]{1,0:T(8,128)S(1)} %convolution_add_fusion.2), channel_id=1, source_target_pairs={{0,1},{1,0},{2,3},{3,2},{4,5},{5,4},{6,7},{7,6},{8,9},{9,8},{10,11... | collective-permute-start | bytes 49160 | tf_op jit(solution)/shard_map/ppermute | solution.py:23
  201.4 4.3 %collective-permute-start = (f32[32,512]{1,0:T(8,128)S(1)}, f32[32,512]{1,0:T(8,128)S(1)}, u32[]{:S(2)}, u32[]{:S(2)}) collective-permute-start(f32[32,512]{1,0:T(8,128)S(1)} %bitcast.130), channel_id=1, source_target_pairs={{0,1},{1,0},{2,3},{3,2},{4,5},{5,4},{6,7},{7,6},{8,9},{9,8},{10,11... | collective-permute-start | bytes 196616 | tf_op jit(solution)/shard_map/ppermute | solution.py:23
  206.2 4.0 %copy-start.2 = (bf16[1,32,512,128]{3,2,1,0:T(8,128)(2,1)S(1)}, bf16[1,32,512,128]{3,2,1,0:T(8,128)(2,1)}, u32[]{:S(2)}) copy-start(bf16[1,32,512,128]{3,2,1,0:T(8,128)(2,1)} %param.19) | copy-start | bytes 12582916
  211.0 4.0 %collective-permute-start.3 = (bf16[32,512]{1,0:T(8,128)(2,1)S(1)}, bf16[32,512]{1,0:T(8,128)(2,1)S(1)}, u32[]{:S(2)}, u32[]{:S(2)}) collective-permute-start(bf16[32,512]{1,0:T(8,128)(2,1)S(1)} %get-tuple-element.14), channel_id=1, source_target_pairs={{0,1},{1,0},{2,3},{3,2},{4,5},{5,4},{6,7},{7,6},{8,9},{9,8},{10,11... | collective-permute-start | bytes 98312 | tf_op jit(solution)/shard_map/ppermute | solution.py:23
Sparse Core Ops, SparseCore 0:
  76.0 60.0 all-gather.1
where the time goes:
time: 223 us
  blocking collectives  71.3 us (32%)
  waiting for transfers between devices  66.2 us (30%)
  starting transfers between devices  25.3 us (11%)
  other arithmetic  15.8 us (7%)
  local copies, waits for them, and re-layouts  14.7 us (7%)
  matrix products  14.6 us (7%)
  between operations  14.6 us (7%)
    psum x1, blocking collectives, local(): mesh_coordinates = lax.psum(partial_coords, 'tensor').astype(jnp.bfloat16)  71.3 us
    all_to_all x1, waiting for transfers between devices, local(): lax.all_to_all(down_pieces, ('dp', 'tensor'), split_axis=0, concat_axis=0...  36.7 us
    all_to_all x1, waiting for transfers between devices, local(): lax.all_to_all(up_pieces, ('dp', 'tensor'), split_axis=0, concat_axis=0,...  13.9 us
    all_to_all x1, starting transfers between devices, local(): lax.all_to_all(asked_table, ('dp', 'tensor'), split_axis=0, concat_axis=0...  11.1 us
    all_to_all x1, waiting for transfers between devices, local(): lax.all_to_all(asked_table, ('dp', 'tensor'), split_axis=0, concat_axis=0...  8.01 us
    ppermute x4, waiting for transfers between devices, from_partner(): return lax.ppermute(block, axis, route)  6.94 us
    all_to_all x1, starting transfers between devices, local(): lax.all_to_all(down_pieces, ('dp', 'tensor'), split_axis=0, concat_axis=0...  5.93 us
    select_n x2, other arithmetic, local(): down_pieces = jnp.where(present, jnp.take(down_table, row_index, axis=0), 0)  5.85 us
  transfers between devices with their start and end apart: 8, of which 5 were waited for; matrix products, arithmetic and copies ran while one was open for 11% of the time, Pallas kernels for 0%

commit v1 on v0

v1 whole, which is shorter than its diff:
```python
import functools
import math

import jax
import jax.numpy as jnp
from jax import lax
from jax.experimental import pallas as pl
from jax.experimental.pallas import tpu as pltpu
from jax.sharding import PartitionSpec as P

HEAD = 128
RANK = 8
THETA = 500000.0
ROUTE = ("tensor", "dp")
BF16 = jnp.bfloat16
F32 = jnp.float32


def owner_kernel(recv_ref, down_ref, up_ref, out_ref):
    acc = jnp.zeros((16, 96), F32)
    for t in range(16):
        acc = acc + lax.dot_general(
            recv_ref[t * 16 : (t + 1) * 16, 0:512],
            down_ref[:, t * 512 : (t + 1) * 512],
            (((1,), (1,)), ((), ())),
            preferred_element_type=F32,
        )
    ids = recv_ref[0:16, 512:640].astype(F32)[:, 0:1].astype(jnp.int32)
    coords = acc.astype(BF16).astype(F32)
    mine = lax.broadcasted_iota(jnp.int32, (16, 32), 1) // RANK == ids
    blocks = []
    for b in range(3):
        block = jnp.concatenate(
            [coords[:, a * 24 + b * 8 : a * 24 + b * 8 + 8] for a in range(4)], axis=1
        )
        blocks.append(jnp.where(mine, block, 0.0).astype(BF16))
    dot = functools.partial(jnp.dot, preferred_element_type=F32)
    low_key = dot(blocks[1], up_ref[:, 8192:9216])
    low_value = dot(blocks[2], up_ref[:, 9216:10240])
    for t in range(16):
        rows = slice(t * 16, (t + 1) * 16)
        head = slice((t // 2) * 128, (t // 2 + 1) * 128)
        out_ref[rows, 0:512] = dot(blocks[0], up_ref[:, t * 512 : (t + 1) * 512])
        out_ref[rows, 512:640] = low_key[:, head]
        out_ref[rows, 640:768] = low_value[:, head]


def owner_low(recv, down, up):
    return pl.pallas_call(
        owner_kernel,
        out_shape=jax.ShapeDtypeStruct((256, 768), F32),
        in_specs=[pl.BlockSpec(memory_space=pltpu.VMEM)] * 3,
        out_specs=pl.BlockSpec(memory_space=pltpu.VMEM),
        compiler_params=pltpu.CompilerParams(vmem_limit_bytes=16 * 2**20),
        cost_estimate=pl.CostEstimate(flops=40_000_000, bytes_accessed=3_400_000, transcendentals=0),
        name="owner_low",
    )(recv, down, up)


def base_kernel(order_ref, hidden_ref, wq_ref, wk_ref, wv_ref, q_ref, kv_ref):
    h = hidden_ref[0]
    q = jnp.dot(h, wq_ref[...], preferred_element_type=F32)
    nt = (((1,), (1,)), ((), ()))
    wkv = jnp.concatenate([wk_ref[...], wv_ref[...]], axis=0)
    kv = lax.dot_general(h, wkv, nt, preferred_element_type=F32)

    @pl.when(pl.program_id(0) == 0)
    def _():
        q_ref[...] = q
        kv_ref[...] = kv

    @pl.when(pl.program_id(0) != 0)
    def _():
        q_ref[...] += q
        kv_ref[...] += kv


def base_project(order, hidden, wq, wkt, wvt):
    return pl.pallas_call(
        base_kernel,
        grid_spec=pltpu.PrefetchScalarGridSpec(
            num_scalar_prefetch=1,
            grid=(16,),
            in_specs=[
                pl.BlockSpec((1, 64, 512), lambda i, o: (i, 0, 0)),
                pl.BlockSpec((512, 512), lambda i, o: (o[i], 0)),
                pl.BlockSpec((64, 512), lambda i, o: (0, o[i])),
                pl.BlockSpec((64, 512), lambda i, o: (0, o[i])),
            ],
            out_specs=[
                pl.BlockSpec((64, 512), lambda i, o: (0, 0)),
                pl.BlockSpec((64, 128), lambda i, o: (0, 0)),
            ],
        ),
        out_shape=[
            jax.ShapeDtypeStruct((64, 512), F32),
            jax.ShapeDtypeStruct((64, 128), F32),
        ],
        compiler_params=pltpu.CompilerParams(vmem_limit_bytes=16 * 2**20),
        cost_estimate=pl.CostEstimate(flops=671_000_000, bytes_accessed=11_700_000, transcendentals=0),
        name="base_project",
    )(order, hidden, wq, wkt, wvt)


def finish_kernel(
    piece_ref, parity_ref, low_ref, q_ref, kv_ref, cos_ref, sin_ref,
    mine_ref, give_ref, key_ref, value_ref, rows_ref,
):
    for i in range(64):
        rows_ref[i : i + 1, :] = low_ref[pl.ds(piece_ref[i], 1), :]

    def rotate(part, cos, sin):
        return part * cos + pltpu.roll(part, 64, 1) * sin

    cos, sin = cos_ref[...], sin_ref[...]
    key_ref[...] = rotate(kv_ref[:, 0:128] + rows_ref[:, 512:640], cos, sin).astype(BF16)
    value_ref[...] = (kv_ref[:, 128:256] + rows_ref[:, 640:768]).astype(BF16)
    parity = parity_ref[0]
    for ref, which in ((mine_ref, parity), (give_ref, 1 - parity)):
        rows = pl.ds(pl.multiple_of(which * 32, 32), 32)
        cos, sin = cos_ref[rows, :], sin_ref[rows, :]
        for h in range(4):
            cols = slice(h * 128, (h + 1) * 128)
            ref[:, cols] = rotate(q_ref[rows, cols] + rows_ref[rows, cols], cos, sin).astype(BF16)


def finish(piece, parity, low, q, kv, cos, sin):
    smem, vmem = pl.BlockSpec(memory_space=pltpu.SMEM), pl.BlockSpec(memory_space=pltpu.VMEM)
    return pl.pallas_call(
        finish_kernel,
        out_shape=[
            jax.ShapeDtypeStruct((32, 512), BF16),
            jax.ShapeDtypeStruct((32, 512), BF16),
            jax.ShapeDtypeStruct((64, 128), BF16),
            jax.ShapeDtypeStruct((64, 128), BF16),
        ],
        in_specs=[smem, smem] + [vmem] * 5,
        out_specs=[vmem] * 4,
        scratch_shapes=[pltpu.VMEM((64, 768), F32)],
        compiler_params=pltpu.CompilerParams(vmem_limit_bytes=16 * 2**20),
        cost_estimate=pl.CostEstimate(flops=1_000_000, bytes_accessed=1_200_000, transcendentals=0),
        name="finish",
    )(piece, parity, low, q, kv, cos, sin)


def attend_block(query_rot, key_new, value_new, key_rows, value_rows, length):
    scale = 1.0 / math.sqrt(HEAD)
    scores = jnp.einsum("sgd,scd->sgc", query_rot, key_rows, preferred_element_type=F32) * scale
    own = jnp.einsum("sgd,sd->sg", query_rot, key_new, preferred_element_type=F32) * scale
    valid = (jnp.arange(key_rows.shape[1])[None, :] < length[:, None])[:, None, :]
    top = jnp.maximum(jnp.max(jnp.where(valid, scores, -jnp.inf), axis=-1), own)
    weights = jnp.where(valid, jnp.exp(scores - top[..., None]), 0.0)
    own_weight = jnp.exp(own - top)
    total = jnp.sum(weights, axis=-1) + own_weight
    out = jnp.einsum("sgc,scd->sgd", weights.astype(BF16), value_rows, preferred_element_type=F32)
    own_rounded = lax.optimization_barrier(own_weight.astype(BF16)).astype(F32)
    out = out + own_rounded[..., None] * value_new.astype(F32)[:, None, :]
    return (out / total[..., None]).astype(BF16)


def local(
    hidden, wq, wk, wv, down_maps, up_maps, key_cache, value_cache, filled, positions, requests, slots
):
    t = lax.axis_index("tensor")
    parity = t % 2
    z, y = t % 4, t // 4

    def z_turn(k):
        return [(4 * a + b, 4 * a + (b + k) % 4) for a in range(4) for b in range(4)]

    def y_turn(k):
        return [(4 * a + b, 4 * ((a + k) % 4) + b) for a in range(4) for b in range(4)]

    swap = [(i, i ^ 1) for i in range(16)]

    match = slots[:, None] == jnp.arange(63)[None, :]
    adapter = jnp.sum(jnp.where(match, requests, 0), axis=1)
    owner = adapter // 4
    earlier = jnp.arange(64)[None, :] < jnp.arange(64)[:, None]
    second = jnp.any(earlier & (slots[:, None] == slots[None, :]), axis=1)
    piece = ((owner % 16) * 8 + owner // 16) * 2 + second.astype(jnp.int32)
    place = (jnp.arange(256)[:, None] == piece[None, :]).astype(BF16)
    ids = jnp.broadcast_to((adapter % 4).astype(BF16)[:, None], (64, 128))
    sent = jnp.dot(place, jnp.concatenate([hidden, ids], axis=1), preferred_element_type=F32)
    sent = sent.astype(BF16).reshape(128, 2, 640)

    def evens_first(x):
        return jnp.swapaxes(x.reshape((32, 2) + x.shape[1:]), 0, 1)

    split = evens_first(hidden).reshape(64, 512)
    around_z = [split] + [lax.ppermute(split, "tensor", z_turn(k)) for k in (1, 2, 3)]
    recv = lax.all_to_all(sent, ROUTE, 0, 0, tiled=True)
    band = jnp.stack(around_z)
    around_y = [band] + [lax.ppermute(band, "tensor", y_turn(k)) for k in (1, 2, 3)]

    low_sent = owner_low(
        recv.reshape(256, 640), down_maps.reshape(96, 8192), up_maps.reshape(32, 10240)
    )
    low = lax.all_to_all(low_sent.reshape(128, 2, 768), ROUTE, 0, 0, tiled=True)

    blocks = jnp.concatenate(around_y)
    turns = jnp.arange(16)
    order = 4 * ((y - turns // 4) % 4) + (z - turns % 4) % 4
    base_q, base_kv = base_project(order.astype(jnp.int32), blocks, wq, wk.T, wv.T)
    other_kv = lax.ppermute(base_kv, "tensor", swap)
    first = jnp.where(parity == 0, base_kv, other_kv)
    last = jnp.where(parity == 0, other_kv, base_kv)
    full_kv = jnp.concatenate(
        [first[:, :64], last[:, :64], first[:, 64:], last[:, 64:]], axis=1
    )

    pos = evens_first(positions).reshape(64)
    freq = THETA ** (-2.0 * jnp.arange(64, dtype=F32) / HEAD)
    angle = pos.astype(F32)[:, None] * freq[None, :]
    cos, sin = jnp.cos(angle), jnp.sin(angle)
    cos, sin = jnp.concatenate([cos, cos], 1), jnp.concatenate([-sin, sin], 1)
    q_mine, q_give, key_all, value_all = finish(
        evens_first(piece).reshape(64), parity.reshape(1), low.reshape(256, 768), base_q, full_kv, cos, sin
    )
    q_got = lax.ppermute(q_give, "tensor", swap)
    is_even = parity == 0
    query = jnp.where(
        is_even,
        jnp.concatenate([q_mine, q_got], axis=1),
        jnp.concatenate([q_got, q_mine], axis=1),
    ).reshape(32, 8, HEAD)

    def interleave(x):
        return jnp.swapaxes(x.reshape(2, 32, -1), 0, 1).reshape(64, -1)

    def my_half(x):
        return interleave(jnp.where(is_even, x[:, :64], x[:, 64:]))

    new_keys, fresh = my_half(key_all), my_half(value_all)
    key_mine = lax.dynamic_slice_in_dim(key_all, parity * 32, 32, 0)
    value_mine = lax.dynamic_slice_in_dim(value_all, parity * 32, 32, 0)
    filled_mine = lax.dynamic_index_in_dim(filled.reshape(32, 2), parity, 1, keepdims=False)
    out = attend_block(query, key_mine, value_mine, key_cache[0], value_cache[0], filled_mine)
    out = out.reshape(32, 1024)
    own = jnp.where(is_even, out[:, :512], out[:, 512:])
    give = jnp.where(is_even, out[:, 512:], out[:, :512])
    back = lax.ppermute(give, "tensor", swap)
    attended = jnp.where(
        is_even, jnp.stack([own, back], axis=1), jnp.stack([back, own], axis=1)
    ).reshape(64, 512)
    return attended, new_keys, fresh


def solution(mesh):
    return jax.shard_map(
        local,
        mesh=mesh,
        in_specs=(
            P("dp", "tensor"),
            P(None, "tensor"),
            P(None, "tensor"),
            P(None, "tensor"),
            P(("dp", "tensor"), None, None),
            P(("dp", "tensor"), None, None),
            P("tensor", "dp", None, None),
            P("tensor", "dp", None, None),
            P("dp"),
            P("dp"),
            P("dp", None),
            P("dp"),
        ),
        out_specs=(P("dp", "tensor"), P("dp", "tensor"), P("dp", "tensor")),
        check_vma=False,
    )
```

time: 223 us -> 99.7 us (0.45)
  blocking collectives: 71.3 us -> 0 us
  waiting for transfers between devices: 66.2 us -> 31.3 us
  between operations: 14.6 us -> 1.04 us
  other arithmetic: 15.8 us -> 6.11 us
  matrix products: 14.6 us -> 5.57 us
  Pallas kernels: 0 us -> 7.9 us
  starting transfers between devices: 25.3 us -> 32.7 us
    psum x1 -> x0, blocking collectives: 71.3 us -> none  [local(): mesh_coordinates = lax.psum(partial_coords, 'tensor').astype(jnp.bfloat16)]
    all_to_all x3 -> x2, waiting for transfers between devices: 58.5 us -> 15.3 us  [the longest x1 15.3 us: local(): low = lax.all_to_all(low_sent.reshape(128, 2, 768), ROUTE, 0, 0, tiled=True)]
    ppermute x4 -> x9, starting transfers between devices: 2.37 us -> 14.1 us  [the longest x3 6.06 us: local(): lax.ppermute(split, 'tensor', z_turn(k))]
    ppermute x4 -> x9, waiting for transfers between devices: 6.94 us -> 16 us  [the longest x3 10.5 us: local(): lax.ppermute(band, 'tensor', y_turn(k))]
    dot_general x10 -> x4, matrix products: 14.6 us -> 5.57 us  [the longest x1 3.6 us: attend_block(): jnp.einsum('sgd,scd->sgc', query_rot, key_rows, preferred_element_type=F32)]
    gather x4 -> x0, local copies, waits for them, and re-layouts: 8.94 us -> none  [the longest x1 3.72 us: local(): jnp.take(down_got.reshape(all_size * RCAP, 3 * ADAPTER_RANK, feature_colu...]
    pallas_call x0 -> x3, Pallas kernels: none -> 7.9 us  [the longest x1 6.15 us: base_project(): pl.pallas_call(base_kernel, grid_spec=pltpu.PrefetchScalarGridSpec(num_sc...]
    select_n x8 -> x3, other arithmetic: 7.74 us -> 0.86 us  [the longest x1 0.77 us: local(): first = jnp.where(parity == 0, base_kv, other_kv)]
  transfers between devices with their start and end apart: 8 -> 11, of which waited for: 5 -> 5; matrix products, arithmetic and copies ran while one was open for 11% -> 12% of each run, Pallas kernels for 0% -> 7%
where the time goes in v1:
time: 99.7 us; the launch traced here: 99.1 us
  starting transfers between devices  32.7 us (33%)
  waiting for transfers between devices  31.3 us (31%)
  local copies, waits for them, and re-layouts  14.5 us (15%)
  Pallas kernels  7.9 us (8%)
  other arithmetic  6.11 us (6%)
  matrix products  5.57 us (6%)
  between operations  1.04 us (1%)
    all_to_all x1, waiting for transfers between devices, local(): low = lax.all_to_all(low_sent.reshape(128, 2, 768), ROUTE, 0, 0, tiled=True)  15.3 us
    ppermute x3, waiting for transfers between devices, local(): lax.ppermute(band, 'tensor', y_turn(k))  10.5 us
    all_to_all x1, starting transfers between devices, local(): low = lax.all_to_all(low_sent.reshape(128, 2, 768), ROUTE, 0, 0, tiled=True)  9.6 us
    all_to_all x1, starting transfers between devices, local(): recv = lax.all_to_all(sent, ROUTE, 0, 0, tiled=True)  8.95 us
    unnamed x27, local copies, waits for them, and re-layouts  7.01 us
    pallas_call x1, Pallas kernels, base_project(): pl.pallas_call(base_kernel, grid_spec=pltpu.PrefetchScalarGridSpec(num_sc...  6.15 us
    ppermute x3, starting transfers between devices, local(): lax.ppermute(split, 'tensor', z_turn(k))  6.06 us
    ppermute x3, starting transfers between devices, local(): lax.ppermute(band, 'tensor', y_turn(k))  5.17 us
  transfers between devices with their start and end apart: 11, of which 5 were waited for; matrix products, arithmetic and copies ran while one was open for 12% of the time, Pallas kernels for 7%

profile of v1, /device:TPU:0, one launch (start us, length us, event | category | flops | bytes accessed | tf_op | source)
XLA Modules:
  0.0 99.1 jit_solution(439454596482393185)
XLA Ops:
  0.6 0.9 reshape.180
  1.5 4.0 %collective-permute-start.1 = (bf16[64,512]{1,0:T(8,128)(2,1)S(1)}, bf16[64,512]{1,0:T(8,128)(2,1)S(1)}, u32[]{:S(2)}, u32[]{:S(2)}) collective-permute-start(bf16[64,512]{1,0:T(8,128)(2,1)S(1)} %bitcast.59), channel_id=1, source_target_pairs={{0,2},{1,3},{2,0},{3,1},{4,6},{5,7},{6,4},{7,5},{8,10},{9,11},{10,... | collective-permute-start | bytes 196616 | tf_op jit(solution)/shard_map/ppermute | solution.py:191
  6.3 1.3 %collective-permute-start = (bf16[64,512]{1,0:T(8,128)(2,1)S(1)}, bf16[64,512]{1,0:T(8,128)(2,1)S(1)}, u32[]{:S(2)}, u32[]{:S(2)}) collective-permute-start(bf16[64,512]{1,0:T(8,128)(2,1)S(1)} %bitcast.61), channel_id=1, source_target_pairs={{0,1},{1,2},{2,3},{3,0},{4,5},{5,6},{6,7},{7,4},{8,9},{9,10},{10,1... | collective-permute-start | bytes 196616 | tf_op jit(solution)/shard_map/ppermute | solution.py:191
  7.6 0.9 fusion.27
  9.5 1.1 %convolution_convert_fusion = bf16[256,640]{1,0:T(8,128)(2,1)S(1)} fusion(bf16[64,128]{1,0:T(8,128)(2,1)S(1)} %broadcast_in_dim.59, bf16[64,512]{1,0:T(8,128)(2,1)} %param.12, s32[64]{0:T(128)S(1)} %get-tuple-element.28), kind=kOutput, calls=%fused_computation.5 | convolution fusion | flops 21315584 | bytes 409856 | tf_op jit(solution)/shard_map/dot_general | solution.py:184
  11.4 8.9 %all-to-all-start = ((bf16[128,2,640]{2,1,0:T(2,128)(2,1)}), bf16[128,2,640]{2,1,0:T(2,128)(2,1)S(1)}, u32[]{:S(2)}, u32[]{:S(2)}) async-start(bf16[128,2,640]{2,1,0:T(2,128)(2,1)} %reshape.174), calls=%async_computation | async-start | bytes 655360 | tf_op jit(solution)/shard_map/all_to_all | solution.py:192
  24.9 1.0 %collective-permute-start.3 = (bf16[4,64,512]{2,1,0:T(8,128)(2,1)S(1)}, bf16[4,64,512]{2,1,0:T(8,128)(2,1)S(1)}, u32[]{:S(2)}, u32[]{:S(2)}) collective-permute-start(bf16[4,64,512]{2,1,0:T(8,128)(2,1)S(1)} %pad_maximum_fusion), channel_id=1, source_target_pairs={{0,4},{1,5},{2,6},{3,7},{4,8},{5,9},{6,10},{7,11},{8,12},{9,13},{1... | collective-permute-start | bytes 786440 | tf_op jit(solution)/shard_map/ppermute | solution.py:194
  25.9 2.7 %collective-permute-start.4 = (bf16[4,64,512]{2,1,0:T(8,128)(2,1)S(1)}, bf16[4,64,512]{2,1,0:T(8,128)(2,1)S(1)}, u32[]{:S(2)}, u32[]{:S(2)}) collective-permute-start(bf16[4,64,512]{2,1,0:T(8,128)(2,1)S(1)} %pad_maximum_fusion), channel_id=1, source_target_pairs={{0,8},{1,9},{2,10},{3,11},{4,12},{5,13},{6,14},{7,15},{8,0},{9,1},... | collective-permute-start | bytes 786440 | tf_op jit(solution)/shard_map/ppermute | solution.py:194
  28.6 1.4 %collective-permute-start.5 = (bf16[4,64,512]{2,1,0:T(8,128)(2,1)S(1)}, bf16[4,64,512]{2,1,0:T(8,128)(2,1)S(1)}, u32[]{:S(2)}, u32[]{:S(2)}) collective-permute-start(bf16[4,64,512]{2,1,0:T(8,128)(2,1)S(1)} %pad_maximum_fusion), channel_id=1, source_target_pairs={{0,12},{1,13},{2,14},{3,15},{4,0},{5,1},{6,2},{7,3},{8,4},{9,5},{1... | collective-permute-start | bytes 786440 | tf_op jit(solution)/shard_map/ppermute | solution.py:194
  30.1 4.0 %collective-permute-done.3 = bf16[4,64,512]{2,1,0:T(8,128)(2,1)S(1)} collective-permute-done((bf16[4,64,512]{2,1,0:T(8,128)(2,1)S(1)}, bf16[4,64,512]{2,1,0:T(8,128)(2,1)S(1)}, u32[]{:S(2)}, u32[]{:S(2)}) %collective-permute-start.3) | collective-permute-done | bytes 262176 | tf_op jit(solution)/shard_map/ppermute | solution.py:194
  34.1 6.5 %collective-permute-done.4 = bf16[4,64,512]{2,1,0:T(8,128)(2,1)S(1)} collective-permute-done((bf16[4,64,512]{2,1,0:T(8,128)(2,1)S(1)}, bf16[4,64,512]{2,1,0:T(8,128)(2,1)S(1)}, u32[]{:S(2)}, u32[]{:S(2)}) %collective-permute-start.4) | collective-permute-done | bytes 262176 | tf_op jit(solution)/shard_map/ppermute | solution.py:194
  40.6 3.4 %copy-done = bf16[8192,512]{1,0:T(8,128)(2,1)S(1)} copy-done((bf16[8192,512]{1,0:T(8,128)(2,1)S(1)}, bf16[8192,512]{1,0:T(8,128)(2,1)}, u32[]{:S(2)}) %copy-start) | copy-done | bytes 8388632
  44.0 1.2 %copy-done.2 = bf16[8192,64]{0,1:T(8,128)(2,1)S(1)} copy-done((bf16[8192,64]{0,1:T(8,128)(2,1)S(1)}, bf16[8192,64]{0,1:T(8,128)(2,1)}, u32[]{:S(2)}) %copy-start.2) | copy-done | bytes 1048600
  45.2 1.2 %copy-done.3 = bf16[8192,64]{0,1:T(8,128)(2,1)S(1)} copy-done((bf16[8192,64]{0,1:T(8,128)(2,1)S(1)}, bf16[8192,64]{0,1:T(8,128)(2,1)}, u32[]{:S(2)}) %copy-start.3) | copy-done | bytes 1048600
  46.5 6.1 %base_project.1 = (f32[64,512]{1,0:T(8,128)S(1)}, f32[64,128]{1,0:T(8,128)}) custom-call(s32[16]{0:T(128)S(1)} %fusion.45.order_ref, bf16[16,64,512]{2,1,0:T(8,128)(2,1)S(1)} %constant_dynamic-update-slice_fusion.hidden_ref, bf16[8192,512]{1,0:T(8,128)(2,1)S(1)} %copy-done, bf16[64,8192]{1,0:T(8,128)(2,1)S(1)} %bitcast.56, bf16[64,8192]{1,0:T(8,128)(2,1)S(1)} %bitcast.57), custom_call_target="tpu_custom_call" | custom-call | flops 671000000 | bytes 11700000 | tf_op jit(solution)/shard_map/base_project/pallas_call | solution.py:79
  52.6 1.7 %collective-permute-start.6 = (f32[64,128]{1,0:T(8,128)}, f32[64,128]{1,0:T(8,128)S(1)}, u32[]{:S(2)}, u32[]{:S(2)}) collective-permute-start(f32[64,128]{1,0:T(8,128)} %get-tuple-element.10), channel_id=1, source_target_pairs={{0,1},{1,0},{2,3},{3,2},{4,5},{5,4},{6,7},{7,6},{8,9},{9,8},{10,11... | collective-permute-start | bytes 98312 | tf_op jit(solution)/shard_map/ppermute | solution.py:205
  54.8 1.1 %copy-done.4 = bf16[4,8,10240]{2,1,0:T(8,128)(2,1)S(1)} copy-done((bf16[4,8,10240]{2,1,0:T(8,128)(2,1)S(1)}, bf16[4,8,10240]{2,1,0:T(8,128)(2,1)}, u32[]{:S(2)}) %copy-start.4) | copy-done | bytes 655384
  55.8 1.0 owner_low.1
  56.8 1.4 %reshape.178 = f32[128,2,768]{2,1,0:T(2,128)} reshape(f32[256,768]{1,0:T(8,128)S(1)} %owner_low.1) | data formatting | bytes 1572864 | tf_op jit(solution)/shard_map/reshape | solution.py:199
  58.2 9.6 %all-to-all-start.1 = ((f32[128,2,768]{2,1,0:T(2,128)}), f32[128,2,768]{2,1,0:T(2,128)S(1)}, u32[]{:S(2)}, u32[]{:S(2)}) async-start(f32[128,2,768]{2,1,0:T(2,128)} %reshape.178), calls=%async_computation.1 | async-start | bytes 1572864 | tf_op jit(solution)/shard_map/all_to_all | solution.py:199
  68.8 15.3 %all-to-all-done.1 = f32[128,2,768]{2,1,0:T(2,128)S(1)} async-done(((f32[128,2,768]{2,1,0:T(2,128)}), f32[128,2,768]{2,1,0:T(2,128)S(1)}, u32[]{:S(2)}, u32[]{:S(2)}) %all-to-all-start.1) | async-done | bytes 786464 | tf_op jit(solution)/shard_map/all_to_all | solution.py:199
  86.1 3.4 %collective-permute-done.7 = bf16[32,512]{1,0:T(8,128)(2,1)S(1)} collective-permute-done((bf16[32,512]{1,0:T(8,128)(2,1)S(1)}, bf16[32,512]{1,0:T(8,128)(2,1)S(1)}, u32[]{:S(2)}, u32[]{:S(2)}) %collective-permute-start.7) | collective-permute-done | bytes 32800 | tf_op jit(solution)/shard_map/ppermute | solution.py:220
  89.7 3.6 %select_reduce_fusion = (f32[32,8]{1,0:T(8,128)S(1)}, f32[32,8,512]{2,1,0:T(8,128)S(1)}) fusion(pred[32,512]{1,0:T(8,128)(4,1)S(1)} %iota_compare_fusion.2, bf16[1,32,512,128]{3,2,1,0:T(8,128)(2,1)} %param.18, bf16[32,4,128]{2,1,0:T(4,128)(2,1)S(1)} %concatenate.34, bf16[32,4,128]{2,1,0:T(4,128)(2,1)S(1)} %concatenate.33, pred[]{:T(512)S(6)} %eq.54), kind=kOutput, calls=%fused_computation.10 | convolution fusion | flops 34242304 | bytes 4801537 | tf_op jit(solution)/shard_map/sgd,scd->sgc/dot_general | solution.py:148
  96.3 2.1 %collective-permute-done.8 = bf16[32,512]{1,0:T(8,128)(2,1)S(1)} collective-permute-done((bf16[32,512]{1,0:T(8,128)(2,1)S(1)}, bf16[32,512]{1,0:T(8,128)(2,1)S(1)}, u32[]{:S(2)}, u32[]{:S(2)}) %collective-permute-start.8) | collective-permute-done | bytes 32800 | tf_op jit(solution)/shard_map/ppermute | solution.py:242
  (81 shorter events, 14.2 us)
Async XLA Ops:
  1.5 23.3 %collective-permute-start.1 = (bf16[64,512]{1,0:T(8,128)(2,1)S(1)}, bf16[64,512]{1,0:T(8,128)(2,1)S(1)}, u32[]{:S(2)}, u32[]{:S(2)}) collective-permute-start(bf16[64,512]{1,0:T(8,128)(2,1)S(1)} %bitcast.59), channel_id=1, source_target_pairs={{0,2},{1,3},{2,0},{3,1},{4,6},{5,7},{6,4},{7,5},{8,10},{9,11},{10,... | collective-permute-start | bytes 196616 | tf_op jit(solution)/shard_map/ppermute | solution.py:191
  5.6 19.2 %collective-permute-start.2 = (bf16[64,512]{1,0:T(8,128)(2,1)S(1)}, bf16[64,512]{1,0:T(8,128)(2,1)S(1)}, u32[]{:S(2)}, u32[]{:S(2)}) collective-permute-start(bf16[64,512]{1,0:T(8,128)(2,1)S(1)} %bitcast.60), channel_id=1, source_target_pairs={{0,3},{1,0},{2,1},{3,2},{4,7},{5,4},{6,5},{7,6},{8,11},{9,8},{10,9... | collective-permute-start | bytes 196616 | tf_op jit(solution)/shard_map/ppermute | solution.py:191
  6.3 18.5 %collective-permute-start = (bf16[64,512]{1,0:T(8,128)(2,1)S(1)}, bf16[64,512]{1,0:T(8,128)(2,1)S(1)}, u32[]{:S(2)}, u32[]{:S(2)}) collective-permute-start(bf16[64,512]{1,0:T(8,128)(2,1)S(1)} %bitcast.61), channel_id=1, source_target_pairs={{0,1},{1,2},{2,3},{3,0},{4,5},{5,6},{6,7},{7,4},{8,9},{9,10},{10,1... | collective-permute-start | bytes 196616 | tf_op jit(solution)/shard_map/ppermute | solution.py:191
  11.4 43.2 %all-to-all-start = ((bf16[128,2,640]{2,1,0:T(2,128)(2,1)}), bf16[128,2,640]{2,1,0:T(2,128)(2,1)S(1)}, u32[]{:S(2)}, u32[]{:S(2)}) async-start(bf16[128,2,640]{2,1,0:T(2,128)(2,1)} %reshape.174), calls=%async_computation | async-start | bytes 655360 | tf_op jit(solution)/shard_map/all_to_all | solution.py:192
  24.9 9.2 %collective-permute-start.3 = (bf16[4,64,512]{2,1,0:T(8,128)(2,1)S(1)}, bf16[4,64,512]{2,1,0:T(8,128)(2,1)S(1)}, u32[]{:S(2)}, u32[]{:S(2)}) collective-permute-start(bf16[4,64,512]{2,1,0:T(8,128)(2,1)S(1)} %pad_maximum_fusion), channel_id=1, source_target_pairs={{0,4},{1,5},{2,6},{3,7},{4,8},{5,9},{6,10},{7,11},{8,12},{9,13},{1... | collective-permute-start | bytes 786440 | tf_op jit(solution)/shard_map/ppermute | solution.py:194
  25.9 14.7 %collective-permute-start.4 = (bf16[4,64,512]{2,1,0:T(8,128)(2,1)S(1)}, bf16[4,64,512]{2,1,0:T(8,128)(2,1)S(1)}, u32[]{:S(2)}, u32[]{:S(2)}) collective-permute-start(bf16[4,64,512]{2,1,0:T(8,128)(2,1)S(1)} %pad_maximum_fusion), channel_id=1, source_target_pairs={{0,8},{1,9},{2,10},{3,11},{4,12},{5,13},{6,14},{7,15},{8,0},{9,1},... | collective-permute-start | bytes 786440 | tf_op jit(solution)/shard_map/ppermute | solution.py:194
  28.6 12.0 %collective-permute-start.5 = (bf16[4,64,512]{2,1,0:T(8,128)(2,1)S(1)}, bf16[4,64,512]{2,1,0:T(8,128)(2,1)S(1)}, u32[]{:S(2)}, u32[]{:S(2)}) collective-permute-start(bf16[4,64,512]{2,1,0:T(8,128)(2,1)S(1)} %pad_maximum_fusion), channel_id=1, source_target_pairs={{0,12},{1,13},{2,14},{3,15},{4,0},{5,1},{6,2},{7,3},{8,4},{9,5},{1... | collective-permute-start | bytes 786440 | tf_op jit(solution)/shard_map/ppermute | solution.py:194
  40.6 3.4 %copy-start = (bf16[8192,512]{1,0:T(8,128)(2,1)S(1)}, bf16[8192,512]{1,0:T(8,128)(2,1)}, u32[]{:S(2)}) copy-start(bf16[8192,512]{1,0:T(8,128)(2,1)} %wq_ref.1) | copy-start | bytes 25165828
  44.0 1.2 %copy-start.2 = (bf16[8192,64]{0,1:T(8,128)(2,1)S(1)}, bf16[8192,64]{0,1:T(8,128)(2,1)}, u32[]{:S(2)}) copy-start(bf16[8192,64]{0,1:T(8,128)(2,1)} %param.14) | copy-start | bytes 3145732
  45.2 1.2 %copy-start.3 = (bf16[8192,64]{0,1:T(8,128)(2,1)S(1)}, bf16[8192,64]{0,1:T(8,128)(2,1)}, u32[]{:S(2)}) copy-start(bf16[8192,64]{0,1:T(8,128)(2,1)} %param.15) | copy-start | bytes 3145732
  46.5 7.9 %copy-start.7 = (f32[64,64]{1,0:T(8,128)S(1)}, f32[64,64]{1,0:T(8,128)}, u32[]{:S(2)}) copy-start(f32[64,64]{1,0:T(8,128)} %get-tuple-element.25) | copy-start | bytes 49156
  46.5 7.9 %copy-start.8 = (f32[64,64]{1,0:T(8,128)S(1)}, f32[64,64]{1,0:T(8,128)}, u32[]{:S(2)}) copy-start(f32[64,64]{1,0:T(8,128)} %get-tuple-element.26) | copy-start | bytes 49156
  46.5 8.0 %copy-start.9 = (s32[2,32]{0,1:T(8,128)S(1)}, s32[2,32]{0,1:T(8,128)}, u32[]{:S(2)}) copy-start(s32[2,32]{0,1:T(8,128)} %fusion.33) | copy-start | bytes 772
  46.5 8.3 %copy-start.1 = (bf16[4,24,8192]{2,1,0:T(8,128)(2,1)S(1)}, bf16[4,24,8192]{2,1,0:T(8,128)(2,1)}, u32[]{:S(2)}) copy-start(bf16[4,24,8192]{2,1,0:T(8,128)(2,1)} %param.16) | copy-start | bytes 4718596
  52.6 15.1 %collective-permute-start.6 = (f32[64,128]{1,0:T(8,128)}, f32[64,128]{1,0:T(8,128)S(1)}, u32[]{:S(2)}, u32[]{:S(2)}) collective-permute-start(f32[64,128]{1,0:T(8,128)} %get-tuple-element.10), channel_id=1, source_target_pairs={{0,1},{1,0},{2,3},{3,2},{4,5},{5,4},{6,7},{7,6},{8,9},{9,8},{10,11... | collective-permute-start | bytes 98312 | tf_op jit(solution)/shard_map/ppermute | solution.py:205
  54.8 1.1 %copy-start.4 = (bf16[4,8,10240]{2,1,0:T(8,128)(2,1)S(1)}, bf16[4,8,10240]{2,1,0:T(8,128)(2,1)}, u32[]{:S(2)}) copy-start(bf16[4,8,10240]{2,1,0:T(8,128)(2,1)} %param.17) | copy-start | bytes 1966084
  55.8 28.8 %copy-start.5 = (f32[64,128]{1,0:T(8,128)S(1)}, f32[64,128]{1,0:T(8,128)}, u32[]{:S(2)}) copy-start(f32[64,128]{1,0:T(8,128)} %pad_maximum_fusion.2.cos_ref) | copy-start | bytes 98308
  58.2 25.9 %all-to-all-start.1 = ((f32[128,2,768]{2,1,0:T(2,128)}), f32[128,2,768]{2,1,0:T(2,128)S(1)}, u32[]{:S(2)}, u32[]{:S(2)}) async-start(f32[128,2,768]{2,1,0:T(2,128)} %reshape.178), calls=%async_computation.1 | async-start | bytes 1572864 | tf_op jit(solution)/shard_map/all_to_all | solution.py:199
  85.5 4.0 %collective-permute-start.7 = (bf16[32,512]{1,0:T(8,128)(2,1)S(1)}, bf16[32,512]{1,0:T(8,128)(2,1)S(1)}, u32[]{:S(2)}, u32[]{:S(2)}) collective-permute-start(bf16[32,512]{1,0:T(8,128)(2,1)S(1)} %get-tuple-element.12), channel_id=1, source_target_pairs={{0,1},{1,0},{2,3},{3,2},{4,5},{5,4},{6,7},{7,6},{8,9},{9,8},{10,11... | collective-permute-start | bytes 98312 | tf_op jit(solution)/shard_map/ppermute | solution.py:220
  89.5 4.1 %copy-start.6 = (bf16[1,32,512,128]{3,2,1,0:T(8,128)(2,1)S(1)}, bf16[1,32,512,128]{3,2,1,0:T(8,128)(2,1)}, u32[]{:S(2)}) copy-start(bf16[1,32,512,128]{3,2,1,0:T(8,128)(2,1)} %param.19) | copy-start | bytes 12582916
  94.4 4.0 %collective-permute-start.8 = (bf16[32,512]{1,0:T(8,128)(2,1)S(1)}, bf16[32,512]{1,0:T(8,128)(2,1)S(1)}, u32[]{:S(2)}, u32[]{:S(2)}) collective-permute-start(bf16[32,512]{1,0:T(8,128)(2,1)S(1)} %get-tuple-element.16), channel_id=1, source_target_pairs={{0,1},{1,0},{2,3},{3,2},{4,5},{5,4},{6,7},{7,6},{8,9},{9,8},{10,11... | collective-permute-start | bytes 98312 | tf_op jit(solution)/shard_map/ppermute | solution.py:242

commit v2 on v1

v2 whole, which is shorter than its diff:
```python
import functools
import math

import jax
import jax.numpy as jnp
from jax import lax
from jax.experimental import pallas as pl
from jax.experimental.pallas import tpu as pltpu
from jax.sharding import PartitionSpec as P

HEAD = 128
RANK = 8
THETA = 500000.0
ROUTE = ("tensor", "dp")
BF16 = jnp.bfloat16
F32 = jnp.float32
SMEM = pl.BlockSpec(memory_space=pltpu.SMEM)
VMEM = pl.BlockSpec(memory_space=pltpu.VMEM)
ANY = pl.BlockSpec(memory_space=pl.ANY)
NT = (((1,), (1,)), ((), ()))
dot = functools.partial(jnp.dot, preferred_element_type=F32)
dot_nt = functools.partial(lax.dot_general, dimension_numbers=NT, preferred_element_type=F32)


def prepare_kernel(
    requests_hbm, slots_hbm, hidden_hbm, sent_ref, plan_ref,
    rows_ref, wide_ref, hidden_ref, requests_ref, slots_ref, sems,
):
    copies = [
        pltpu.make_async_copy(requests_hbm, requests_ref, sems.at[0]),
        pltpu.make_async_copy(slots_hbm, slots_ref, sems.at[1]),
        pltpu.make_async_copy(hidden_hbm, hidden_ref, sems.at[2]),
    ]
    for copy in copies:
        copy.start()
    rows_ref[...] = jnp.zeros_like(rows_ref)
    for copy in copies:
        copy.wait()
    wide_ref[:, 0:512] = hidden_ref[...].astype(F32)
    first = jnp.int32(-1)
    last = jnp.int32(-1)
    for s in range(64):
        slot = slots_ref[s]
        adapter = requests_ref[0, slot]
        owner = adapter >> 2
        place = (owner & 15) * 8 + (owner >> 4)
        plan_ref[s] = place
        zero = slot == 0
        rank = jnp.where(zero & (first >= 0), 1, 0)
        last = jnp.where(zero, s, last)
        first = jnp.where(zero & (first < 0), s, first)
        code = ((adapter & 3) + 4 * (s % 2)).astype(F32)
        wide_ref[s : s + 1, 512:640] = jnp.full((1, 128), code, F32)
        rows_ref[place, pl.ds(rank, 1), :] = wide_ref[s : s + 1, :]
    plan_ref[64] = first
    plan_ref[65] = last
    sent_ref[...] = rows_ref[...].astype(BF16)


def in_hbm(*arrays):
    return [pltpu.with_memory_space_constraint(x, pltpu.HBM) for x in arrays]


def prepare(requests, slots, hidden):
    return pl.pallas_call(
        prepare_kernel,
        out_shape=[
            jax.ShapeDtypeStruct((128, 2, 640), BF16),
            jax.ShapeDtypeStruct((66,), jnp.int32),
        ],
        in_specs=[ANY] * 3,
        out_specs=[VMEM, SMEM],
        scratch_shapes=[
            pltpu.VMEM((128, 2, 640), F32),
            pltpu.VMEM((64, 640), F32),
            pltpu.VMEM((64, 512), BF16),
            pltpu.SMEM((1, 63), jnp.int32),
            pltpu.SMEM((64,), jnp.int32),
            pltpu.SemaphoreType.DMA((3,)),
        ],
        cost_estimate=pl.CostEstimate(flops=1_000_000, bytes_accessed=500_000, transcendentals=0),
        compiler_params=pltpu.CompilerParams(vmem_limit_bytes=4 * 2**20),
        name="prepare",
    )(*in_hbm(requests, slots, hidden))


def owner_kernel(recv_ref, down_hbm, up_hbm, out_ref, down_ref, up_ref, coords_ref, code_ref, sems):
    parts = [
        pltpu.make_async_copy(
            down_hbm.at[:, i * 2048 : (i + 1) * 2048], down_ref.at[:, i * 2048 : (i + 1) * 2048], sems.at[i]
        )
        for i in range(4)
    ]
    copy = pltpu.make_async_copy(up_hbm, up_ref, sems.at[4])
    for part in parts:
        part.start()
    copy.start()
    acc = jnp.zeros((16, 96), F32)
    for t in range(16):
        if t % 4 == 0:
            parts[t // 4].wait()
        acc = acc + dot_nt(
            recv_ref[t * 8 : (t + 1) * 8, :, 0:512].reshape(16, 512),
            down_ref[:, t * 512 : (t + 1) * 512],
        )
    coords_ref[:, 0:96] = acc.astype(BF16).astype(F32)
    code_ref[...] = recv_ref[0:8, :, 512:640].reshape(16, 128).astype(F32)
    one, two = coords_ref[pl.ds(0, 8, 2), :], coords_ref[pl.ds(1, 8, 2), :]
    code = code_ref[pl.ds(0, 8, 2), :][:, 0:1].astype(jnp.int32)
    odd = code >= 4
    coords = jnp.concatenate([jnp.where(odd, two, one), jnp.where(odd, one, two)], axis=0)
    ids = jnp.concatenate([code, code], axis=0) & 3
    mine = (lax.broadcasted_iota(jnp.int32, (16, 32), 1) >> 3) == ids
    blocks = []
    for b in range(3):
        block = jnp.concatenate(
            [coords[:, a * 24 + b * 8 : a * 24 + b * 8 + 8] for a in range(4)], axis=1
        )
        blocks.append(jnp.where(mine, block, 0.0).astype(BF16))
    copy.wait()
    low_key = dot(blocks[1], up_ref[:, 8192:9216])
    low_value = dot(blocks[2], up_ref[:, 9216:10240])
    for j in range(8):
        low_query = dot(blocks[0], up_ref[:, j * 1024 : (j + 1) * 1024])
        head = slice(j * 128, (j + 1) * 128)
        for p in range(2):
            rows, half = slice((2 * j + p) * 8, (2 * j + p + 1) * 8), slice(p * 8, p * 8 + 8)
            out_ref[rows, 0, 0:1024] = low_query[half]
            out_ref[rows, 0, 1024:1152] = low_key[half, head]
            out_ref[rows, 0, 1152:1280] = low_value[half, head]


def owner_low(recv, down, up):
    return pl.pallas_call(
        owner_kernel,
        out_shape=jax.ShapeDtypeStruct((128, 1, 1280), F32),
        in_specs=[VMEM, ANY, ANY],
        out_specs=VMEM,
        scratch_shapes=[
            pltpu.VMEM((96, 8192), BF16),
            pltpu.VMEM((32, 10240), BF16),
            pltpu.VMEM((16, 128), F32),
            pltpu.VMEM((16, 128), F32),
            pltpu.SemaphoreType.DMA((5,)),
        ],
        cost_estimate=pl.CostEstimate(flops=40_000_000, bytes_accessed=3_400_000, transcendentals=0),
        compiler_params=pltpu.CompilerParams(vmem_limit_bytes=8 * 2**20),
        name="owner_low",
    )(recv, *in_hbm(down, up))


def base_kernel(
    order_ref, plan_ref, h0_ref, h1_ref, h2_ref, h3_ref, wq_hbm, wk_hbm, wv_hbm, key_hbm, value_hbm, _,
    mine_ref, give_ref, key2_ref, value2_ref, wq_ref, wk_ref, wv_ref, acc_ref, sems,
):
    order = [order_ref[i] * 512 for i in range(16)]
    parity = order_ref[16]
    kv = [
        pltpu.make_async_copy(wk_hbm, wk_ref, sems.at[16]),
        pltpu.make_async_copy(wv_hbm, wv_ref, sems.at[17]),
    ]
    cache = [
        pltpu.make_async_copy(key_hbm.at[plan_ref[65] >> 1], key2_ref, sems.at[18]),
        pltpu.make_async_copy(value_hbm.at[plan_ref[65] >> 1], value2_ref, sems.at[19]),
    ]
    blocks = [
        pltpu.make_async_copy(
            wq_hbm.at[pl.ds(pl.multiple_of(order[i], 512), 512), :], wq_ref.at[i], sems.at[i]
        )
        for i in range(16)
    ]
    for copy in kv + blocks + cache:
        copy.start()
    for copy in kv:
        copy.wait()
    q = jnp.zeros((64, 512), F32)
    for i in range(16):
        h = (h0_ref, h1_ref, h2_ref, h3_ref)[i // 4][i % 4]
        cols = pl.ds(pl.multiple_of(order[i], 512), 512)
        wkv = jnp.concatenate([wk_ref[:, cols], wv_ref[:, cols]], axis=0)
        kv_part = dot_nt(h, wkv)
        if i == 0:
            acc_ref[:, 512:640] = kv_part
        else:
            acc_ref[:, 512:640] += kv_part
        blocks[i].wait()
        if i == 0:
            acc_ref[:, 0:512] = dot(h, wq_ref[i])
        else:
            acc_ref[:, 0:512] += dot(h, wq_ref[i])
    mine_ref[...] = acc_ref[pl.ds(pl.multiple_of(parity * 32, 32), 32), :]
    give_ref[...] = acc_ref[pl.ds(pl.multiple_of((1 - parity) * 32, 32), 32), :]
    for copy in cache:
        copy.wait()


def base_project(order, plan, bands, wq, wkt, wvt, keys, values, after):
    return pl.pallas_call(
        base_kernel,
        out_shape=[
            jax.ShapeDtypeStruct((32, 640), F32),
            jax.ShapeDtypeStruct((32, 640), F32),
            jax.ShapeDtypeStruct(keys.shape[1:], BF16),
            jax.ShapeDtypeStruct(values.shape[1:], BF16),
        ],
        in_specs=[SMEM] * 2 + [VMEM] * 4 + [ANY] * 6,
        out_specs=[VMEM] * 4,
        scratch_shapes=[
            pltpu.VMEM((16, 512, 512), BF16),
            pltpu.VMEM((64, 8192), BF16),
            pltpu.VMEM((64, 8192), BF16),
            pltpu.VMEM((64, 640), F32),
            pltpu.SemaphoreType.DMA((20,)),
        ],
        cost_estimate=pl.CostEstimate(flops=671_000_000, bytes_accessed=11_700_000, transcendentals=0),
        compiler_params=pltpu.CompilerParams(vmem_limit_bytes=16 * 2**20),
        name="base_project",
    )(order, plan, *bands, *in_hbm(wq, wkt, wvt, keys, values), after)


def rotate(part, cos, sin):
    return part * cos + pltpu.roll(part, 64, 1) * sin


def attend(query, key_new, value_new, keys, values, used):
    scale = 1.0 / math.sqrt(HEAD)
    scores = dot_nt(query.astype(BF16), keys) * scale
    own = jnp.sum(query * key_new, axis=1, keepdims=True) * scale
    valid = lax.broadcasted_iota(jnp.int32, scores.shape, 1) < used
    top = jnp.max(jnp.where(valid, scores, -jnp.inf), axis=1, keepdims=True)
    top = jnp.maximum(top, own)
    weights = jnp.where(valid, jnp.exp(scores - top), 0.0)
    own_weight = jnp.exp(own - top)
    total = jnp.sum(weights, axis=1, keepdims=True) + own_weight
    out = dot(weights.astype(BF16), values) + own_weight.astype(BF16).astype(F32) * value_new
    return out / total


def sides(parity, mine, other):
    even = parity == 0
    return jnp.where(even, mine, other), jnp.where(even, other, mine)


def project(parity, mine, other, low, cos, sin):
    def rounded(x):
        return x.astype(BF16).astype(F32)

    left, right = sides(parity, mine, other)
    heads = []
    for h in range(8):
        base = (left if h < 4 else right)[:, (h % 4) * 128 : (h % 4 + 1) * 128]
        heads.append(rounded(rotate(base + low[:, h * 128 : (h + 1) * 128], cos, sin)))
    key = jnp.concatenate([left[:, 512:576], right[:, 512:576]], axis=1) + low[:, 1024:1152]
    value = jnp.concatenate([left[:, 576:640], right[:, 576:640]], axis=1) + low[:, 1152:1280]
    return heads, rounded(rotate(key, cos, sin)), rounded(value)


def split(parity, outs, key, value):
    low = jnp.concatenate(outs[:4] + [key[:, :64], value[:, :64]], axis=1)
    high = jnp.concatenate(outs[4:] + [key[:, 64:], value[:, 64:]], axis=1)
    return sides(parity, low, high)


def attend_kernel(
    plan_ref, parity_ref, used_ref, low_ref, mine_ref, other_ref, cos_ref, sin_ref, key_hbm, value_hbm,
    keep_ref, give_ref, rows_ref, query_ref, fresh_ref, out_ref, key_ref, value_ref, sems,
):
    copies = []
    for g in range(4):
        hbm, ref = ((key_hbm, key_ref), (value_hbm, value_ref))[g // 2]
        part = pl.ds((g % 2) * 16, 16)
        copies.append(pltpu.make_async_copy(hbm.at[part], ref.at[part], sems.at[g]))
        copies[-1].start()
    parity = parity_ref[0]
    for i in range(32):
        rows_ref[i : i + 1, :] = low_ref[plan_ref[2 * i + parity]]
    heads, key, value = project(
        parity, mine_ref[...], other_ref[...], rows_ref[...], cos_ref[...], sin_ref[...]
    )
    for h in range(8):
        query_ref[pl.ds(h, 32, 8), :] = heads[h]
        fresh_ref[pl.ds(h, 32, 8), :] = value
    scale = 1.0 / math.sqrt(HEAD)
    lane = lax.broadcasted_iota(jnp.int32, (128, 128), 1) >> 3
    near_key = key.astype(BF16)
    halves = []
    for half in range(2):
        queries = query_ref[half * 128 : (half + 1) * 128, :].T
        spread = jnp.concatenate(
            [jnp.where(lane == s, queries, 0.0).astype(BF16) for s in range(16)], axis=0
        )
        near = jnp.concatenate(
            [near_key[half * 16 + s : half * 16 + s + 1, :] for s in range(16)], axis=1
        )
        own = dot(jnp.broadcast_to(near, (16, 2048)), spread)[0:1] * scale
        copies[half].wait()
        block = jnp.concatenate([key_ref[half * 16 + s] for s in range(16)], axis=1)
        scores = dot(block, spread) * scale
        valid = lax.broadcasted_iota(jnp.int32, (512, 128), 0) < used_ref[half : half + 1, :]
        top = jnp.max(jnp.where(valid, scores, -jnp.inf), axis=0, keepdims=True)
        top = jnp.maximum(top, own)
        weights = jnp.where(valid, jnp.exp(scores - top), 0.0)
        own_weight = jnp.exp(own - top)
        total = jnp.sum(weights, axis=0, keepdims=True) + own_weight
        pair = jnp.concatenate([own_weight, total, jnp.zeros((6, 128), F32)], axis=0).T
        halves.append((weights.T.astype(BF16), pair))
    for half in range(2):
        copies[2 + half].wait()
        weights, pair = halves[half]
        rows = slice(half * 128, (half + 1) * 128)
        own = pair[:, 0:1].astype(BF16).astype(F32) * fresh_ref[rows, :]
        total = pair[:, 1:2]
        for s in range(16):
            eight = slice(s * 8, (s + 1) * 8)
            out = dot(weights[eight], value_ref[half * 16 + s])
            out_ref[half * 128 + s * 8 : half * 128 + s * 8 + 8, :] = (out + own[eight]) / total[eight]
    outs = [out_ref[pl.ds(h, 32, 8), :] for h in range(8)]
    keep, give = split(parity, outs, key, value)
    keep_ref[...] = keep.astype(BF16)
    give_ref[...] = give.astype(BF16)


def attend_all(plan, parity, used, low, mine, other, cos, sin, keys, values):
    return pl.pallas_call(
        attend_kernel,
        out_shape=[jax.ShapeDtypeStruct((32, 640), BF16)] * 2,
        in_specs=[SMEM] * 2 + [VMEM] * 6 + [ANY] * 2,
        out_specs=[VMEM] * 2,
        scratch_shapes=[
            pltpu.VMEM((32, 1280), F32),
            pltpu.VMEM((256, 128), F32),
            pltpu.VMEM((256, 128), F32),
            pltpu.VMEM((256, 128), F32),
            pltpu.VMEM(keys.shape, BF16),
            pltpu.VMEM(values.shape, BF16),
            pltpu.SemaphoreType.DMA((4,)),
        ],
        cost_estimate=pl.CostEstimate(flops=70_000_000, bytes_accessed=1_000_000, transcendentals=131_072),
        compiler_params=pltpu.CompilerParams(vmem_limit_bytes=20 * 2**20),
        name="attend_all",
    )(plan, parity, used, low, mine, other, cos, sin, keys, values)


def amend_kernel(
    plan_ref, parity_ref, used_ref, row_ref, mine_ref, other_ref, cos_ref, sin_ref, key_ref, value_ref,
    keep_in, give_in, keep_ref, give_ref, query_ref,
):
    parity = parity_ref[0]
    first, last = plan_ref[64], plan_ref[65]
    here = ((first & 1) == parity) & ((last & 1) == parity)
    i = last >> 1
    one = pl.ds(i, 1)
    heads, key, value = project(
        parity, mine_ref[one, :], other_ref[one, :], row_ref[0:1, :], cos_ref[one, :], sin_ref[one, :]
    )
    for h in range(8):
        query_ref[h : h + 1, :] = heads[h]
    out = attend(query_ref[...], key, value, key_ref[...], value_ref[...], used_ref[last])
    keep, give = split(parity, [out[h : h + 1] for h in range(8)], key, value)
    hit = (lax.broadcasted_iota(jnp.int32, (32, 640), 0) == i) & here
    keep_ref[...] = jnp.where(hit, keep, keep_in[...].astype(F32)).astype(BF16)
    give_ref[...] = jnp.where(hit, give, give_in[...].astype(F32)).astype(BF16)


def amend(plan, parity, used, row, mine, other, cos, sin, keys, values, keep, give):
    return pl.pallas_call(
        amend_kernel,
        out_shape=[jax.ShapeDtypeStruct((32, 640), BF16)] * 2,
        in_specs=[SMEM] * 3 + [VMEM] * 9,
        out_specs=[VMEM] * 2,
        scratch_shapes=[pltpu.VMEM((8, 128), F32)],
        cost_estimate=pl.CostEstimate(flops=2_000_000, bytes_accessed=500_000, transcendentals=4096),
        compiler_params=pltpu.CompilerParams(vmem_limit_bytes=4 * 2**20),
        name="amend",
    )(plan, parity, used, row, mine, other, cos, sin, keys, values, keep, give)


def pick_kernel(plan_ref, low_ref, row_ref):
    row_ref[...] = low_ref[plan_ref[plan_ref[64]]]


def pick(plan, low):
    return pl.pallas_call(
        pick_kernel,
        out_shape=jax.ShapeDtypeStruct((1, 1280), F32),
        in_specs=[SMEM, VMEM],
        out_specs=VMEM,
        compiler_params=pltpu.CompilerParams(vmem_limit_bytes=2 * 2**20),
        name="pick",
    )(plan, low)


def weave_kernel(parity_ref, keep_ref, back_ref, out_ref, key_ref, value_ref, rows_ref):
    even, odd = sides(parity_ref[0], keep_ref[...].astype(F32), back_ref[...].astype(F32))
    for c in range(5):
        cols = slice(c * 128, (c + 1) * 128)
        rows_ref[pl.ds(0, 32, 2), :] = even[:, cols]
        rows_ref[pl.ds(1, 32, 2), :] = odd[:, cols]
        both = rows_ref[...].astype(BF16)
        if c < 4:
            out_ref[:, cols] = both
        else:
            key_ref[...] = both[:, 0:64]
            value_ref[...] = both[:, 64:128]


def weave(parity, keep, back):
    return pl.pallas_call(
        weave_kernel,
        out_shape=[
            jax.ShapeDtypeStruct((64, 512), BF16),
            jax.ShapeDtypeStruct((64, 64), BF16),
            jax.ShapeDtypeStruct((64, 64), BF16),
        ],
        in_specs=[SMEM, VMEM, VMEM],
        out_specs=[VMEM] * 3,
        scratch_shapes=[pltpu.VMEM((64, 128), F32)],
        compiler_params=pltpu.CompilerParams(vmem_limit_bytes=2 * 2**20),
        name="weave",
    )(parity, keep, back)


def local(
    hidden, wq, wk, wv, down_maps, up_maps, key_cache, value_cache, filled, positions, requests, slots
):
    t = lax.axis_index("tensor")
    parity = t & 1
    z, y = t & 3, t >> 2
    swap = [(i, i ^ 1) for i in range(16)]

    def z_turn(k):
        return [(4 * a + b, 4 * a + (b + k) % 4) for a in range(4) for b in range(4)]

    def y_turn(k):
        return [(4 * a + b, 4 * ((a + k) % 4) + b) for a in range(4) for b in range(4)]

    sent, plan = prepare(requests, slots, hidden)
    rows = jnp.swapaxes(hidden.reshape(32, 2, 512), 0, 1).reshape(64, 512)
    around_z = [rows] + [lax.ppermute(rows, "tensor", z_turn(k)) for k in (1, 2, 3)]
    recv = lax.all_to_all(sent, ROUTE, 0, 0, tiled=True)
    band = jnp.stack(around_z)
    bands = [band] + [lax.ppermute(band, "tensor", y_turn(k)) for k in (1, 2, 3)]

    low_sent = owner_low(
        recv, down_maps.reshape(96, 8192), up_maps.reshape(32, 10240)
    )
    low_sent, *bands = lax.optimization_barrier((low_sent, *bands))
    low = lax.all_to_all(low_sent, ROUTE, 0, 0, tiled=True)

    turns = jnp.arange(16)
    order = 4 * ((y - (turns >> 2)) & 3) + ((z - turns) & 3)
    order = jnp.concatenate([order, parity[None]]).astype(jnp.int32)
    mine, give, key2, value2 = base_project(
        order, plan, bands, wq, wk.T, wv.T, key_cache[0], value_cache[0], low_sent
    )
    other = lax.ppermute(give, "tensor", swap)

    pos = lax.dynamic_index_in_dim(positions.reshape(32, 2), parity, 1, keepdims=False)
    freq = THETA ** (-2.0 * jnp.arange(64, dtype=F32) / HEAD)
    angle = pos.astype(F32)[:, None] * freq[None, :]
    cos, sin = jnp.cos(angle), jnp.sin(angle)
    cos, sin = jnp.concatenate([cos, cos], 1), jnp.concatenate([-sin, sin], 1)

    which = parity.reshape(1)
    row = lax.ppermute(pick(plan, low), "tensor", swap)
    keys, values = in_hbm(key_cache[0], value_cache[0])
    used = lax.dynamic_index_in_dim(filled.reshape(32, 2), parity, 1, keepdims=False)
    used = jnp.repeat(used, 8).reshape(2, 128)
    keep, give = attend_all(plan, which, used, low, mine, other, cos, sin, keys, values)
    keep, give = amend(
        plan, which, filled, row, mine, other, cos, sin, key2, value2, keep, give
    )
    back = lax.ppermute(give, "tensor", swap)
    return tuple(weave(which, keep, back))


def solution(mesh):
    return jax.shard_map(
        local,
        mesh=mesh,
        in_specs=(
            P("dp", "tensor"),
            P(None, "tensor"),
            P(None, "tensor"),
            P(None, "tensor"),
            P(("dp", "tensor"), None, None),
            P(("dp", "tensor"), None, None),
            P("tensor", "dp", None, None),
            P("tensor", "dp", None, None),
            P("dp"),
            P("dp"),
            P("dp", None),
            P("dp"),
        ),
        out_specs=(P("dp", "tensor"), P("dp", "tensor"), P("dp", "tensor")),
        check_vma=False,
    )
```

time: 99.7 us -> 73.1 us (0.73)
  local copies, waits for them, and re-layouts: 14.5 us -> 1.53 us
  waiting for transfers between devices: 31.3 us -> 18.9 us
  Pallas kernels: 7.9 us -> 19.9 us
  other arithmetic: 6.11 us -> 0.53 us
  matrix products: 5.57 us -> 0 us
  starting transfers between devices: 32.7 us -> 31.1 us
    pallas_call x3 -> x7, Pallas kernels: 7.9 us -> 19.9 us  [the longest x1 6.2 us: attend_all(): pl.pallas_call(attend_kernel, out_shape=[jax.ShapeDtypeStruct((32, 640),...]
    all_to_all x1, waiting for transfers between devices: 15.3 us -> 6.81 us  [local(): low = lax.all_to_all(low_sent, ROUTE, 0, 0, tiled=True)]
    unnamed x27 -> x4, local copies, waits for them, and re-layouts: 7.01 us -> 0.01 us
    ppermute x3, waiting for transfers between devices: 10.5 us -> 3.51 us  [local(): lax.ppermute(band, 'tensor', y_turn(k))]
    all_to_all x1, waiting for transfers between devices: 0.01 us -> 6.19 us  [local(): recv = lax.all_to_all(sent, ROUTE, 0, 0, tiled=True)]
    dot_general x4 -> x0, matrix products: 5.57 us -> none  [the longest x1 3.6 us: attend_block(): jnp.einsum('sgd,scd->sgc', query_rot, key_rows, preferred_element_type=F32)]
    ppermute x5, waiting for transfers between devices: 3.41 us -> 0.01 us  [the longest x3 0.01 us: local(): lax.ppermute(rows, 'tensor', z_turn(k))]
    reshape x7 -> x3, local copies, waits for them, and re-layouts: 3.84 us -> 0.99 us  [the longest x2 0.89 us: local(): rows = jnp.swapaxes(hidden.reshape(32, 2, 512), 0, 1).reshape(64, 512)]
  transfers between devices with their start and end apart: 11 -> 11, of which waited for: 5 -> 4; matrix products, arithmetic and copies ran while one was open for 12% -> 2% of each run, Pallas kernels for 7% -> 25%
where the time goes in v2:
time: 73.1 us; the launch traced here: 72.8 us
  starting transfers between devices  31.1 us (43%)
  Pallas kernels  19.9 us (27%)
  waiting for transfers between devices  18.9 us (26%)
  local copies, waits for them, and re-layouts  1.53 us (2%)
  between operations  0.83 us (1%)
    all_to_all x1, starting transfers between devices, local(): recv = lax.all_to_all(sent, ROUTE, 0, 0, tiled=True)  8.05 us
    all_to_all x1, starting transfers between devices, local(): low = lax.all_to_all(low_sent, ROUTE, 0, 0, tiled=True)  7.88 us
    all_to_all x1, waiting for transfers between devices, local(): low = lax.all_to_all(low_sent, ROUTE, 0, 0, tiled=True)  6.81 us
    ppermute x3, starting transfers between devices, local(): lax.ppermute(rows, 'tensor', z_turn(k))  6.66 us
    pallas_call x1, Pallas kernels, attend_all(): pl.pallas_call(attend_kernel, out_shape=[jax.ShapeDtypeStruct((32, 640),...  6.2 us
    all_to_all x1, waiting for transfers between devices, local(): recv = lax.all_to_all(sent, ROUTE, 0, 0, tiled=True)  6.19 us
    pallas_call x1, Pallas kernels, base_project(): pl.pallas_call(base_kernel, out_shape=[jax.ShapeDtypeStruct((32, 640), F3...  5.77 us
    ppermute x3, starting transfers between devices, local(): lax.ppermute(band, 'tensor', y_turn(k))  5.17 us
  transfers between devices with their start and end apart: 11, of which 4 were waited for; matrix products, arithmetic and copies ran while one was open for 2% of the time, Pallas kernels for 25%

profile of v2, /device:TPU:0, one launch (start us, length us, event | category | flops | bytes accessed | tf_op | source)
XLA Modules:
  0.0 72.8 jit_solution(15273296601384313818)
XLA Ops:
  0.7 0.9 %reshape.38 = bf16[32,2,512]{2,1,0:T(2,128)(2,1)S(1)} reshape(bf16[64,512]{1,0:T(8,128)(2,1)} %hidden_hbm.1) | data formatting | bytes 131072 | tf_op jit(solution)/shard_map/reshape | solution.py:438
  1.6 2.1 %collective-permute-start = (bf16[64,512]{1,0:T(8,128)(2,1)S(1)}, bf16[64,512]{1,0:T(8,128)(2,1)S(1)}, u32[]{:S(2)}, u32[]{:S(2)}) collective-permute-start(bf16[64,512]{1,0:T(8,128)(2,1)S(1)} %bitcast.23), channel_id=1, source_target_pairs={{0,1},{1,2},{2,3},{3,0},{4,5},{5,6},{6,7},{7,4},{8,9},{9,10},{10,1... | collective-permute-start | bytes 196616 | tf_op jit(solution)/shard_map/ppermute | solution.py:439
  3.6 3.6 %collective-permute-start.1 = (bf16[64,512]{1,0:T(8,128)(2,1)S(1)}, bf16[64,512]{1,0:T(8,128)(2,1)S(1)}, u32[]{:S(2)}, u32[]{:S(2)}) collective-permute-start(bf16[64,512]{1,0:T(8,128)(2,1)S(1)} %bitcast.24), channel_id=1, source_target_pairs={{0,2},{1,3},{2,0},{3,1},{4,6},{5,7},{6,4},{7,5},{8,10},{9,11},{10,... | collective-permute-start | bytes 196616 | tf_op jit(solution)/shard_map/ppermute | solution.py:439
  7.2 1.0 %collective-permute-start.2 = (bf16[64,512]{1,0:T(8,128)(2,1)S(1)}, bf16[64,512]{1,0:T(8,128)(2,1)S(1)}, u32[]{:S(2)}, u32[]{:S(2)}) collective-permute-start(bf16[64,512]{1,0:T(8,128)(2,1)S(1)} %bitcast.25), channel_id=1, source_target_pairs={{0,3},{1,0},{2,1},{3,2},{4,7},{5,4},{6,5},{7,6},{8,11},{9,8},{10,9... | collective-permute-start | bytes 196616 | tf_op jit(solution)/shard_map/ppermute | solution.py:439
  8.2 2.4 %prepare.1 = (bf16[128,2,640]{2,1,0:T(2,128)(2,1)}, s32[66]{0:T(128)S(1)}) custom-call(s32[1,63]{1,0:T(1,128)} %requests_hbm.1, s32[64]{0:T(128)} %slots_hbm.1, bf16[64,512]{1,0:T(8,128)(2,1)} %hidden_hbm.1), custom_call_target="tpu_custom_call" | custom-call | flops 1000000 | bytes 500000 | tf_op jit(solution)/shard_map/prepare/pallas_call | solution.py:65
  10.7 8.0 %all-to-all-start = ((bf16[128,2,640]{2,1,0:T(2,128)(2,1)}), bf16[128,2,640]{2,1,0:T(2,128)(2,1)S(1)}, u32[]{:S(2)}, u32[]{:S(2)}) async-start(bf16[128,2,640]{2,1,0:T(2,128)(2,1)} %get-tuple-element.19), calls=%async_computation | async-start | bytes 655360 | tf_op jit(solution)/shard_map/all_to_all | solution.py:440
  18.8 1.0 %collective-permute-start.3 = (bf16[4,64,512]{2,1,0:T(8,128)(2,1)S(1)}, bf16[4,64,512]{2,1,0:T(8,128)(2,1)S(1)}, u32[]{:S(2)}, u32[]{:S(2)}) collective-permute-start(bf16[4,64,512]{2,1,0:T(8,128)(2,1)S(1)} %pad_maximum_fusion.h0_ref), channel_id=1, source_target_pairs={{0,4},{1,5},{2,6},{3,7},{4,8},{5,9},{6,10},{7,11},{8,12},{9,13},{1... | collective-permute-start | bytes 786440 | tf_op jit(solution)/shard_map/ppermute | solution.py:442
  19.8 2.7 %collective-permute-start.4 = (bf16[4,64,512]{2,1,0:T(8,128)(2,1)S(1)}, bf16[4,64,512]{2,1,0:T(8,128)(2,1)S(1)}, u32[]{:S(2)}, u32[]{:S(2)}) collective-permute-start(bf16[4,64,512]{2,1,0:T(8,128)(2,1)S(1)} %pad_maximum_fusion.h0_ref), channel_id=1, source_target_pairs={{0,8},{1,9},{2,10},{3,11},{4,12},{5,13},{6,14},{7,15},{8,0},{9,1},... | collective-permute-start | bytes 786440 | tf_op jit(solution)/shard_map/ppermute | solution.py:442
  22.5 1.4 %collective-permute-start.5 = (bf16[4,64,512]{2,1,0:T(8,128)(2,1)S(1)}, bf16[4,64,512]{2,1,0:T(8,128)(2,1)S(1)}, u32[]{:S(2)}, u32[]{:S(2)}) collective-permute-start(bf16[4,64,512]{2,1,0:T(8,128)(2,1)S(1)} %pad_maximum_fusion.h0_ref), channel_id=1, source_target_pairs={{0,12},{1,13},{2,14},{3,15},{4,0},{5,1},{6,2},{7,3},{8,4},{9,5},{1... | collective-permute-start | bytes 786440 | tf_op jit(solution)/shard_map/ppermute | solution.py:442
  24.0 6.2 %all-to-all-done.recv_ref = bf16[128,2,640]{2,1,0:T(2,128)(2,1)S(1)} async-done(((bf16[128,2,640]{2,1,0:T(2,128)(2,1)}), bf16[128,2,640]{2,1,0:T(2,128)(2,1)S(1)}, u32[]{:S(2)}, u32[]{:S(2)}) %all-to-all-start) | async-done | bytes 327712 | tf_op jit(solution)/shard_map/all_to_all | solution.py:440
  30.2 3.2 %owner_low.1._ = f32[128,1,1280]{2,1,0:T(1,128)} custom-call(bf16[128,2,640]{2,1,0:T(2,128)(2,1)S(1)} %all-to-all-done.recv_ref, bf16[96,8192]{1,0:T(8,128)(2,1)} %bitcast.19, bf16[32,10240]{1,0:T(8,128)(2,1)} %bitcast.22), custom_call_target="tpu_custom_call" | custom-call | flops 40000000 | bytes 3400000 | tf_op jit(solution)/shard_map/owner_low/pallas_call | solution.py:134
  33.4 3.5 %collective-permute-done.4.h2_ref = bf16[4,64,512]{2,1,0:T(8,128)(2,1)S(1)} collective-permute-done((bf16[4,64,512]{2,1,0:T(8,128)(2,1)S(1)}, bf16[4,64,512]{2,1,0:T(8,128)(2,1)S(1)}, u32[]{:S(2)}, u32[]{:S(2)}) %collective-permute-start.4) | collective-permute-done | bytes 262176 | tf_op jit(solution)/shard_map/ppermute | solution.py:442
  36.9 7.9 %all-to-all-start.1 = ((f32[128,1,1280]{2,1,0:T(1,128)}), f32[128,1,1280]{2,1,0:T(1,128)S(1)}, u32[]{:S(2)}, u32[]{:S(2)}) async-start(f32[128,1,1280]{2,1,0:T(1,128)} %owner_low.1._), calls=%async_computation.1 | async-start | bytes 1310720 | tf_op jit(solution)/shard_map/all_to_all | solution.py:448
  45.5 0.2 convert_reduce_fusion
  45.9 5.8 %base_project.1 = (f32[32,640]{1,0:T(8,128)S(1)}, f32[32,640]{1,0:T(8,128)S(1)}, bf16[512,128]{1,0:T(8,128)(2,1)S(1)}, bf16[512,128]{1,0:T(8,128)(2,1)S(1)}) custom-call(s32[17]{0:T(128)S(1)} %pad_add_fusion.order_ref, s32[66]{0:T(128)S(1)} %get-tuple-element.18.plan_ref, bf16[4,64,512]{2,1,0:T(8,128)(2,1)S(1)} %pad_maximum_fusion.h0_ref, ...), custom_call_target="tpu_custom_call" | custom-call | flops 671000000 | bytes 11700000 | tf_op jit(solution)/shard_map/base_project/pallas_call | solution.py:198
  51.7 1.2 %collective-permute-start.7 = (f32[32,640]{1,0:T(8,128)S(1)}, f32[32,640]{1,0:T(8,128)S(1)}, u32[]{:S(2)}, u32[]{:S(2)}) collective-permute-start(f32[32,640]{1,0:T(8,128)S(1)} %get-tuple-element.26), channel_id=1, source_target_pairs={{0,1},{1,0},{2,3},{3,2},{4,5},{5,4},{6,7},{7,6},{8,9},{9,8},{10,11... | collective-permute-start | bytes 245768 | tf_op jit(solution)/shard_map/ppermute | solution.py:456
  52.9 6.8 %all-to-all-done.1.low_ref = f32[128,1,1280]{2,1,0:T(1,128)S(1)} async-done(((f32[128,1,1280]{2,1,0:T(1,128)}), f32[128,1,1280]{2,1,0:T(1,128)S(1)}, u32[]{:S(2)}, u32[]{:S(2)}) %all-to-all-start.1) | async-done | bytes 655392 | tf_op jit(solution)/shard_map/all_to_all | solution.py:448
  59.7 0.5 pick.1
  60.3 0.5 collective-permute-start.6
  60.8 6.2 %attend_all.1 = (bf16[32,640]{1,0:T(8,128)(2,1)S(1)}, bf16[32,640]{1,0:T(8,128)(2,1)S(1)}) custom-call(s32[66]{0:T(128)S(1)} %get-tuple-element.18.plan_ref, s32[1]{0:T(128)} %bitcast.parity_ref, s32[2,128]{1,0:T(2,128)S(1)} %broadcast_in_dim.12.used_ref, f32[128,1,1280]{2,1,0:T(1,128)S(1)} %all-to-all-done.1.low_ref, ...), custom_call_target="tpu_custom_call" | custom-call | flops 70000000 | bytes 1000000 | tf_op jit(solution)/shard_map/attend_all/pallas_call | solution.py:324
  67.0 1.0 %amend.1 = (bf16[32,640]{1,0:T(8,128)(2,1)S(1)}, bf16[32,640]{1,0:T(8,128)(2,1)S(1)}) custom-call(s32[66]{0:T(128)S(1)} %get-tuple-element.18.plan_ref, s32[1]{0:T(128)} %bitcast.parity_ref, s32[64]{0:T(128)S(1)} %copy-done, f32[1,1280]{1,0:T(1,128)S(1)} %collective-permute-done.6.row_ref, f32[32,640]{1,0:T(8,128)S(1)} %get-tuple-element.25.mine_ref, ...), custom_call_target="tpu_custom_call" | custom-call | flops 2000000 | bytes 500000 | tf_op jit(solution)/shard_map/amend/pallas_call | solution.py:366
  68.0 1.7 %collective-permute-start.8 = (bf16[32,640]{1,0:T(8,128)(2,1)S(1)}, bf16[32,640]{1,0:T(8,128)(2,1)S(1)}, u32[]{:S(2)}, u32[]{:S(2)}) collective-permute-start(bf16[32,640]{1,0:T(8,128)(2,1)S(1)} %get-tuple-element.32), channel_id=1, source_target_pairs={{0,1},{1,0},{2,3},{3,2},{4,5},{5,4},{6,7},{7,6},{8,9},{9,8},{10,11... | collective-permute-start | bytes 122888 | tf_op jit(solution)/shard_map/ppermute | solution.py:473
  69.7 2.4 %collective-permute-done.8.back_ref = bf16[32,640]{1,0:T(8,128)(2,1)S(1)} collective-permute-done((bf16[32,640]{1,0:T(8,128)(2,1)S(1)}, bf16[32,640]{1,0:T(8,128)(2,1)S(1)}, u32[]{:S(2)}, u32[]{:S(2)}) %collective-permute-start.8) | collective-permute-done | bytes 40992 | tf_op jit(solution)/shard_map/ppermute | solution.py:473
  72.1 0.7 weave.1
  (24 shorter events, 1.0 us)
Async XLA Ops:
  0.6 44.2 %copy-start.1 = (s32[64]{0:T(128)S(1)}, s32[64]{0:T(128)}, u32[]{:S(2)}) copy-start(s32[64]{0:T(128)} %param.21) | copy-start | bytes 772
  0.6 44.3 %copy-start = (s32[64]{0:T(128)S(1)}, s32[64]{0:T(128)}, u32[]{:S(2)}) copy-start(s32[64]{0:T(128)} %used_ref.1) | copy-start | bytes 772
  1.6 17.2 %collective-permute-start = (bf16[64,512]{1,0:T(8,128)(2,1)S(1)}, bf16[64,512]{1,0:T(8,128)(2,1)S(1)}, u32[]{:S(2)}, u32[]{:S(2)}) collective-permute-start(bf16[64,512]{1,0:T(8,128)(2,1)S(1)} %bitcast.23), channel_id=1, source_target_pairs={{0,1},{1,2},{2,3},{3,0},{4,5},{5,6},{6,7},{7,4},{8,9},{9,10},{10,1... | collective-permute-start | bytes 196616 | tf_op jit(solution)/shard_map/ppermute | solution.py:439
  3.6 15.1 %collective-permute-start.1 = (bf16[64,512]{1,0:T(8,128)(2,1)S(1)}, bf16[64,512]{1,0:T(8,128)(2,1)S(1)}, u32[]{:S(2)}, u32[]{:S(2)}) collective-permute-start(bf16[64,512]{1,0:T(8,128)(2,1)S(1)} %bitcast.24), channel_id=1, source_target_pairs={{0,2},{1,3},{2,0},{3,1},{4,6},{5,7},{6,4},{7,5},{8,10},{9,11},{10,... | collective-permute-start | bytes 196616 | tf_op jit(solution)/shard_map/ppermute | solution.py:439
  7.2 11.5 %collective-permute-start.2 = (bf16[64,512]{1,0:T(8,128)(2,1)S(1)}, bf16[64,512]{1,0:T(8,128)(2,1)S(1)}, u32[]{:S(2)}, u32[]{:S(2)}) collective-permute-start(bf16[64,512]{1,0:T(8,128)(2,1)S(1)} %bitcast.25), channel_id=1, source_target_pairs={{0,3},{1,0},{2,1},{3,2},{4,7},{5,4},{6,5},{7,6},{8,11},{9,8},{10,9... | collective-permute-start | bytes 196616 | tf_op jit(solution)/shard_map/ppermute | solution.py:439
  10.7 19.5 %all-to-all-start = ((bf16[128,2,640]{2,1,0:T(2,128)(2,1)}), bf16[128,2,640]{2,1,0:T(2,128)(2,1)S(1)}, u32[]{:S(2)}, u32[]{:S(2)}) async-start(bf16[128,2,640]{2,1,0:T(2,128)(2,1)} %get-tuple-element.19), calls=%async_computation | async-start | bytes 655360 | tf_op jit(solution)/shard_map/all_to_all | solution.py:440
  18.8 14.6 %collective-permute-start.3 = (bf16[4,64,512]{2,1,0:T(8,128)(2,1)S(1)}, bf16[4,64,512]{2,1,0:T(8,128)(2,1)S(1)}, u32[]{:S(2)}, u32[]{:S(2)}) collective-permute-start(bf16[4,64,512]{2,1,0:T(8,128)(2,1)S(1)} %pad_maximum_fusion.h0_ref), channel_id=1, source_target_pairs={{0,4},{1,5},{2,6},{3,7},{4,8},{5,9},{6,10},{7,11},{8,12},{9,13},{1... | collective-permute-start | bytes 786440 | tf_op jit(solution)/shard_map/ppermute | solution.py:442
  19.8 17.1 %collective-permute-start.4 = (bf16[4,64,512]{2,1,0:T(8,128)(2,1)S(1)}, bf16[4,64,512]{2,1,0:T(8,128)(2,1)S(1)}, u32[]{:S(2)}, u32[]{:S(2)}) collective-permute-start(bf16[4,64,512]{2,1,0:T(8,128)(2,1)S(1)} %pad_maximum_fusion.h0_ref), channel_id=1, source_target_pairs={{0,8},{1,9},{2,10},{3,11},{4,12},{5,13},{6,14},{7,15},{8,0},{9,1},... | collective-permute-start | bytes 786440 | tf_op jit(solution)/shard_map/ppermute | solution.py:442
  22.5 14.4 %collective-permute-start.5 = (bf16[4,64,512]{2,1,0:T(8,128)(2,1)S(1)}, bf16[4,64,512]{2,1,0:T(8,128)(2,1)S(1)}, u32[]{:S(2)}, u32[]{:S(2)}) collective-permute-start(bf16[4,64,512]{2,1,0:T(8,128)(2,1)S(1)} %pad_maximum_fusion.h0_ref), channel_id=1, source_target_pairs={{0,12},{1,13},{2,14},{3,15},{4,0},{5,1},{6,2},{7,3},{8,4},{9,5},{1... | collective-permute-start | bytes 786440 | tf_op jit(solution)/shard_map/ppermute | solution.py:442
  36.9 22.8 %all-to-all-start.1 = ((f32[128,1,1280]{2,1,0:T(1,128)}), f32[128,1,1280]{2,1,0:T(1,128)S(1)}, u32[]{:S(2)}, u32[]{:S(2)}) async-start(f32[128,1,1280]{2,1,0:T(1,128)} %owner_low.1._), calls=%async_computation.1 | async-start | bytes 1310720 | tf_op jit(solution)/shard_map/all_to_all | solution.py:448
  51.7 9.1 %collective-permute-start.7 = (f32[32,640]{1,0:T(8,128)S(1)}, f32[32,640]{1,0:T(8,128)S(1)}, u32[]{:S(2)}, u32[]{:S(2)}) collective-permute-start(f32[32,640]{1,0:T(8,128)S(1)} %get-tuple-element.26), channel_id=1, source_target_pairs={{0,1},{1,0},{2,3},{3,2},{4,5},{5,4},{6,7},{7,6},{8,9},{9,8},{10,11... | collective-permute-start | bytes 245768 | tf_op jit(solution)/shard_map/ppermute | solution.py:456
  60.3 6.7 %collective-permute-start.6 = (f32[1,1280]{1,0:T(1,128)S(1)}, f32[1,1280]{1,0:T(1,128)S(1)}, u32[]{:S(2)}, u32[]{:S(2)}) collective-permute-start(f32[1,1280]{1,0:T(1,128)S(1)} %pick.1), channel_id=1, source_target_pairs={{0,1},{1,0},{2,3},{3,2},{4,5},{5,4},{6,7},{7,6},{8,9},{9,8},{10,11... | collective-permute-start | bytes 15368 | tf_op jit(solution)/shard_map/ppermute | solution.py:465
  68.0 4.1 %collective-permute-start.8 = (bf16[32,640]{1,0:T(8,128)(2,1)S(1)}, bf16[32,640]{1,0:T(8,128)(2,1)S(1)}, u32[]{:S(2)}, u32[]{:S(2)}) collective-permute-start(bf16[32,640]{1,0:T(8,128)(2,1)S(1)} %get-tuple-element.32), channel_id=1, source_target_pairs={{0,1},{1,0},{2,3},{3,2},{4,5},{5,4},{6,7},{7,6},{8,9},{9,8},{10,11... | collective-permute-start | bytes 122888 | tf_op jit(solution)/shard_map/ppermute | solution.py:473

commit v3 on v2

--- a/solution.py
+++ b/solution.py
@@ -23,15 +23,19 @@
 
 
 def prepare_kernel(
-    requests_hbm, slots_hbm, hidden_hbm, sent_ref, plan_ref,
-    rows_ref, wide_ref, hidden_ref, requests_ref, slots_ref, sems,
+    requests_hbm, slots_hbm, hidden_hbm, down_hbm, up_hbm, sent_ref, plan_ref, down_ref, up_ref, hidden_ref,
+    rows_ref, wide_ref, requests_ref, slots_ref, sems,
 ):
     copies = [
         pltpu.make_async_copy(requests_hbm, requests_ref, sems.at[0]),
         pltpu.make_async_copy(slots_hbm, slots_ref, sems.at[1]),
         pltpu.make_async_copy(hidden_hbm, hidden_ref, sems.at[2]),
     ]
-    for copy in copies:
+    maps = [
+        pltpu.make_async_copy(down_hbm, down_ref, sems.at[3]),
+        pltpu.make_async_copy(up_hbm, up_ref, sems.at[4]),
+    ]
+    for copy in copies + maps:
         copy.start()
     rows_ref[...] = jnp.zeros_like(rows_ref)
     for copy in copies:
@@ -55,50 +59,59 @@
     plan_ref[64] = first
     plan_ref[65] = last
     sent_ref[...] = rows_ref[...].astype(BF16)
+    for copy in maps:
+        copy.wait()
 
 
 def in_hbm(*arrays):
     return [pltpu.with_memory_space_constraint(x, pltpu.HBM) for x in arrays]
 
 
-def prepare(requests, slots, hidden):
+def prepare(requests, slots, hidden, down, up):
     return pl.pallas_call(
         prepare_kernel,
         out_shape=[
-            jax.ShapeDtypeStruct((128, 2, 640), BF16),
+            pltpu.HBM((128, 2, 640), BF16),
             jax.ShapeDtypeStruct((66,), jnp.int32),
-        ],
-        in_specs=[ANY] * 3,
-        out_specs=[VMEM, SMEM],
+            pltpu.VMEM(down.shape, BF16),
+            pltpu.VMEM(up.shape, BF16),
+            pltpu.VMEM(hidden.shape, BF16),
+        ],
+        in_specs=[ANY] * 5,
+        out_specs=[VMEM, SMEM, ANY, ANY, VMEM],
         scratch_shapes=[
             pltpu.VMEM((128, 2, 640), F32),
             pltpu.VMEM((64, 640), F32),
-            pltpu.VMEM((64, 512), BF16),
             pltpu.SMEM((1, 63), jnp.int32),
             pltpu.SMEM((64,), jnp.int32),
-            pltpu.SemaphoreType.DMA((3,)),
+            pltpu.SemaphoreType.DMA((5,)),
         ],
         cost_estimate=pl.CostEstimate(flops=1_000_000, bytes_accessed=500_000, transcendentals=0),
         compiler_params=pltpu.CompilerParams(vmem_limit_bytes=4 * 2**20),
         name="prepare",
-    )(*in_hbm(requests, slots, hidden))
-
-
-def owner_kernel(recv_ref, down_hbm, up_hbm, out_ref, down_ref, up_ref, coords_ref, code_ref, sems):
-    parts = [
-        pltpu.make_async_copy(
-            down_hbm.at[:, i * 2048 : (i + 1) * 2048], down_ref.at[:, i * 2048 : (i + 1) * 2048], sems.at[i]
-        )
-        for i in range(4)
-    ]
-    copy = pltpu.make_async_copy(up_hbm, up_ref, sems.at[4])
-    for part in parts:
-        part.start()
-    copy.start()
+    )(*in_hbm(requests, slots, hidden, down, up))
+
+
+def band_kernel(_, h0_ref, h1_ref, h2_ref, h3_ref, out_ref):
+    for k, ref in enumerate((h0_ref, h1_ref, h2_ref, h3_ref)):
+        out_ref[k] = ref[...]
+
+
+def stack_band(plan, blocks):
+    return pl.pallas_call(
+        band_kernel,
+        out_shape=jax.ShapeDtypeStruct((4, 64, 512), BF16),
+        in_specs=[SMEM] + [VMEM] * 4,
+        out_specs=VMEM,
+        cost_estimate=pl.CostEstimate(flops=1000, bytes_accessed=500_000, transcendentals=0),
+        compiler_params=pltpu.CompilerParams(vmem_limit_bytes=4 * 2**20),
+        name="stack_band",
+    )(plan, *blocks)
+
+
+def owner_kernel(recv_ref, down_ref, up_ref, out_ref, coords_ref, code_ref):
     acc = jnp.zeros((16, 96), F32)
     for t in range(16):
-        if t % 4 == 0:
-            parts[t // 4].wait()
         acc = acc + dot_nt(
             recv_ref[t * 8 : (t + 1) * 8, :, 0:512].reshape(16, 512),
             down_ref[:, t * 512 : (t + 1) * 512],
@@ -117,7 +130,6 @@
             [coords[:, a * 24 + b * 8 : a * 24 + b * 8 + 8] for a in range(4)], axis=1
         )
         blocks.append(jnp.where(mine, block, 0.0).astype(BF16))
-    copy.wait()
     low_key = dot(blocks[1], up_ref[:, 8192:9216])
     low_value = dot(blocks[2], up_ref[:, 9216:10240])
     for j in range(8):
@@ -134,88 +146,122 @@
     return pl.pallas_call(
         owner_kernel,
         out_shape=jax.ShapeDtypeStruct((128, 1, 1280), F32),
-        in_specs=[VMEM, ANY, ANY],
+        in_specs=[VMEM] * 3,
         out_specs=VMEM,
         scratch_shapes=[
-            pltpu.VMEM((96, 8192), BF16),
-            pltpu.VMEM((32, 10240), BF16),
             pltpu.VMEM((16, 128), F32),
             pltpu.VMEM((16, 128), F32),
-            pltpu.SemaphoreType.DMA((5,)),
         ],
         cost_estimate=pl.CostEstimate(flops=40_000_000, bytes_accessed=3_400_000, transcendentals=0),
         compiler_params=pltpu.CompilerParams(vmem_limit_bytes=8 * 2**20),
         name="owner_low",
-    )(recv, *in_hbm(down, up))
+    )(recv, down, up)
+
+
+def weight_copies(rows, wq_hbm, wk_hbm, wv_hbm, wq_ref, wkv_ref, sems):
+    copies = []
+    for i, row in enumerate(rows):
+        part = pl.ds(pl.multiple_of(row, 512), 512)
+        copies.append(
+            [
+                pltpu.make_async_copy(wk_hbm.at[:, part], wkv_ref.at[i, 0:64], sems.at[0, i]),
+                pltpu.make_async_copy(wv_hbm.at[:, part], wkv_ref.at[i, 64:128], sems.at[1, i]),
+                pltpu.make_async_copy(wq_hbm.at[part], wq_ref.at[i], sems.at[2, i]),
+            ]
+        )
+    for block in copies:
+        for copy in block:
+            copy.start()
+    return copies
+
+
+def add_blocks(hiddens, copies, wq_ref, wkv_ref, q, kv):
+    for i, hidden in enumerate(hiddens):
+        for copy in copies[i]:
+            copy.wait()
+        q = q + dot(hidden, wq_ref[i])
+        kv = kv + dot_nt(hidden, wkv_ref[i])
+    return q, kv
 
 
 def base_kernel(
-    order_ref, plan_ref, h0_ref, h1_ref, h2_ref, h3_ref, wq_hbm, wk_hbm, wv_hbm, key_hbm, value_hbm, _,
-    mine_ref, give_ref, key2_ref, value2_ref, wq_ref, wk_ref, wv_ref, acc_ref, sems,
+    place_ref, h0_ref, h1_ref, h3_ref, wq_hbm, wk_hbm, wv_hbm, _, out_ref, wq_ref, wkv_ref, sems
 ):
-    order = [order_ref[i] * 512 for i in range(16)]
-    parity = order_ref[16]
-    kv = [
-        pltpu.make_async_copy(wk_hbm, wk_ref, sems.at[16]),
-        pltpu.make_async_copy(wv_hbm, wv_ref, sems.at[17]),
+    y, z = place_ref[0], place_ref[1]
+    rows = [(((y - a) & 3) * 4 + ((z - b) & 3)) * 512 for a in (0, 1, 3) for b in range(4)]
+    copies = weight_copies(rows, wq_hbm, wk_hbm, wv_hbm, wq_ref, wkv_ref, sems)
+    hiddens = [ref[b] for ref in (h0_ref, h1_ref, h3_ref) for b in range(4)]
+    q, kv = add_blocks(
+        hiddens, copies, wq_ref, wkv_ref, jnp.zeros((64, 512), F32), jnp.zeros((64, 128), F32)
+    )
+    out_ref[:, 0:512] = q
+    out_ref[:, 512:640] = kv
+
+
+def rest_kernel(
+    place_ref, plan_ref, part_ref, ha_ref, hb_ref, wq_hbm, wk_hbm, wv_hbm, key_hbm, value_hbm,
+    mine_ref, give_ref, key2_ref, value2_ref, wq_ref, wkv_ref, acc_ref, sems, cache_sems,
+):
+    y, z = place_ref[0], place_ref[1]
+    rows = [(((y - 2) & 3) * 4 + ((z - b) & 3)) * 512 for b in range(4)]
+    copies = weight_copies(rows, wq_hbm, wk_hbm, wv_hbm, wq_ref, wkv_ref, sems)
+    cache = [
+        pltpu.make_async_copy(key_hbm.at[plan_ref[65] >> 1], key2_ref, cache_sems.at[0]),
+        pltpu.make_async_copy(value_hbm.at[plan_ref[65] >> 1], value2_ref, cache_sems.at[1]),
     ]
-    cache = [
-        pltpu.make_async_copy(key_hbm.at[plan_ref[65] >> 1], key2_ref, sems.at[18]),
-        pltpu.make_async_copy(value_hbm.at[plan_ref[65] >> 1], value2_ref, sems.at[19]),
-    ]
-    blocks = [
-        pltpu.make_async_copy(
-            wq_hbm.at[pl.ds(pl.multiple_of(order[i], 512), 512), :], wq_ref.at[i], sems.at[i]
-        )
-        for i in range(16)
-    ]
-    for copy in kv + blocks + cache:
+    for copy in cache:
         copy.start()
-    for copy in kv:
-        copy.wait()
-    q = jnp.zeros((64, 512), F32)
-    for i in range(16):
-        h = (h0_ref, h1_ref, h2_ref, h3_ref)[i // 4][i % 4]
-        cols = pl.ds(pl.multiple_of(order[i], 512), 512)
-        wkv = jnp.concatenate([wk_ref[:, cols], wv_ref[:, cols]], axis=0)
-        kv_part = dot_nt(h, wkv)
-        if i == 0:
-            acc_ref[:, 512:640] = kv_part
-        else:
-            acc_ref[:, 512:640] += kv_part
-        blocks[i].wait()
-        if i == 0:
-            acc_ref[:, 0:512] = dot(h, wq_ref[i])
-        else:
-            acc_ref[:, 0:512] += dot(h, wq_ref[i])
-    mine_ref[...] = acc_ref[pl.ds(pl.multiple_of(parity * 32, 32), 32), :]
-    give_ref[...] = acc_ref[pl.ds(pl.multiple_of((1 - parity) * 32, 32), 32), :]
+    hiddens = [ha_ref[0], ha_ref[1], hb_ref[0], hb_ref[1]]
+    q, kv = add_blocks(hiddens, copies, wq_ref, wkv_ref, part_ref[:, 0:512], part_ref[:, 512:640])
+    parity = z & 1
+    for c in range(5):
+        cols = slice(c * 128, (c + 1) * 128)
+        acc_ref[...] = q[:, cols] if c < 4 else kv
+        even, odd = acc_ref[pl.ds(0, 32, 2), :], acc_ref[pl.ds(1, 32, 2), :]
+        mine_ref[:, cols], give_ref[:, cols] = sides(parity, even, odd)
     for copy in cache:
         copy.wait()
 
 
-def base_project(order, plan, bands, wq, wkt, wvt, keys, values, after):
+def base_project(place, bands, wq, wkt, wvt, after):
     return pl.pallas_call(
         base_kernel,
+        out_shape=jax.ShapeDtypeStruct((64, 640), F32),
+        in_specs=[SMEM] + [VMEM] * 3 + [ANY] * 4,
+        out_specs=VMEM,
+        scratch_shapes=[
+            pltpu.VMEM((12, 512, 512), BF16),
+            pltpu.VMEM((12, 128, 512), BF16),
+            pltpu.SemaphoreType.DMA((3, 12)),
+        ],
+        cost_estimate=pl.CostEstimate(flops=503_000_000, bytes_accessed=8_800_000, transcendentals=0),
+        compiler_params=pltpu.CompilerParams(vmem_limit_bytes=16 * 2**20),
+        name="base_project",
+    )(place, *bands, *in_hbm(wq, wkt, wvt), after)
+
+
+def base_rest(place, plan, part, halves, wq, wkt, wvt, keys, values):
+    return pl.pallas_call(
+        rest_kernel,
         out_shape=[
             jax.ShapeDtypeStruct((32, 640), F32),
             jax.ShapeDtypeStruct((32, 640), F32),
             jax.ShapeDtypeStruct(keys.shape[1:], BF16),
             jax.ShapeDtypeStruct(values.shape[1:], BF16),
         ],
-        in_specs=[SMEM] * 2 + [VMEM] * 4 + [ANY] * 6,
+        in_specs=[SMEM] * 2 + [VMEM] * 3 + [ANY] * 5,
         out_specs=[VMEM] * 4,
         scratch_shapes=[
-            pltpu.VMEM((16, 512, 512), BF16),
-            pltpu.VMEM((64, 8192), BF16),
-            pltpu.VMEM((64, 8192), BF16),
-            pltpu.VMEM((64, 640), F32),
-            pltpu.SemaphoreType.DMA((20,)),
-        ],
-        cost_estimate=pl.CostEstimate(flops=671_000_000, bytes_accessed=11_700_000, transcendentals=0),
-        compiler_params=pltpu.CompilerParams(vmem_limit_bytes=16 * 2**20),
-        name="base_project",
-    )(order, plan, *bands, *in_hbm(wq, wkt, wvt, keys, values), after)
+            pltpu.VMEM((4, 512, 512), BF16),
+            pltpu.VMEM((4, 128, 512), BF16),
+            pltpu.VMEM((64, 128), F32),
+            pltpu.SemaphoreType.DMA((3, 4)),
+            pltpu.SemaphoreType.DMA((2,)),
+        ],
+        cost_estimate=pl.CostEstimate(flops=168_000_000, bytes_accessed=3_200_000, transcendentals=0),
+        compiler_params=pltpu.CompilerParams(vmem_limit_bytes=8 * 2**20),
+        name="base_rest",
+    )(place, plan, part, *halves, *in_hbm(wq, wkt, wvt, keys, values))
 
 
 def rotate(part, cos, sin):
@@ -263,7 +309,7 @@
 
 def attend_kernel(
     plan_ref, parity_ref, used_ref, low_ref, mine_ref, other_ref, cos_ref, sin_ref, key_hbm, value_hbm,
-    keep_ref, give_ref, rows_ref, query_ref, fresh_ref, out_ref, key_ref, value_ref, sems,
+    keep_ref, give_ref, rows_ref, query_ref, near_ref, fresh_ref, out_ref, key_ref, value_ref, sems,
 ):
     copies = []
     for g in range(4):
@@ -279,41 +325,34 @@
     )
     for h in range(8):
         query_ref[pl.ds(h, 32, 8), :] = heads[h]
+        near_ref[pl.ds(h, 32, 8), :] = key
         fresh_ref[pl.ds(h, 32, 8), :] = value
     scale = 1.0 / math.sqrt(HEAD)
-    lane = lax.broadcasted_iota(jnp.int32, (128, 128), 1) >> 3
-    near_key = key.astype(BF16)
     halves = []
     for half in range(2):
-        queries = query_ref[half * 128 : (half + 1) * 128, :].T
-        spread = jnp.concatenate(
-            [jnp.where(lane == s, queries, 0.0).astype(BF16) for s in range(16)], axis=0
-        )
-        near = jnp.concatenate(
-            [near_key[half * 16 + s : half * 16 + s + 1, :] for s in range(16)], axis=1
-        )
-        own = dot(jnp.broadcast_to(near, (16, 2048)), spread)[0:1] * scale
+        rows = slice(half * 128, (half + 1) * 128)
+        query = query_ref[rows, :]
+        own = jnp.sum(query * near_ref[rows, :], axis=1, keepdims=True) * scale
         copies[half].wait()
-        block = jnp.concatenate([key_ref[half * 16 + s] for s in range(16)], axis=1)
-        scores = dot(block, spread) * scale
-        valid = lax.broadcasted_iota(jnp.int32, (512, 128), 0) < used_ref[half : half + 1, :]
-        top = jnp.max(jnp.where(valid, scores, -jnp.inf), axis=0, keepdims=True)
+        scores = jnp.concatenate(
+            [dot_nt(query[s * 8 : s * 8 + 8].astype(BF16), key_ref[half * 16 + s]) for s in range(16)], axis=0
+        ) * scale
+        valid = lax.broadcasted_iota(jnp.int32, (128, 512), 1) < used_ref[rows, :]
+        top = jnp.max(jnp.where(valid, scores, -jnp.inf), axis=1, keepdims=True)
         top = jnp.maximum(top, own)
         weights = jnp.where(valid, jnp.exp(scores - top), 0.0)
         own_weight = jnp.exp(own - top)
-        total = jnp.sum(weights, axis=0, keepdims=True) + own_weight
-        pair = jnp.concatenate([own_weight, total, jnp.zeros((6, 128), F32)], axis=0).T
-        halves.append((weights.T.astype(BF16), pair))
+        total = jnp.sum(weights, axis=1, keepdims=True) + own_weight
+        halves.append((weights.astype(BF16), own_weight, total))
     for half in range(2):
         copies[2 + half].wait()
-        weights, pair = halves[half]
+        weights, own_weight, total = halves[half]
         rows = slice(half * 128, (half + 1) * 128)
-        own = pair[:, 0:1].astype(BF16).astype(F32) * fresh_ref[rows, :]
-        total = pair[:, 1:2]
-        for s in range(16):
-            eight = slice(s * 8, (s + 1) * 8)
-            out = dot(weights[eight], value_ref[half * 16 + s])
-            out_ref[half * 128 + s * 8 : half * 128 + s * 8 + 8, :] = (out + own[eight]) / total[eight]
+        own = own_weight.astype(BF16).astype(F32) * fresh_ref[rows, :]
+        out = jnp.concatenate(
+            [dot(weights[s * 8 : s * 8 + 8], value_ref[half * 16 + s]) for s in range(16)], axis=0
+        )
+        out_ref[rows, :] = (out + own) / total
     outs = [out_ref[pl.ds(h, 32, 8), :] for h in range(8)]
     keep, give = split(parity, outs, key, value)
     keep_ref[...] = keep.astype(BF16)
@@ -328,6 +367,7 @@
         out_specs=[VMEM] * 2,
         scratch_shapes=[
             pltpu.VMEM((32, 1280), F32),
+            pltpu.VMEM((256, 128), F32),
             pltpu.VMEM((256, 128), F32),
             pltpu.VMEM((256, 128), F32),
             pltpu.VMEM((256, 128), F32),
@@ -434,24 +474,26 @@
     def y_turn(k):
         return [(4 * a + b, 4 * ((a + k) % 4) + b) for a in range(4) for b in range(4)]
 
-    sent, plan = prepare(requests, slots, hidden)
-    rows = jnp.swapaxes(hidden.reshape(32, 2, 512), 0, 1).reshape(64, 512)
-    around_z = [rows] + [lax.ppermute(rows, "tensor", z_turn(k)) for k in (1, 2, 3)]
+    sent, plan, down_near, up_near, hidden_near = prepare(
+        requests, slots, hidden, down_maps.reshape(96, 8192), up_maps.reshape(32, 10240)
+    )
+    around_z = [hidden] + [lax.ppermute(hidden, "tensor", z_turn(k)) for k in (1, 2, 3)]
     recv = lax.all_to_all(sent, ROUTE, 0, 0, tiled=True)
-    band = jnp.stack(around_z)
-    bands = [band] + [lax.ppermute(band, "tensor", y_turn(k)) for k in (1, 2, 3)]
-
-    low_sent = owner_low(
-        recv, down_maps.reshape(96, 8192), up_maps.reshape(32, 10240)
-    )
-    low_sent, *bands = lax.optimization_barrier((low_sent, *bands))
+    band = stack_band(plan, [hidden_near] + around_z[1:])
+    up, down = (lax.ppermute(band, "tensor", y_turn(k)) for k in (1, 3))
+
+    halves = [
+        lax.ppermute(up[0:2], "tensor", y_turn(1)), lax.ppermute(down[2:4], "tensor", y_turn(3))
+    ]
+    recv, up, down = lax.optimization_barrier((recv, up, down))
+    low_sent = owner_low(recv, down_near, up_near)
+    low_sent, *halves = lax.optimization_barrier((low_sent, *halves))
     low = lax.all_to_all(low_sent, ROUTE, 0, 0, tiled=True)
 
-    turns = jnp.arange(16)
-    order = 4 * ((y - (turns >> 2)) & 3) + ((z - turns) & 3)
-    order = jnp.concatenate([order, parity[None]]).astype(jnp.int32)
-    mine, give, key2, value2 = base_project(
-        order, plan, bands, wq, wk.T, wv.T, key_cache[0], value_cache[0], low_sent
+    place = jnp.stack([y, z]).astype(jnp.int32)
+    part = base_project(place, (band, up, down), wq, wk.T, wv.T, low_sent)
+    mine, give, key2, value2 = base_rest(
+        place, plan, part, halves, wq, wk.T, wv.T, key_cache[0], value_cache[0]
     )
     other = lax.ppermute(give, "tensor", swap)
 
@@ -465,7 +507,7 @@
     row = lax.ppermute(pick(plan, low), "tensor", swap)
     keys, values = in_hbm(key_cache[0], value_cache[0])
     used = lax.dynamic_index_in_dim(filled.reshape(32, 2), parity, 1, keepdims=False)
-    used = jnp.repeat(used, 8).reshape(2, 128)
+    used = jnp.repeat(used, 8).reshape(256, 1)
     keep, give = attend_all(plan, which, used, low, mine, other, cos, sin, keys, values)
     keep, give = amend(
         plan, which, filled, row, mine, other, cos, sin, key2, value2, keep, give

time: 73.1 us -> 67.5 us (0.923)
  waiting for transfers between devices: 18.9 us -> 15.1 us
  starting transfers between devices: 31.1 us -> 29.3 us
    all_to_all x1, starting transfers between devices: 7.88 us -> 4.76 us  [local(): low = lax.all_to_all(low_sent, ROUTE, 0, 0, tiled=True)]
    pallas_call x2 -> x4, Pallas kernels: 8.21 us -> 10.8 us  [the longest x1 4.64 us: base_project(): pl.pallas_call(base_kernel, out_shape=jax.ShapeDtypeStruct((64, 640), F32...]
    ppermute x6 -> x7, waiting for transfers between devices: 3.52 us -> 0.96 us  [the longest x3 0.95 us: local(): lax.ppermute(hidden, 'tensor', z_turn(k))]
    all_to_all x1, waiting for transfers between devices: 6.81 us -> 4.86 us  [local(): low = lax.all_to_all(low_sent, ROUTE, 0, 0, tiled=True)]
    pallas_call x1, Pallas kernels: 6.2 us -> 4.7 us  [attend_all(): pl.pallas_call(attend_kernel, out_shape=[jax.ShapeDtypeStruct((32, 640),...]
    pallas_call x1, Pallas kernels: 3.23 us -> 1.86 us  [owner_low(): pl.pallas_call(owner_kernel, out_shape=jax.ShapeDtypeStruct((128, 1, 1280...]
    ppermute x6 -> x7, starting transfers between devices: 11.8 us -> 13.2 us  [the longest x3 6.66 us: local(): lax.ppermute(hidden, 'tensor', z_turn(k))]
    slice x0 -> x2, local copies, waits for them, and re-layouts: none -> 1.33 us  [the longest x1 0.67 us: local(): down[2:4]]
  transfers between devices with their start and end apart: 11 -> 12, of which waited for: 4 -> 4; matrix products, arithmetic and copies ran while one was open for 2% -> 4% of each run, Pallas kernels for 25% -> 26%
where the time goes in v3:
time: 67.5 us; the launch traced here: 67.3 us
  starting transfers between devices  29.3 us (43%)
  Pallas kernels  19.6 us (29%)
  waiting for transfers between devices  15.1 us (22%)
  local copies, waits for them, and re-layouts  1.88 us (3%)
  between operations  0.81 us (1%)
    all_to_all x1, starting transfers between devices, local(): recv = lax.all_to_all(sent, ROUTE, 0, 0, tiled=True)  8.03 us
    all_to_all x1, waiting for transfers between devices, local(): recv = lax.all_to_all(sent, ROUTE, 0, 0, tiled=True)  6.86 us
    ppermute x3, starting transfers between devices, local(): lax.ppermute(hidden, 'tensor', z_turn(k))  6.66 us
    all_to_all x1, waiting for transfers between devices, local(): low = lax.all_to_all(low_sent, ROUTE, 0, 0, tiled=True)  4.86 us
    all_to_all x1, starting transfers between devices, local(): low = lax.all_to_all(low_sent, ROUTE, 0, 0, tiled=True)  4.76 us
    pallas_call x1, Pallas kernels, attend_all(): pl.pallas_call(attend_kernel, out_shape=[jax.ShapeDtypeStruct((32, 640),...  4.7 us
    pallas_call x1, Pallas kernels, base_project(): pl.pallas_call(base_kernel, out_shape=jax.ShapeDtypeStruct((64, 640), F32...  4.64 us
    ppermute x2, starting transfers between devices, local(): up, down = (lax.ppermute(band, 'tensor', y_turn(k)) for k in (1, 3))  3.31 us
  transfers between devices with their start and end apart: 12, of which 4 were waited for; matrix products, arithmetic and copies ran while one was open for 4% of the time, Pallas kernels for 26%

profile of v3, /device:TPU:0, one launch (start us, length us, event | category | flops | bytes accessed | tf_op | source)
XLA Modules:
  0.0 67.3 jit_solution(1019901752311229308)
XLA Ops:
  0.6 2.1 %collective-permute-start = (bf16[64,512]{1,0:T(8,128)(2,1)}, bf16[64,512]{1,0:T(8,128)(2,1)S(1)}, u32[]{:S(2)}, u32[]{:S(2)}) collective-permute-start(bf16[64,512]{1,0:T(8,128)(2,1)} %hidden_hbm.1), channel_id=1, source_target_pairs={{0,1},{1,2},{2,3},{3,0},{4,5},{5,6},{6,7},{7,4},{8,9},{9,10},{10,1... | collective-permute-start | bytes 196616 | tf_op jit(solution)/shard_map/ppermute | solution.py:480
  2.7 3.6 %collective-permute-start.1 = (bf16[64,512]{1,0:T(8,128)(2,1)}, bf16[64,512]{1,0:T(8,128)(2,1)S(1)}, u32[]{:S(2)}, u32[]{:S(2)}) collective-permute-start(bf16[64,512]{1,0:T(8,128)(2,1)} %hidden_hbm.1), channel_id=1, source_target_pairs={{0,2},{1,3},{2,0},{3,1},{4,6},{5,7},{6,4},{7,5},{8,10},{9,11},{10,... | collective-permute-start | bytes 196616 | tf_op jit(solution)/shard_map/ppermute | solution.py:480
  6.3 1.0 %collective-permute-start.2 = (bf16[64,512]{1,0:T(8,128)(2,1)}, bf16[64,512]{1,0:T(8,128)(2,1)S(1)}, u32[]{:S(2)}, u32[]{:S(2)}) collective-permute-start(bf16[64,512]{1,0:T(8,128)(2,1)} %hidden_hbm.1), channel_id=1, source_target_pairs={{0,3},{1,0},{2,1},{3,2},{4,7},{5,4},{6,5},{7,6},{8,11},{9,8},{10,9... | collective-permute-start | bytes 196616 | tf_op jit(solution)/shard_map/ppermute | solution.py:480
  7.3 2.5 %prepare.1 = (bf16[128,2,640]{2,1,0:T(2,128)(2,1)}, s32[66]{0:T(128)S(1)}, bf16[96,8192]{1,0:T(8,128)(2,1)S(1)}, bf16[32,10240]{1,0:T(8,128)(2,1)S(1)}, bf16[64,512]{1,0:T(8,128)(2,1)S(1)}) custom-call(s32[1,63]{1,0:T(1,128)} %requests_hbm.1, s32[64]{0:T(128)} %slots_hbm.1, bf16[64,512]{1,0:T(8,128)(2,1)} %hidden_hbm.1, bf16[96,8192]{1,0:T(8,128)(2,1)} %bitcast.17, ...), custom_call_target="tpu_custom_call" | custom-call | flops 1000000 | bytes 500000 | tf_op jit(solution)/shard_map/prepare/pallas_call | solution.py:71
  9.8 0.9 %collective-permute-done.2.h3_ref = bf16[64,512]{1,0:T(8,128)(2,1)S(1)} collective-permute-done((bf16[64,512]{1,0:T(8,128)(2,1)}, bf16[64,512]{1,0:T(8,128)(2,1)S(1)}, u32[]{:S(2)}, u32[]{:S(2)}) %collective-permute-start.2) | collective-permute-done | bytes 65568 | tf_op jit(solution)/shard_map/ppermute | solution.py:480
  11.3 1.6 %collective-permute-start.3 = (bf16[4,64,512]{2,1,0:T(8,128)(2,1)S(1)}, bf16[4,64,512]{2,1,0:T(8,128)(2,1)S(1)}, u32[]{:S(2)}, u32[]{:S(2)}) collective-permute-start(bf16[4,64,512]{2,1,0:T(8,128)(2,1)S(1)} %stack_band.1.h0_ref), channel_id=1, source_target_pairs={{0,4},{1,5},{2,6},{3,7},{4,8},{5,9},{6,10},{7,11},{8,12},{9,13},{1... | collective-permute-start | bytes 786440 | tf_op jit(solution)/shard_map/ppermute | solution.py:483
  13.0 1.7 %collective-permute-start.4 = (bf16[4,64,512]{2,1,0:T(8,128)(2,1)S(1)}, bf16[4,64,512]{2,1,0:T(8,128)(2,1)S(1)}, u32[]{:S(2)}, u32[]{:S(2)}) collective-permute-start(bf16[4,64,512]{2,1,0:T(8,128)(2,1)S(1)} %stack_band.1.h0_ref), channel_id=1, source_target_pairs={{0,12},{1,13},{2,14},{3,15},{4,0},{5,1},{6,2},{7,3},{8,4},{9,5},{1... | collective-permute-start | bytes 786440 | tf_op jit(solution)/shard_map/ppermute | solution.py:483
  14.6 8.0 %all-to-all-start = ((bf16[128,2,640]{2,1,0:T(2,128)(2,1)}), bf16[128,2,640]{2,1,0:T(2,128)(2,1)S(1)}, u32[]{:S(2)}, u32[]{:S(2)}) async-start(bf16[128,2,640]{2,1,0:T(2,128)(2,1)} %get-tuple-element.23), calls=%async_computation | async-start | bytes 655360 | tf_op jit(solution)/shard_map/all_to_all | solution.py:481
  22.7 0.7 slice.8
  23.3 1.0 %collective-permute-start.5 = (bf16[2,64,512]{2,1,0:T(8,128)(2,1)}, bf16[2,64,512]{2,1,0:T(8,128)(2,1)S(1)}, u32[]{:S(2)}, u32[]{:S(2)}) collective-permute-start(bf16[2,64,512]{2,1,0:T(8,128)(2,1)} %slice.8), channel_id=1, source_target_pairs={{0,4},{1,5},{2,6},{3,7},{4,8},{5,9},{6,10},{7,11},{8,12},{9,13},{1... | collective-permute-start | bytes 393224 | tf_op jit(solution)/shard_map/ppermute | solution.py:486
  24.3 0.7 slice.9
  25.0 2.3 %collective-permute-start.6 = (bf16[2,64,512]{2,1,0:T(8,128)(2,1)}, bf16[2,64,512]{2,1,0:T(8,128)(2,1)}, u32[]{:S(2)}, u32[]{:S(2)}) collective-permute-start(bf16[2,64,512]{2,1,0:T(8,128)(2,1)} %slice.9), channel_id=1, source_target_pairs={{0,12},{1,13},{2,14},{3,15},{4,0},{5,1},{6,2},{7,3},{8,4},{9,5},{1... | collective-permute-start | bytes 393224 | tf_op jit(solution)/shard_map/ppermute | solution.py:486
  27.3 6.9 %all-to-all-done.recv_ref = bf16[128,2,640]{2,1,0:T(2,128)(2,1)S(1)} async-done(((bf16[128,2,640]{2,1,0:T(2,128)(2,1)}), bf16[128,2,640]{2,1,0:T(2,128)(2,1)S(1)}, u32[]{:S(2)}, u32[]{:S(2)}) %all-to-all-start) | async-done | bytes 327712 | tf_op jit(solution)/shard_map/all_to_all | solution.py:481
  34.1 1.9 %owner_low.1._ = f32[128,1,1280]{2,1,0:T(1,128)} custom-call(bf16[128,2,640]{2,1,0:T(2,128)(2,1)S(1)} %all-to-all-done.recv_ref, bf16[96,8192]{1,0:T(8,128)(2,1)S(1)} %get-tuple-element.26.down_ref, bf16[32,10240]{1,0:T(8,128)(2,1)S(1)} %get-tuple-element.27.up_ref), custom_call_target="tpu_custom_call" | custom-call | flops 40000000 | bytes 3400000 | tf_op jit(solution)/shard_map/owner_low/pallas_call | solution.py:146
  36.0 4.8 %all-to-all-start.1 = ((f32[128,1,1280]{2,1,0:T(1,128)}), f32[128,1,1280]{2,1,0:T(1,128)S(1)}, u32[]{:S(2)}, u32[]{:S(2)}) async-start(f32[128,1,1280]{2,1,0:T(1,128)} %owner_low.1._), calls=%async_computation.1 | async-start | bytes 1310720 | tf_op jit(solution)/shard_map/all_to_all | solution.py:491
  41.8 4.6 %base_project.1.part_ref = f32[64,640]{1,0:T(8,128)S(1)} custom-call(s32[2]{0:T(128)S(1)} %pad_add_fusion.place_ref, bf16[4,64,512]{2,1,0:T(8,128)(2,1)S(1)} %stack_band.1.h0_ref, bf16[4,64,512]{2,1,0:T(8,128)(2,1)S(1)} %collective-permute-done.3.h1_ref, bf16[4,64,512]{2,1,0:T(8,128)(2,1)S(1)} %collective-permute-done.4.h3_ref, bf16[8192,512]{1,0:T(8,128)(2,1)} %wq_hbm.3, ...), custom_call_target="tpu_custom_call" | custom-call | flops 503000000 | bytes 8800000 | tf_op jit(solution)/shard_map/base_project/pallas_call | solution.py:227
  46.4 3.2 %base_rest.1 = (f32[32,640]{1,0:T(8,128)S(1)}, f32[32,640]{1,0:T(8,128)S(1)}, bf16[512,128]{1,0:T(8,128)(2,1)S(1)}, bf16[512,128]{1,0:T(8,128)(2,1)S(1)}) custom-call(s32[2]{0:T(128)S(1)} %pad_add_fusion.place_ref, s32[66]{0:T(128)S(1)} %get-tuple-element.22._.plan_ref, f32[64,640]{1,0:T(8,128)S(1)} %base_project.1.part_ref, ...), custom_call_target="tpu_custom_call" | custom-call | flops 168000000 | bytes 3200000 | tf_op jit(solution)/shard_map/base_rest/pallas_call | solution.py:244
  49.6 1.2 %collective-permute-start.8 = (f32[32,640]{1,0:T(8,128)S(1)}, f32[32,640]{1,0:T(8,128)S(1)}, u32[]{:S(2)}, u32[]{:S(2)}) collective-permute-start(f32[32,640]{1,0:T(8,128)S(1)} %get-tuple-element.34), channel_id=1, source_target_pairs={{0,1},{1,0},{2,3},{3,2},{4,5},{5,4},{6,7},{7,6},{8,9},{9,8},{10,11... | collective-permute-start | bytes 245768 | tf_op jit(solution)/shard_map/ppermute | solution.py:498
  50.8 4.9 %all-to-all-done.1.low_ref = f32[128,1,1280]{2,1,0:T(1,128)S(1)} async-done(((f32[128,1,1280]{2,1,0:T(1,128)}), f32[128,1,1280]{2,1,0:T(1,128)S(1)}, u32[]{:S(2)}, u32[]{:S(2)}) %all-to-all-start.1) | async-done | bytes 655392 | tf_op jit(solution)/shard_map/all_to_all | solution.py:491
  56.8 4.7 %attend_all.1 = (bf16[32,640]{1,0:T(8,128)(2,1)S(1)}, bf16[32,640]{1,0:T(8,128)(2,1)S(1)}) custom-call(s32[66]{0:T(128)S(1)} %get-tuple-element.22._.plan_ref, s32[1]{0:T(128)} %bitcast.parity_ref, s32[256,1]{1,0:T(8,128)S(1)} %reshape_reshape.4.used_ref, f32[128,1,1280]{2,1,0:T(1,128)S(1)} %all-to-all-done.1.low_ref, ...), custom_call_target="tpu_custom_call" | custom-call | flops 70000000 | bytes 1000000 | tf_op jit(solution)/shard_map/attend_all/pallas_call | solution.py:363
  61.5 1.0 %amend.1 = (bf16[32,640]{1,0:T(8,128)(2,1)S(1)}, bf16[32,640]{1,0:T(8,128)(2,1)S(1)}) custom-call(s32[66]{0:T(128)S(1)} %get-tuple-element.22._.plan_ref, s32[1]{0:T(128)} %bitcast.parity_ref, s32[64]{0:T(128)S(1)} %copy-done, f32[1,1280]{1,0:T(1,128)S(1)} %collective-permute-done.7.row_ref, f32[32,640]{1,0:T(8,128)S(1)} %get-tuple-element.33.mine_ref, ...), custom_call_target="tpu_custom_call" | custom-call | flops 2000000 | bytes 500000 | tf_op jit(solution)/shard_map/amend/pallas_call | solution.py:406
  62.5 1.7 %collective-permute-start.9 = (bf16[32,640]{1,0:T(8,128)(2,1)S(1)}, bf16[32,640]{1,0:T(8,128)(2,1)S(1)}, u32[]{:S(2)}, u32[]{:S(2)}) collective-permute-start(bf16[32,640]{1,0:T(8,128)(2,1)S(1)} %get-tuple-element.40), channel_id=1, source_target_pairs={{0,1},{1,0},{2,3},{3,2},{4,5},{5,4},{6,7},{7,6},{8,9},{9,8},{10,11... | collective-permute-start | bytes 122888 | tf_op jit(solution)/shard_map/ppermute | solution.py:515
  64.1 2.4 %collective-permute-done.9.back_ref = bf16[32,640]{1,0:T(8,128)(2,1)S(1)} collective-permute-done((bf16[32,640]{1,0:T(8,128)(2,1)S(1)}, bf16[32,640]{1,0:T(8,128)(2,1)S(1)}, u32[]{:S(2)}, u32[]{:S(2)}) %collective-permute-start.9) | collective-permute-done | bytes 40992 | tf_op jit(solution)/shard_map/ppermute | solution.py:515
  66.5 0.7 %weave.1 = (bf16[64,512]{1,0:T(8,128)(2,1)}, bf16[64,64]{1,0:T(8,128)(2,1)}, bf16[64,64]{1,0:T(8,128)(2,1)}) custom-call(s32[1]{0:T(128)} %bitcast.parity_ref, bf16[32,640]{1,0:T(8,128)(2,1)S(1)} %get-tuple-element.39.keep_ref, bf16[32,640]{1,0:T(8,128)(2,1)S(1)} %collective-permute-done.9.back_ref), custom_call_target="tpu_custom_call" | custom-call | tf_op jit(solution)/shard_map/weave/pallas_call | solution.py:448
  (25 shorter events, 2.7 us)
Async XLA Ops:
  0.6 9.2 %collective-permute-start = (bf16[64,512]{1,0:T(8,128)(2,1)}, bf16[64,512]{1,0:T(8,128)(2,1)S(1)}, u32[]{:S(2)}, u32[]{:S(2)}) collective-permute-start(bf16[64,512]{1,0:T(8,128)(2,1)} %hidden_hbm.1), channel_id=1, source_target_pairs={{0,1},{1,2},{2,3},{3,0},{4,5},{5,6},{6,7},{7,4},{8,9},{9,10},{10,1... | collective-permute-start | bytes 196616 | tf_op jit(solution)/shard_map/ppermute | solution.py:480
  2.7 7.1 %collective-permute-start.1 = (bf16[64,512]{1,0:T(8,128)(2,1)}, bf16[64,512]{1,0:T(8,128)(2,1)S(1)}, u32[]{:S(2)}, u32[]{:S(2)}) collective-permute-start(bf16[64,512]{1,0:T(8,128)(2,1)} %hidden_hbm.1), channel_id=1, source_target_pairs={{0,2},{1,3},{2,0},{3,1},{4,6},{5,7},{6,4},{7,5},{8,10},{9,11},{10,... | collective-permute-start | bytes 196616 | tf_op jit(solution)/shard_map/ppermute | solution.py:480
  6.3 4.5 %collective-permute-start.2 = (bf16[64,512]{1,0:T(8,128)(2,1)}, bf16[64,512]{1,0:T(8,128)(2,1)S(1)}, u32[]{:S(2)}, u32[]{:S(2)}) collective-permute-start(bf16[64,512]{1,0:T(8,128)(2,1)} %hidden_hbm.1), channel_id=1, source_target_pairs={{0,3},{1,0},{2,1},{3,2},{4,7},{5,4},{6,5},{7,6},{8,11},{9,8},{10,9... | collective-permute-start | bytes 196616 | tf_op jit(solution)/shard_map/ppermute | solution.py:480
  7.3 33.5 %copy-start.1 = (s32[64]{0:T(128)S(1)}, s32[64]{0:T(128)}, u32[]{:S(2)}) copy-start(s32[64]{0:T(128)} %param.21) | copy-start | bytes 772
  7.3 33.6 %copy-start = (s32[64]{0:T(128)S(1)}, s32[64]{0:T(128)}, u32[]{:S(2)}) copy-start(s32[64]{0:T(128)} %used_ref.1) | copy-start | bytes 772
  11.3 11.3 %collective-permute-start.3 = (bf16[4,64,512]{2,1,0:T(8,128)(2,1)S(1)}, bf16[4,64,512]{2,1,0:T(8,128)(2,1)S(1)}, u32[]{:S(2)}, u32[]{:S(2)}) collective-permute-start(bf16[4,64,512]{2,1,0:T(8,128)(2,1)S(1)} %stack_band.1.h0_ref), channel_id=1, source_target_pairs={{0,4},{1,5},{2,6},{3,7},{4,8},{5,9},{6,10},{7,11},{8,12},{9,13},{1... | collective-permute-start | bytes 786440 | tf_op jit(solution)/shard_map/ppermute | solution.py:483
  13.0 11.3 %collective-permute-start.4 = (bf16[4,64,512]{2,1,0:T(8,128)(2,1)S(1)}, bf16[4,64,512]{2,1,0:T(8,128)(2,1)S(1)}, u32[]{:S(2)}, u32[]{:S(2)}) collective-permute-start(bf16[4,64,512]{2,1,0:T(8,128)(2,1)S(1)} %stack_band.1.h0_ref), channel_id=1, source_target_pairs={{0,12},{1,13},{2,14},{3,15},{4,0},{5,1},{6,2},{7,3},{8,4},{9,5},{1... | collective-permute-start | bytes 786440 | tf_op jit(solution)/shard_map/ppermute | solution.py:483
  14.6 19.5 %all-to-all-start = ((bf16[128,2,640]{2,1,0:T(2,128)(2,1)}), bf16[128,2,640]{2,1,0:T(2,128)(2,1)S(1)}, u32[]{:S(2)}, u32[]{:S(2)}) async-start(bf16[128,2,640]{2,1,0:T(2,128)(2,1)} %get-tuple-element.23), calls=%async_computation | async-start | bytes 655360 | tf_op jit(solution)/shard_map/all_to_all | solution.py:481
  23.3 12.6 %collective-permute-start.5 = (bf16[2,64,512]{2,1,0:T(8,128)(2,1)}, bf16[2,64,512]{2,1,0:T(8,128)(2,1)S(1)}, u32[]{:S(2)}, u32[]{:S(2)}) collective-permute-start(bf16[2,64,512]{2,1,0:T(8,128)(2,1)} %slice.8), channel_id=1, source_target_pairs={{0,4},{1,5},{2,6},{3,7},{4,8},{5,9},{6,10},{7,11},{8,12},{9,13},{1... | collective-permute-start | bytes 393224 | tf_op jit(solution)/shard_map/ppermute | solution.py:486
  25.0 11.0 %collective-permute-start.6 = (bf16[2,64,512]{2,1,0:T(8,128)(2,1)}, bf16[2,64,512]{2,1,0:T(8,128)(2,1)}, u32[]{:S(2)}, u32[]{:S(2)}) collective-permute-start(bf16[2,64,512]{2,1,0:T(8,128)(2,1)} %slice.9), channel_id=1, source_target_pairs={{0,12},{1,13},{2,14},{3,15},{4,0},{5,1},{6,2},{7,3},{8,4},{9,5},{1... | collective-permute-start | bytes 393224 | tf_op jit(solution)/shard_map/ppermute | solution.py:486
  36.0 19.7 %all-to-all-start.1 = ((f32[128,1,1280]{2,1,0:T(1,128)}), f32[128,1,1280]{2,1,0:T(1,128)S(1)}, u32[]{:S(2)}, u32[]{:S(2)}) async-start(f32[128,1,1280]{2,1,0:T(1,128)} %owner_low.1._), calls=%async_computation.1 | async-start | bytes 1310720 | tf_op jit(solution)/shard_map/all_to_all | solution.py:491
  49.6 7.2 %collective-permute-start.8 = (f32[32,640]{1,0:T(8,128)S(1)}, f32[32,640]{1,0:T(8,128)S(1)}, u32[]{:S(2)}, u32[]{:S(2)}) collective-permute-start(f32[32,640]{1,0:T(8,128)S(1)} %get-tuple-element.34), channel_id=1, source_target_pairs={{0,1},{1,0},{2,3},{3,2},{4,5},{5,4},{6,7},{7,6},{8,9},{9,8},{10,11... | collective-permute-start | bytes 245768 | tf_op jit(solution)/shard_map/ppermute | solution.py:498
  56.2 5.2 %collective-permute-start.7 = (f32[1,1280]{1,0:T(1,128)S(1)}, f32[1,1280]{1,0:T(1,128)S(1)}, u32[]{:S(2)}, u32[]{:S(2)}) collective-permute-start(f32[1,1280]{1,0:T(1,128)S(1)} %pick.1), channel_id=1, source_target_pairs={{0,1},{1,0},{2,3},{3,2},{4,5},{5,4},{6,7},{7,6},{8,9},{9,8},{10,11... | collective-permute-start | bytes 15368 | tf_op jit(solution)/shard_map/ppermute | solution.py:507
  62.5 4.1 %collective-permute-start.9 = (bf16[32,640]{1,0:T(8,128)(2,1)S(1)}, bf16[32,640]{1,0:T(8,128)(2,1)S(1)}, u32[]{:S(2)}, u32[]{:S(2)}) collective-permute-start(bf16[32,640]{1,0:T(8,128)(2,1)S(1)} %get-tuple-element.40), channel_id=1, source_target_pairs={{0,1},{1,0},{2,3},{3,2},{4,5},{5,4},{6,7},{7,6},{8,9},{9,8},{10,11... | collective-permute-start | bytes 122888 | tf_op jit(solution)/shard_map/ppermute | solution.py:515

commit v4 on v3

--- a/solution.py
+++ b/solution.py
@@ -22,25 +22,30 @@
 dot_nt = functools.partial(lax.dot_general, dimension_numbers=NT, preferred_element_type=F32)
 
 
-def prepare_kernel(
-    requests_hbm, slots_hbm, hidden_hbm, down_hbm, up_hbm, sent_ref, plan_ref, down_ref, up_ref, hidden_ref,
-    rows_ref, wide_ref, requests_ref, slots_ref, sems,
+def plan_kernel(
+    z_ref, requests_hbm, slots_hbm, hidden_hbm, down_hbm, up_hbm,
+    plan_ref, spread_ref, code_ref, down_ref, up_ref, hidden_ref,
+    eye_ref, wide_ref, requests_ref, slots_ref, sems,
 ):
     copies = [
         pltpu.make_async_copy(requests_hbm, requests_ref, sems.at[0]),
         pltpu.make_async_copy(slots_hbm, slots_ref, sems.at[1]),
+    ]
+    near = [
         pltpu.make_async_copy(hidden_hbm, hidden_ref, sems.at[2]),
-    ]
-    maps = [
         pltpu.make_async_copy(down_hbm, down_ref, sems.at[3]),
         pltpu.make_async_copy(up_hbm, up_ref, sems.at[4]),
     ]
-    for copy in copies + maps:
+    for copy in copies + near:
         copy.start()
-    rows_ref[...] = jnp.zeros_like(rows_ref)
+    spread_ref[...] = jnp.zeros_like(spread_ref)
+    code_ref[...] = jnp.zeros_like(code_ref)
+    shape = eye_ref.shape
+    rows, cols = (lax.broadcasted_iota(jnp.int32, shape, d) for d in range(2))
+    eye_ref[...] = jnp.where(rows == cols, 1.0, 0.0)
     for copy in copies:
         copy.wait()
-    wide_ref[:, 0:512] = hidden_ref[...].astype(F32)
+    z = z_ref[0]
     first = jnp.int32(-1)
     last = jnp.int32(-1)
     for s in range(64):
@@ -54,12 +59,17 @@
         last = jnp.where(zero, s, last)
         first = jnp.where(zero & (first < 0), s, first)
         code = ((adapter & 3) + 4 * (s % 2)).astype(F32)
-        wide_ref[s : s + 1, 512:640] = jnp.full((1, 128), code, F32)
-        rows_ref[place, pl.ds(rank, 1), :] = wide_ref[s : s + 1, :]
+        wide_ref[s : s + 1, :] = jnp.full((1, 128), code, F32)
+        row = pl.ds(((place >> 5) * 8 + (place & 7)) * 2 + rank, 1)
+
+        @pl.when(((place >> 3) & 3) == z)
+        def _():
+            spread_ref[row, :] = eye_ref[s : s + 1, :]
+            code_ref[row, :] = wide_ref[s : s + 1, :]
+
     plan_ref[64] = first
     plan_ref[65] = last
-    sent_ref[...] = rows_ref[...].astype(BF16)
-    for copy in maps:
+    for copy in near:
         copy.wait()
 
 
@@ -67,29 +77,50 @@
     return [pltpu.with_memory_space_constraint(x, pltpu.HBM) for x in arrays]
 
 
-def prepare(requests, slots, hidden, down, up):
-    return pl.pallas_call(
-        prepare_kernel,
+def make_plan(z, requests, slots, hidden, down, up):
+    return pl.pallas_call(
+        plan_kernel,
         out_shape=[
-            pltpu.HBM((128, 2, 640), BF16),
             jax.ShapeDtypeStruct((66,), jnp.int32),
+            jax.ShapeDtypeStruct((64, 128), F32),
+            jax.ShapeDtypeStruct((64, 128), F32),
             pltpu.VMEM(down.shape, BF16),
             pltpu.VMEM(up.shape, BF16),
             pltpu.VMEM(hidden.shape, BF16),
         ],
-        in_specs=[ANY] * 5,
-        out_specs=[VMEM, SMEM, ANY, ANY, VMEM],
+        in_specs=[SMEM] + [ANY] * 5,
+        out_specs=[SMEM, VMEM, VMEM, ANY, ANY, VMEM],
         scratch_shapes=[
-            pltpu.VMEM((128, 2, 640), F32),
-            pltpu.VMEM((64, 640), F32),
+            pltpu.VMEM((64, 128), F32),
+            pltpu.VMEM((64, 128), F32),
             pltpu.SMEM((1, 63), jnp.int32),
             pltpu.SMEM((64,), jnp.int32),
             pltpu.SemaphoreType.DMA((5,)),
         ],
         cost_estimate=pl.CostEstimate(flops=1_000_000, bytes_accessed=500_000, transcendentals=0),
         compiler_params=pltpu.CompilerParams(vmem_limit_bytes=4 * 2**20),
-        name="prepare",
-    )(*in_hbm(requests, slots, hidden, down, up))
+        name="make_plan",
+    )(z, *in_hbm(requests, slots, hidden, down, up))
+
+
+def send_kernel(spread_ref, code_ref, h0_ref, h1_ref, h2_ref, h3_ref, sent_ref):
+    spread = spread_ref[:, 0:64].astype(BF16)
+    for k, ref in enumerate((h0_ref, h1_ref, h2_ref, h3_ref)):
+        rows = dot(spread, ref[...])
+        sent_ref[:, :, k * 512 : (k + 1) * 512] = rows.reshape(32, 2, 512).astype(BF16)
+    sent_ref[:, :, 2048:2176] = code_ref[...].reshape(32, 2, 128).astype(BF16)
+
+
+def send_rows(spread, code, blocks):
+    return pl.pallas_call(
+        send_kernel,
+        out_shape=pltpu.HBM((32, 2, 2176), BF16),
+        in_specs=[VMEM] * 6,
+        out_specs=VMEM,
+        cost_estimate=pl.CostEstimate(flops=1_000_000, bytes_accessed=500_000, transcendentals=0),
+        compiler_params=pltpu.CompilerParams(vmem_limit_bytes=4 * 2**20),
+        name="send_rows",
+    )(spread, code, *blocks)
 
 
 def band_kernel(_, h0_ref, h1_ref, h2_ref, h3_ref, out_ref):
@@ -109,15 +140,33 @@
     )(plan, *blocks)
 
 
-def owner_kernel(recv_ref, down_ref, up_ref, out_ref, coords_ref, code_ref):
+def halves_kernel(up_ref, down_ref, a_ref, b_ref):
+    a_ref[...] = up_ref[0:2]
+    b_ref[...] = down_ref[2:4]
+
+
+def take_halves(up, down):
+    return pl.pallas_call(
+        halves_kernel,
+        out_shape=[jax.ShapeDtypeStruct((2, 64, 512), BF16)] * 2,
+        in_specs=[VMEM] * 2,
+        out_specs=[VMEM] * 2,
+        cost_estimate=pl.CostEstimate(flops=1000, bytes_accessed=500_000, transcendentals=0),
+        compiler_params=pltpu.CompilerParams(vmem_limit_bytes=4 * 2**20),
+        name="take_halves",
+    )(up, down)
+
+
+def owner_kernel(z_ref, recv_ref, down_ref, up_ref, out_ref, coords_ref, code_ref):
+    z = z_ref[0]
     acc = jnp.zeros((16, 96), F32)
-    for t in range(16):
-        acc = acc + dot_nt(
-            recv_ref[t * 8 : (t + 1) * 8, :, 0:512].reshape(16, 512),
-            down_ref[:, t * 512 : (t + 1) * 512],
-        )
+    for y in range(4):
+        for k in range(4):
+            rows = recv_ref[y * 8 : (y + 1) * 8, :, k * 512 : (k + 1) * 512].reshape(16, 512)
+            cols = pl.ds(pl.multiple_of((4 * y + ((z - k) & 3)) * 512, 512), 512)
+            acc = acc + dot_nt(rows, down_ref[:, cols])
     coords_ref[:, 0:96] = acc.astype(BF16).astype(F32)
-    code_ref[...] = recv_ref[0:8, :, 512:640].reshape(16, 128).astype(F32)
+    code_ref[...] = recv_ref[0:8, :, 2048:2176].reshape(16, 128).astype(F32)
     one, two = coords_ref[pl.ds(0, 8, 2), :], coords_ref[pl.ds(1, 8, 2), :]
     code = code_ref[pl.ds(0, 8, 2), :][:, 0:1].astype(jnp.int32)
     odd = code >= 4
@@ -142,11 +191,11 @@
             out_ref[rows, 0, 1152:1280] = low_value[half, head]
 
 
-def owner_low(recv, down, up):
+def owner_low(z, recv, down, up):
     return pl.pallas_call(
         owner_kernel,
         out_shape=jax.ShapeDtypeStruct((128, 1, 1280), F32),
-        in_specs=[VMEM] * 3,
+        in_specs=[SMEM] + [VMEM] * 3,
         out_specs=VMEM,
         scratch_shapes=[
             pltpu.VMEM((16, 128), F32),
@@ -155,7 +204,7 @@
         cost_estimate=pl.CostEstimate(flops=40_000_000, bytes_accessed=3_400_000, transcendentals=0),
         compiler_params=pltpu.CompilerParams(vmem_limit_bytes=8 * 2**20),
         name="owner_low",
-    )(recv, down, up)
+    )(z, recv, down, up)
 
 
 def weight_copies(rows, wq_hbm, wk_hbm, wv_hbm, wq_ref, wkv_ref, sems):
@@ -185,25 +234,11 @@
 
 
 def base_kernel(
-    place_ref, h0_ref, h1_ref, h3_ref, wq_hbm, wk_hbm, wv_hbm, _, out_ref, wq_ref, wkv_ref, sems
-):
-    y, z = place_ref[0], place_ref[1]
-    rows = [(((y - a) & 3) * 4 + ((z - b) & 3)) * 512 for a in (0, 1, 3) for b in range(4)]
-    copies = weight_copies(rows, wq_hbm, wk_hbm, wv_hbm, wq_ref, wkv_ref, sems)
-    hiddens = [ref[b] for ref in (h0_ref, h1_ref, h3_ref) for b in range(4)]
-    q, kv = add_blocks(
-        hiddens, copies, wq_ref, wkv_ref, jnp.zeros((64, 512), F32), jnp.zeros((64, 128), F32)
-    )
-    out_ref[:, 0:512] = q
-    out_ref[:, 512:640] = kv
-
-
-def rest_kernel(
-    place_ref, plan_ref, part_ref, ha_ref, hb_ref, wq_hbm, wk_hbm, wv_hbm, key_hbm, value_hbm,
+    place_ref, plan_ref, h0_ref, h1_ref, ha_ref, hb_ref, h3_ref, wq_hbm, wk_hbm, wv_hbm, key_hbm, value_hbm, _,
     mine_ref, give_ref, key2_ref, value2_ref, wq_ref, wkv_ref, acc_ref, sems, cache_sems,
 ):
     y, z = place_ref[0], place_ref[1]
-    rows = [(((y - 2) & 3) * 4 + ((z - b) & 3)) * 512 for b in range(4)]
+    rows = [(((y - a) & 3) * 4 + ((z - b) & 3)) * 512 for a in range(4) for b in range(4)]
     copies = weight_copies(rows, wq_hbm, wk_hbm, wv_hbm, wq_ref, wkv_ref, sems)
     cache = [
         pltpu.make_async_copy(key_hbm.at[plan_ref[65] >> 1], key2_ref, cache_sems.at[0]),
@@ -211,8 +246,14 @@
     ]
     for copy in cache:
         copy.start()
-    hiddens = [ha_ref[0], ha_ref[1], hb_ref[0], hb_ref[1]]
-    q, kv = add_blocks(hiddens, copies, wq_ref, wkv_ref, part_ref[:, 0:512], part_ref[:, 512:640])
+    hiddens = [ref[b] for ref in (h0_ref, h1_ref) for b in range(4)]
+    hiddens += [ha_ref[0], ha_ref[1], hb_ref[0], hb_ref[1]] + [h3_ref[b] for b in range(4)]
+    q, kv = jnp.zeros((64, 512), F32), jnp.zeros((64, 128), F32)
+    for i, hidden in enumerate(hiddens):
+        for copy in copies[i]:
+            copy.wait()
+        q = q + dot(hidden, wq_ref[i])
+        kv = kv + dot_nt(hidden, wkv_ref[i])
     parity = z & 1
     for c in range(5):
         cols = slice(c * 128, (c + 1) * 128)
@@ -223,45 +264,28 @@
         copy.wait()
 
 
-def base_project(place, bands, wq, wkt, wvt, after):
+def base_project(place, plan, bands, wq, wkt, wvt, keys, values, after):
     return pl.pallas_call(
         base_kernel,
-        out_shape=jax.ShapeDtypeStruct((64, 640), F32),
-        in_specs=[SMEM] + [VMEM] * 3 + [ANY] * 4,
-        out_specs=VMEM,
-        scratch_shapes=[
-            pltpu.VMEM((12, 512, 512), BF16),
-            pltpu.VMEM((12, 128, 512), BF16),
-            pltpu.SemaphoreType.DMA((3, 12)),
-        ],
-        cost_estimate=pl.CostEstimate(flops=503_000_000, bytes_accessed=8_800_000, transcendentals=0),
-        compiler_params=pltpu.CompilerParams(vmem_limit_bytes=16 * 2**20),
-        name="base_project",
-    )(place, *bands, *in_hbm(wq, wkt, wvt), after)
-
-
-def base_rest(place, plan, part, halves, wq, wkt, wvt, keys, values):
-    return pl.pallas_call(
-        rest_kernel,
         out_shape=[
             jax.ShapeDtypeStruct((32, 640), F32),
             jax.ShapeDtypeStruct((32, 640), F32),
             jax.ShapeDtypeStruct(keys.shape[1:], BF16),
             jax.ShapeDtypeStruct(values.shape[1:], BF16),
         ],
-        in_specs=[SMEM] * 2 + [VMEM] * 3 + [ANY] * 5,
+        in_specs=[SMEM] * 2 + [VMEM] * 5 + [ANY] * 6,
         out_specs=[VMEM] * 4,
         scratch_shapes=[
-            pltpu.VMEM((4, 512, 512), BF16),
-            pltpu.VMEM((4, 128, 512), BF16),
+            pltpu.VMEM((16, 512, 512), BF16),
+            pltpu.VMEM((16, 128, 512), BF16),
             pltpu.VMEM((64, 128), F32),
-            pltpu.SemaphoreType.DMA((3, 4)),
+            pltpu.SemaphoreType.DMA((3, 16)),
             pltpu.SemaphoreType.DMA((2,)),
         ],
-        cost_estimate=pl.CostEstimate(flops=168_000_000, bytes_accessed=3_200_000, transcendentals=0),
-        compiler_params=pltpu.CompilerParams(vmem_limit_bytes=8 * 2**20),
-        name="base_rest",
-    )(place, plan, part, *halves, *in_hbm(wq, wkt, wvt, keys, values))
+        cost_estimate=pl.CostEstimate(flops=671_000_000, bytes_accessed=11_700_000, transcendentals=0),
+        compiler_params=pltpu.CompilerParams(vmem_limit_bytes=16 * 2**20),
+        name="base_project",
+    )(place, plan, *bands, *in_hbm(wq, wkt, wvt, keys, values), after)
 
 
 def rotate(part, cos, sin):
@@ -474,29 +498,30 @@
     def y_turn(k):
         return [(4 * a + b, 4 * ((a + k) % 4) + b) for a in range(4) for b in range(4)]
 
-    sent, plan, down_near, up_near, hidden_near = prepare(
-        requests, slots, hidden, down_maps.reshape(96, 8192), up_maps.reshape(32, 10240)
+    plan, spread, code, down_near, up_near, hidden_near = make_plan(
+        z.reshape(1), requests, slots, hidden, down_maps.reshape(96, 8192), up_maps.reshape(32, 10240)
     )
-    around_z = [hidden] + [lax.ppermute(hidden, "tensor", z_turn(k)) for k in (1, 2, 3)]
-    recv = lax.all_to_all(sent, ROUTE, 0, 0, tiled=True)
-    band = stack_band(plan, [hidden_near] + around_z[1:])
+    around_z = [hidden_near] + [lax.ppermute(hidden, "tensor", z_turn(k)) for k in (1, 2, 3)]
+    sent = send_rows(spread, code, around_z)
+    rings = [[g * 16 + a * 4 + b for a in range(4) for g in range(8)] for b in range(4)]
+    recv = lax.all_to_all(sent, ("dp", "tensor"), 0, 0, tiled=True, axis_index_groups=rings)
+    band = stack_band(plan, around_z)
     up, down = (lax.ppermute(band, "tensor", y_turn(k)) for k in (1, 3))
 
-    halves = [
-        lax.ppermute(up[0:2], "tensor", y_turn(1)), lax.ppermute(down[2:4], "tensor", y_turn(3))
-    ]
+    halves = take_halves(up, down)
+    halves = [lax.ppermute(half, "tensor", y_turn(k)) for half, k in zip(halves, (1, 3))]
     recv, up, down = lax.optimization_barrier((recv, up, down))
-    low_sent = owner_low(recv, down_near, up_near)
+    low_sent = owner_low(z.reshape(1), recv, down_near, up_near)
     low_sent, *halves = lax.optimization_barrier((low_sent, *halves))
     low = lax.all_to_all(low_sent, ROUTE, 0, 0, tiled=True)
 
     place = jnp.stack([y, z]).astype(jnp.int32)
-    part = base_project(place, (band, up, down), wq, wk.T, wv.T, low_sent)
-    mine, give, key2, value2 = base_rest(
-        place, plan, part, halves, wq, wk.T, wv.T, key_cache[0], value_cache[0]
+    mine, give, key2, value2 = base_project(
+        place, plan, (band, up, *halves, down), wq, wk.T, wv.T, key_cache[0], value_cache[0], low_sent
     )
     other = lax.ppermute(give, "tensor", swap)
 
+    positions, filled, mine = lax.optimization_barrier((positions, filled, mine))
     pos = lax.dynamic_index_in_dim(positions.reshape(32, 2), parity, 1, keepdims=False)
     freq = THETA ** (-2.0 * jnp.arange(64, dtype=F32) / HEAD)
     angle = pos.astype(F32)[:, None] * freq[None, :]

time: 67.5 us -> 66 us (0.978)
    all_to_all x1, starting transfers between devices: 8.03 us -> 6.11 us  [local(): lax.all_to_all(sent, ('dp', 'tensor'), 0, 0, tiled=True, axis_index_group...]
    all_to_all x1, waiting for transfers between devices: 6.86 us -> 5.12 us  [local(): lax.all_to_all(sent, ('dp', 'tensor'), 0, 0, tiled=True, axis_index_group...]
    all_to_all x1, starting transfers between devices: 4.76 us -> 6.44 us  [local(): low = lax.all_to_all(low_sent, ROUTE, 0, 0, tiled=True)]
    all_to_all x1, waiting for transfers between devices: 4.86 us -> 6.48 us  [local(): low = lax.all_to_all(low_sent, ROUTE, 0, 0, tiled=True)]
    slice x2 -> x0, local copies, waits for them, and re-layouts: 1.33 us -> none  [the longest x1 0.67 us: local(): down[2:4]]
    pallas_call x3 -> x4, Pallas kernels: 10.3 us -> 9.64 us  [the longest x1 5.52 us: base_project(): pl.pallas_call(base_kernel, out_shape=[jax.ShapeDtypeStruct((32, 640), F3...]
  transfers between devices with their start and end apart: 12 -> 12, of which waited for: 4 -> 5; matrix products, arithmetic and copies ran while one was open for 4% -> 2% of each run, Pallas kernels for 26% -> 25%
where the time goes in v4:
time: 66 us; the launch traced here: 65.8 us
  starting transfers between devices  29.1 us (44%)
  Pallas kernels  19 us (29%)
  waiting for transfers between devices  15.1 us (23%)
  local copies, waits for them, and re-layouts  1.22 us (2%)
  between operations  0.82 us (1%)
    ppermute x3, starting transfers between devices, local(): lax.ppermute(hidden, 'tensor', z_turn(k))  6.66 us
    all_to_all x1, waiting for transfers between devices, local(): low = lax.all_to_all(low_sent, ROUTE, 0, 0, tiled=True)  6.48 us
    all_to_all x1, starting transfers between devices, local(): low = lax.all_to_all(low_sent, ROUTE, 0, 0, tiled=True)  6.44 us
    all_to_all x1, starting transfers between devices, local(): lax.all_to_all(sent, ('dp', 'tensor'), 0, 0, tiled=True, axis_index_group...  6.11 us
    pallas_call x1, Pallas kernels, base_project(): pl.pallas_call(base_kernel, out_shape=[jax.ShapeDtypeStruct((32, 640), F3...  5.52 us
    all_to_all x1, waiting for transfers between devices, local(): lax.all_to_all(sent, ('dp', 'tensor'), 0, 0, tiled=True, axis_index_group...  5.12 us
    pallas_call x1, Pallas kernels, attend_all(): pl.pallas_call(attend_kernel, out_shape=[jax.ShapeDtypeStruct((32, 640),...  4.7 us
    ppermute x2, starting transfers between devices, local(): up, down = (lax.ppermute(band, 'tensor', y_turn(k)) for k in (1, 3))  3.31 us
  transfers between devices with their start and end apart: 12, of which 5 were waited for; matrix products, arithmetic and copies ran while one was open for 2% of the time, Pallas kernels for 25%

profile of v4, /device:TPU:0, one launch (start us, length us, event | category | flops | bytes accessed | tf_op | source)
XLA Modules:
  0.0 65.8 jit_solution(2269912193613653788)
XLA Ops:
  0.6 2.1 %collective-permute-start = (bf16[64,512]{1,0:T(8,128)(2,1)}, bf16[64,512]{1,0:T(8,128)(2,1)S(1)}, u32[]{:S(2)}, u32[]{:S(2)}) collective-permute-start(bf16[64,512]{1,0:T(8,128)(2,1)} %hidden_hbm.1), channel_id=1, source_target_pairs={{0,1},{1,2},{2,3},{3,0},{4,5},{5,6},{6,7},{7,4},{8,9},{9,10},{10,1... | collective-permute-start | bytes 196616 | tf_op jit(solution)/shard_map/ppermute | solution.py:504
  2.7 3.6 %collective-permute-start.1 = (bf16[64,512]{1,0:T(8,128)(2,1)}, bf16[64,512]{1,0:T(8,128)(2,1)S(1)}, u32[]{:S(2)}, u32[]{:S(2)}) collective-permute-start(bf16[64,512]{1,0:T(8,128)(2,1)} %hidden_hbm.1), channel_id=1, source_target_pairs={{0,2},{1,3},{2,0},{3,1},{4,6},{5,7},{6,4},{7,5},{8,10},{9,11},{10,... | collective-permute-start | bytes 196616 | tf_op jit(solution)/shard_map/ppermute | solution.py:504
  6.3 1.0 %collective-permute-start.2 = (bf16[64,512]{1,0:T(8,128)(2,1)}, bf16[64,512]{1,0:T(8,128)(2,1)S(1)}, u32[]{:S(2)}, u32[]{:S(2)}) collective-permute-start(bf16[64,512]{1,0:T(8,128)(2,1)} %hidden_hbm.1), channel_id=1, source_target_pairs={{0,3},{1,0},{2,1},{3,2},{4,7},{5,4},{6,5},{7,6},{8,11},{9,8},{10,9... | collective-permute-start | bytes 196616 | tf_op jit(solution)/shard_map/ppermute | solution.py:504
  7.3 2.3 %make_plan.1 = (s32[66]{0:T(128)S(1)}, f32[64,128]{1,0:T(8,128)S(1)}, f32[64,128]{1,0:T(8,128)S(1)}, bf16[96,8192]{1,0:T(8,128)(2,1)S(1)}, bf16[32,10240]{1,0:T(8,128)(2,1)S(1)}, /*index=5*/bf16[64,512]{1,0:T(8,128)(2,1)S(1)}) custom-call(s32[1]{0:T(128)} %bitcast.1.z_ref, s32[1,63]{1,0:T(1,128)} %requests_hbm.1, s32[64]{0:T(128)} %slots_hbm.1, ...), custom_call_target="tpu_custom_call" | custom-call | flops 1000000 | bytes 500000 | tf_op jit(solution)/shard_map/make_plan/pallas_call | solution.py:81
  9.7 1.1 %collective-permute-done.2.h3_ref = bf16[64,512]{1,0:T(8,128)(2,1)S(1)} collective-permute-done((bf16[64,512]{1,0:T(8,128)(2,1)}, bf16[64,512]{1,0:T(8,128)(2,1)S(1)}, u32[]{:S(2)}, u32[]{:S(2)}) %collective-permute-start.2) | collective-permute-done | bytes 65568 | tf_op jit(solution)/shard_map/ppermute | solution.py:504
  11.3 1.6 %collective-permute-start.3 = (bf16[4,64,512]{2,1,0:T(8,128)(2,1)S(1)}, bf16[4,64,512]{2,1,0:T(8,128)(2,1)S(1)}, u32[]{:S(2)}, u32[]{:S(2)}) collective-permute-start(bf16[4,64,512]{2,1,0:T(8,128)(2,1)S(1)} %stack_band.1.h0_ref), channel_id=1, source_target_pairs={{0,4},{1,5},{2,6},{3,7},{4,8},{5,9},{6,10},{7,11},{8,12},{9,13},{1... | collective-permute-start | bytes 786440 | tf_op jit(solution)/shard_map/ppermute | solution.py:509
  13.0 1.7 %collective-permute-start.4 = (bf16[4,64,512]{2,1,0:T(8,128)(2,1)S(1)}, bf16[4,64,512]{2,1,0:T(8,128)(2,1)S(1)}, u32[]{:S(2)}, u32[]{:S(2)}) collective-permute-start(bf16[4,64,512]{2,1,0:T(8,128)(2,1)S(1)} %stack_band.1.h0_ref), channel_id=1, source_target_pairs={{0,12},{1,13},{2,14},{3,15},{4,0},{5,1},{6,2},{7,3},{8,4},{9,5},{1... | collective-permute-start | bytes 786440 | tf_op jit(solution)/shard_map/ppermute | solution.py:509
  14.6 1.1 %send_rows.1 = bf16[32,2,2176]{2,1,0:T(2,128)(2,1)} custom-call(f32[64,128]{1,0:T(8,128)S(1)} %get-tuple-element.30.spread_ref, f32[64,128]{1,0:T(8,128)S(1)} %get-tuple-element.31.code_ref, bf16[64,512]{1,0:T(8,128)(2,1)S(1)} %get-tuple-element.29.h0_ref, bf16[64,512]{1,0:T(8,128)(2,1)S(1)} %collective-permute-done.h1_ref, ...), custom_call_target="tpu_custom_call" | custom-call | flops 1000000 | bytes 500000 | tf_op jit(solution)/shard_map/send_rows/pallas_call | solution.py:115
  15.7 6.1 %all-to-all-start = ((bf16[32,2,2176]{2,1,0:T(2,128)(2,1)}), bf16[32,2,2176]{2,1,0:T(2,128)(2,1)S(1)}, u32[]{:S(2)}, u32[]{:S(2)}) async-start(bf16[32,2,2176]{2,1,0:T(2,128)(2,1)} %send_rows.1), calls=%async_computation | async-start | bytes 557056 | tf_op jit(solution)/shard_map/all_to_all | solution.py:507
  21.9 0.7 %take_halves.1 = (bf16[2,64,512]{2,1,0:T(8,128)(2,1)}, bf16[2,64,512]{2,1,0:T(8,128)(2,1)}) custom-call(bf16[4,64,512]{2,1,0:T(8,128)(2,1)S(1)} %collective-permute-done.3.up_ref.h1_ref, bf16[4,64,512]{2,1,0:T(8,128)(2,1)S(1)} %collective-permute-done.4.down_ref.h3_ref), custom_call_target="tpu_custom_call" | custom-call | flops 1000 | bytes 500000 | tf_op jit(solution)/shard_map/take_halves/pallas_call | solution.py:149
  22.6 1.8 %collective-permute-start.5 = (bf16[2,64,512]{2,1,0:T(8,128)(2,1)}, bf16[2,64,512]{2,1,0:T(8,128)(2,1)S(1)}, u32[]{:S(2)}, u32[]{:S(2)}) collective-permute-start(bf16[2,64,512]{2,1,0:T(8,128)(2,1)} %get-tuple-element.36), channel_id=1, source_target_pairs={{0,4},{1,5},{2,6},{3,7},{4,8},{5,9},{6,10},{7,11},{8,12},{9,13},{1... | collective-permute-start | bytes 393224 | tf_op jit(solution)/shard_map/ppermute | solution.py:512
  24.4 1.4 %collective-permute-start.6 = (bf16[2,64,512]{2,1,0:T(8,128)(2,1)}, bf16[2,64,512]{2,1,0:T(8,128)(2,1)S(1)}, u32[]{:S(2)}, u32[]{:S(2)}) collective-permute-start(bf16[2,64,512]{2,1,0:T(8,128)(2,1)} %get-tuple-element.37), channel_id=1, source_target_pairs={{0,12},{1,13},{2,14},{3,15},{4,0},{5,1},{6,2},{7,3},{8,4},{9,5},{1... | collective-permute-start | bytes 393224 | tf_op jit(solution)/shard_map/ppermute | solution.py:512
  25.8 5.1 %all-to-all-done.recv_ref = bf16[32,2,2176]{2,1,0:T(2,128)(2,1)S(1)} async-done(((bf16[32,2,2176]{2,1,0:T(2,128)(2,1)}), bf16[32,2,2176]{2,1,0:T(2,128)(2,1)S(1)}, u32[]{:S(2)}, u32[]{:S(2)}) %all-to-all-start) | async-done | bytes 278560 | tf_op jit(solution)/shard_map/all_to_all | solution.py:507
  30.9 1.9 %owner_low.1._ = f32[128,1,1280]{2,1,0:T(1,128)} custom-call(s32[1]{0:T(128)} %bitcast.1.z_ref, bf16[32,2,2176]{2,1,0:T(2,128)(2,1)S(1)} %all-to-all-done.recv_ref, bf16[96,8192]{1,0:T(8,128)(2,1)S(1)} %get-tuple-element.34.down_ref, bf16[32,10240]{1,0:T(8,128)(2,1)S(1)} %get-tuple-element.35.up_ref), custom_call_target="tpu_custom_call" | custom-call | flops 40000000 | bytes 3400000 | tf_op jit(solution)/shard_map/owner_low/pallas_call | solution.py:195
  32.8 6.4 %all-to-all-start.1 = ((f32[128,1,1280]{2,1,0:T(1,128)}), f32[128,1,1280]{2,1,0:T(1,128)S(1)}, u32[]{:S(2)}, u32[]{:S(2)}) async-start(f32[128,1,1280]{2,1,0:T(1,128)} %owner_low.1._), calls=%async_computation.1 | async-start | bytes 1310720 | tf_op jit(solution)/shard_map/all_to_all | solution.py:516
  39.4 0.7 copy-done.1
  40.0 5.5 %base_project.1 = (f32[32,640]{1,0:T(8,128)S(1)}, f32[32,640]{1,0:T(8,128)S(1)}, bf16[512,128]{1,0:T(8,128)(2,1)S(1)}, bf16[512,128]{1,0:T(8,128)(2,1)S(1)}) custom-call(s32[2]{0:T(128)S(1)} %pad_add_fusion.place_ref, s32[66]{0:T(128)S(1)} %copy-done.1, bf16[4,64,512]{2,1,0:T(8,128)(2,1)S(1)} %stack_band.1.h0_ref, ...), custom_call_target="tpu_custom_call" | custom-call | flops 671000000 | bytes 11700000 | tf_op jit(solution)/shard_map/base_project/pallas_call | solution.py:268
  46.1 1.2 %collective-permute-start.8 = (f32[32,640]{1,0:T(8,128)S(1)}, f32[32,640]{1,0:T(8,128)S(1)}, u32[]{:S(2)}, u32[]{:S(2)}) collective-permute-start(f32[32,640]{1,0:T(8,128)S(1)} %get-tuple-element.45), channel_id=1, source_target_pairs={{0,1},{1,0},{2,3},{3,2},{4,5},{5,4},{6,7},{7,6},{8,9},{9,8},{10,11... | collective-permute-start | bytes 245768 | tf_op jit(solution)/shard_map/ppermute | solution.py:522
  47.7 6.5 %all-to-all-done.1.low_ref = f32[128,1,1280]{2,1,0:T(1,128)S(1)} async-done(((f32[128,1,1280]{2,1,0:T(1,128)}), f32[128,1,1280]{2,1,0:T(1,128)S(1)}, u32[]{:S(2)}, u32[]{:S(2)}) %all-to-all-start.1) | async-done | bytes 655392 | tf_op jit(solution)/shard_map/all_to_all | solution.py:516
  55.3 4.7 %attend_all.1 = (bf16[32,640]{1,0:T(8,128)(2,1)S(1)}, bf16[32,640]{1,0:T(8,128)(2,1)S(1)}) custom-call(s32[66]{0:T(128)S(1)} %copy-done.2, s32[1]{0:T(128)} %bitcast.parity_ref, s32[256,1]{1,0:T(8,128)S(1)} %reshape_reshape.4.used_ref, f32[128,1,1280]{2,1,0:T(1,128)S(1)} %all-to-all-done.1.low_ref, f32[32,640]{1,0:T(8,128)S(1)} %get-tuple-element.44.mine_ref, ...), custom_call_target="tpu_custom_call" | custom-call | flops 70000000 | bytes 1000000 | tf_op jit(solution)/shard_map/attend_all/pallas_call | solution.py:387
  60.0 1.0 %amend.1 = (bf16[32,640]{1,0:T(8,128)(2,1)S(1)}, bf16[32,640]{1,0:T(8,128)(2,1)S(1)}) custom-call(s32[66]{0:T(128)S(1)} %copy-done.2, s32[1]{0:T(128)} %bitcast.parity_ref, s32[64]{0:T(128)S(1)} %copy-done.3, f32[1,1280]{1,0:T(1,128)S(1)} %collective-permute-done.7.row_ref, f32[32,640]{1,0:T(8,128)S(1)} %get-tuple-element.44.mine_ref, ...), custom_call_target="tpu_custom_call" | custom-call | flops 2000000 | bytes 500000 | tf_op jit(solution)/shard_map/amend/pallas_call | solution.py:430
  61.0 1.7 %collective-permute-start.9 = (bf16[32,640]{1,0:T(8,128)(2,1)S(1)}, bf16[32,640]{1,0:T(8,128)(2,1)S(1)}, u32[]{:S(2)}, u32[]{:S(2)}) collective-permute-start(bf16[32,640]{1,0:T(8,128)(2,1)S(1)} %get-tuple-element.52), channel_id=1, source_target_pairs={{0,1},{1,0},{2,3},{3,2},{4,5},{5,4},{6,7},{7,6},{8,9},{9,8},{10,11... | collective-permute-start | bytes 122888 | tf_op jit(solution)/shard_map/ppermute | solution.py:540
  62.6 2.4 %collective-permute-done.9.back_ref = bf16[32,640]{1,0:T(8,128)(2,1)S(1)} collective-permute-done((bf16[32,640]{1,0:T(8,128)(2,1)S(1)}, bf16[32,640]{1,0:T(8,128)(2,1)S(1)}, u32[]{:S(2)}, u32[]{:S(2)}) %collective-permute-start.9) | collective-permute-done | bytes 40992 | tf_op jit(solution)/shard_map/ppermute | solution.py:540
  65.0 0.7 %weave.1 = (bf16[64,512]{1,0:T(8,128)(2,1)}, bf16[64,64]{1,0:T(8,128)(2,1)}, bf16[64,64]{1,0:T(8,128)(2,1)}) custom-call(s32[1]{0:T(128)} %bitcast.parity_ref, bf16[32,640]{1,0:T(8,128)(2,1)S(1)} %get-tuple-element.51.keep_ref, bf16[32,640]{1,0:T(8,128)(2,1)S(1)} %collective-permute-done.9.back_ref), custom_call_target="tpu_custom_call" | custom-call | tf_op jit(solution)/shard_map/weave/pallas_call | solution.py:472
  (30 shorter events, 2.8 us)
Async XLA Ops:
  0.6 9.0 %collective-permute-start = (bf16[64,512]{1,0:T(8,128)(2,1)}, bf16[64,512]{1,0:T(8,128)(2,1)S(1)}, u32[]{:S(2)}, u32[]{:S(2)}) collective-permute-start(bf16[64,512]{1,0:T(8,128)(2,1)} %hidden_hbm.1), channel_id=1, source_target_pairs={{0,1},{1,2},{2,3},{3,0},{4,5},{5,6},{6,7},{7,4},{8,9},{9,10},{10,1... | collective-permute-start | bytes 196616 | tf_op jit(solution)/shard_map/ppermute | solution.py:504
  2.7 7.0 %collective-permute-start.1 = (bf16[64,512]{1,0:T(8,128)(2,1)}, bf16[64,512]{1,0:T(8,128)(2,1)S(1)}, u32[]{:S(2)}, u32[]{:S(2)}) collective-permute-start(bf16[64,512]{1,0:T(8,128)(2,1)} %hidden_hbm.1), channel_id=1, source_target_pairs={{0,2},{1,3},{2,0},{3,1},{4,6},{5,7},{6,4},{7,5},{8,10},{9,11},{10,... | collective-permute-start | bytes 196616 | tf_op jit(solution)/shard_map/ppermute | solution.py:504
  6.3 4.5 %collective-permute-start.2 = (bf16[64,512]{1,0:T(8,128)(2,1)}, bf16[64,512]{1,0:T(8,128)(2,1)S(1)}, u32[]{:S(2)}, u32[]{:S(2)}) collective-permute-start(bf16[64,512]{1,0:T(8,128)(2,1)} %hidden_hbm.1), channel_id=1, source_target_pairs={{0,3},{1,0},{2,1},{3,2},{4,7},{5,4},{6,5},{7,6},{8,11},{9,8},{10,9... | collective-permute-start | bytes 196616 | tf_op jit(solution)/shard_map/ppermute | solution.py:504
  9.6 1.7 %copy-start = (s32[66]{0:T(128)}, s32[66]{0:T(128)S(1)}, u32[]{:S(2)}) copy-start(s32[66]{0:T(128)S(1)} %get-tuple-element.28._.plan_ref) | copy-start | bytes 796
  11.3 10.5 %collective-permute-start.3 = (bf16[4,64,512]{2,1,0:T(8,128)(2,1)S(1)}, bf16[4,64,512]{2,1,0:T(8,128)(2,1)S(1)}, u32[]{:S(2)}, u32[]{:S(2)}) collective-permute-start(bf16[4,64,512]{2,1,0:T(8,128)(2,1)S(1)} %stack_band.1.h0_ref), channel_id=1, source_target_pairs={{0,4},{1,5},{2,6},{3,7},{4,8},{5,9},{6,10},{7,11},{8,12},{9,13},{1... | collective-permute-start | bytes 786440 | tf_op jit(solution)/shard_map/ppermute | solution.py:509
  13.0 8.9 %collective-permute-start.4 = (bf16[4,64,512]{2,1,0:T(8,128)(2,1)S(1)}, bf16[4,64,512]{2,1,0:T(8,128)(2,1)S(1)}, u32[]{:S(2)}, u32[]{:S(2)}) collective-permute-start(bf16[4,64,512]{2,1,0:T(8,128)(2,1)S(1)} %stack_band.1.h0_ref), channel_id=1, source_target_pairs={{0,12},{1,13},{2,14},{3,15},{4,0},{5,1},{6,2},{7,3},{8,4},{9,5},{1... | collective-permute-start | bytes 786440 | tf_op jit(solution)/shard_map/ppermute | solution.py:509
  15.7 15.2 %all-to-all-start = ((bf16[32,2,2176]{2,1,0:T(2,128)(2,1)}), bf16[32,2,2176]{2,1,0:T(2,128)(2,1)S(1)}, u32[]{:S(2)}, u32[]{:S(2)}) async-start(bf16[32,2,2176]{2,1,0:T(2,128)(2,1)} %send_rows.1), calls=%async_computation | async-start | bytes 557056 | tf_op jit(solution)/shard_map/all_to_all | solution.py:507
  22.6 10.2 %collective-permute-start.5 = (bf16[2,64,512]{2,1,0:T(8,128)(2,1)}, bf16[2,64,512]{2,1,0:T(8,128)(2,1)S(1)}, u32[]{:S(2)}, u32[]{:S(2)}) collective-permute-start(bf16[2,64,512]{2,1,0:T(8,128)(2,1)} %get-tuple-element.36), channel_id=1, source_target_pairs={{0,4},{1,5},{2,6},{3,7},{4,8},{5,9},{6,10},{7,11},{8,12},{9,13},{1... | collective-permute-start | bytes 393224 | tf_op jit(solution)/shard_map/ppermute | solution.py:512
  24.4 8.4 %collective-permute-start.6 = (bf16[2,64,512]{2,1,0:T(8,128)(2,1)}, bf16[2,64,512]{2,1,0:T(8,128)(2,1)S(1)}, u32[]{:S(2)}, u32[]{:S(2)}) collective-permute-start(bf16[2,64,512]{2,1,0:T(8,128)(2,1)} %get-tuple-element.37), channel_id=1, source_target_pairs={{0,12},{1,13},{2,14},{3,15},{4,0},{5,1},{6,2},{7,3},{8,4},{9,5},{1... | collective-permute-start | bytes 393224 | tf_op jit(solution)/shard_map/ppermute | solution.py:512
  32.8 21.4 %all-to-all-start.1 = ((f32[128,1,1280]{2,1,0:T(1,128)}), f32[128,1,1280]{2,1,0:T(1,128)S(1)}, u32[]{:S(2)}, u32[]{:S(2)}) async-start(f32[128,1,1280]{2,1,0:T(1,128)} %owner_low.1._), calls=%async_computation.1 | async-start | bytes 1310720 | tf_op jit(solution)/shard_map/all_to_all | solution.py:516
  39.4 0.7 copy-start.1
  40.0 5.5 %copy-start.4 = (s32[64]{0:T(128)S(1)}, s32[64]{0:T(128)}, u32[]{:S(2)}) copy-start(s32[64]{0:T(128)} %param.21) | copy-start | bytes 772
  40.0 5.6 %copy-start.3 = (s32[64]{0:T(128)S(1)}, s32[64]{0:T(128)}, u32[]{:S(2)}) copy-start(s32[64]{0:T(128)} %used_ref) | copy-start | bytes 772
  40.0 14.2 %copy-start.2 = (s32[66]{0:T(128)S(1)}, s32[66]{0:T(128)}, u32[]{:S(2)}) copy-start(s32[66]{0:T(128)} %copy-done) | copy-start | bytes 796
  46.1 9.1 %collective-permute-start.8 = (f32[32,640]{1,0:T(8,128)S(1)}, f32[32,640]{1,0:T(8,128)S(1)}, u32[]{:S(2)}, u32[]{:S(2)}) collective-permute-start(f32[32,640]{1,0:T(8,128)S(1)} %get-tuple-element.45), channel_id=1, source_target_pairs={{0,1},{1,0},{2,3},{3,2},{4,5},{5,4},{6,7},{7,6},{8,9},{9,8},{10,11... | collective-permute-start | bytes 245768 | tf_op jit(solution)/shard_map/ppermute | solution.py:522
  54.8 5.2 %collective-permute-start.7 = (f32[1,1280]{1,0:T(1,128)S(1)}, f32[1,1280]{1,0:T(1,128)S(1)}, u32[]{:S(2)}, u32[]{:S(2)}) collective-permute-start(f32[1,1280]{1,0:T(1,128)S(1)} %pick.1), channel_id=1, source_target_pairs={{0,1},{1,0},{2,3},{3,2},{4,5},{5,4},{6,7},{7,6},{8,9},{9,8},{10,11... | collective-permute-start | bytes 15368 | tf_op jit(solution)/shard_map/ppermute | solution.py:532
  61.0 4.1 %collective-permute-start.9 = (bf16[32,640]{1,0:T(8,128)(2,1)S(1)}, bf16[32,640]{1,0:T(8,128)(2,1)S(1)}, u32[]{:S(2)}, u32[]{:S(2)}) collective-permute-start(bf16[32,640]{1,0:T(8,128)(2,1)S(1)} %get-tuple-element.52), channel_id=1, source_target_pairs={{0,1},{1,0},{2,3},{3,2},{4,5},{5,4},{6,7},{7,6},{8,9},{9,8},{10,11... | collective-permute-start | bytes 122888 | tf_op jit(solution)/shard_map/ppermute | solution.py:540

commit v5 on v4

--- a/solution.py
+++ b/solution.py
@@ -23,8 +23,8 @@
 
 
 def plan_kernel(
-    z_ref, requests_hbm, slots_hbm, hidden_hbm, down_hbm, up_hbm,
-    plan_ref, spread_ref, code_ref, down_ref, up_ref, hidden_ref,
+    z_ref, requests_hbm, slots_hbm, hidden_hbm, down_hbm, up_hbm, key_hbm, value_hbm,
+    plan_ref, spread_ref, code_ref, down_ref, up_ref, hidden_ref, pair_ref,
     eye_ref, wide_ref, requests_ref, slots_ref, sems,
 ):
     copies = [
@@ -69,7 +69,14 @@
 
     plan_ref[64] = first
     plan_ref[65] = last
-    for copy in near:
+    column = jnp.maximum(last, 0) >> 1
+    cache = [
+        pltpu.make_async_copy(key_hbm.at[column], pair_ref.at[0], sems.at[5]),
+        pltpu.make_async_copy(value_hbm.at[column], pair_ref.at[1], sems.at[6]),
+    ]
+    for copy in cache:
+        copy.start()
+    for copy in near + cache:
         copy.wait()
 
 
@@ -77,7 +84,7 @@
     return [pltpu.with_memory_space_constraint(x, pltpu.HBM) for x in arrays]
 
 
-def make_plan(z, requests, slots, hidden, down, up):
+def make_plan(z, requests, slots, hidden, down, up, keys, values):
     return pl.pallas_call(
         plan_kernel,
         out_shape=[
@@ -87,20 +94,21 @@
             pltpu.VMEM(down.shape, BF16),
             pltpu.VMEM(up.shape, BF16),
             pltpu.VMEM(hidden.shape, BF16),
-        ],
-        in_specs=[SMEM] + [ANY] * 5,
-        out_specs=[SMEM, VMEM, VMEM, ANY, ANY, VMEM],
+            jax.ShapeDtypeStruct((2,) + keys.shape[1:], BF16),
+        ],
+        in_specs=[SMEM] + [ANY] * 7,
+        out_specs=[SMEM, VMEM, VMEM, ANY, ANY, VMEM, VMEM],
         scratch_shapes=[
             pltpu.VMEM((64, 128), F32),
             pltpu.VMEM((64, 128), F32),
             pltpu.SMEM((1, 63), jnp.int32),
             pltpu.SMEM((64,), jnp.int32),
-            pltpu.SemaphoreType.DMA((5,)),
+            pltpu.SemaphoreType.DMA((7,)),
         ],
         cost_estimate=pl.CostEstimate(flops=1_000_000, bytes_accessed=500_000, transcendentals=0),
         compiler_params=pltpu.CompilerParams(vmem_limit_bytes=4 * 2**20),
         name="make_plan",
-    )(z, *in_hbm(requests, slots, hidden, down, up))
+    )(z, *in_hbm(requests, slots, hidden, down, up, keys, values))
 
 
 def send_kernel(spread_ref, code_ref, h0_ref, h1_ref, h2_ref, h3_ref, sent_ref):
@@ -234,18 +242,12 @@
 
 
 def base_kernel(
-    place_ref, plan_ref, h0_ref, h1_ref, ha_ref, hb_ref, h3_ref, wq_hbm, wk_hbm, wv_hbm, key_hbm, value_hbm, _,
-    mine_ref, give_ref, key2_ref, value2_ref, wq_ref, wkv_ref, acc_ref, sems, cache_sems,
+    place_ref, plan_ref, h0_ref, h1_ref, ha_ref, hb_ref, h3_ref, wq_hbm, wk_hbm, wv_hbm, _,
+    mine_ref, give_ref, wq_ref, wkv_ref, acc_ref, sems,
 ):
     y, z = place_ref[0], place_ref[1]
     rows = [(((y - a) & 3) * 4 + ((z - b) & 3)) * 512 for a in range(4) for b in range(4)]
     copies = weight_copies(rows, wq_hbm, wk_hbm, wv_hbm, wq_ref, wkv_ref, sems)
-    cache = [
-        pltpu.make_async_copy(key_hbm.at[plan_ref[65] >> 1], key2_ref, cache_sems.at[0]),
-        pltpu.make_async_copy(value_hbm.at[plan_ref[65] >> 1], value2_ref, cache_sems.at[1]),
-    ]
-    for copy in cache:
-        copy.start()
     hiddens = [ref[b] for ref in (h0_ref, h1_ref) for b in range(4)]
     hiddens += [ha_ref[0], ha_ref[1], hb_ref[0], hb_ref[1]] + [h3_ref[b] for b in range(4)]
     q, kv = jnp.zeros((64, 512), F32), jnp.zeros((64, 128), F32)
@@ -259,51 +261,35 @@
         cols = slice(c * 128, (c + 1) * 128)
         acc_ref[...] = q[:, cols] if c < 4 else kv
         even, odd = acc_ref[pl.ds(0, 32, 2), :], acc_ref[pl.ds(1, 32, 2), :]
-        mine_ref[:, cols], give_ref[:, cols] = sides(parity, even, odd)
-    for copy in cache:
-        copy.wait()
-
-
-def base_project(place, plan, bands, wq, wkt, wvt, keys, values, after):
+        mine_ref[0:32, cols], give_ref[0:32, cols] = sides(parity, even, odd)
+    row = pl.ds(plan_ref[65] >> 1, 1)
+    mine_ref[32:40, :] = jnp.broadcast_to(give_ref[row, :], (8, 640))
+    give_ref[32:40, :] = jnp.broadcast_to(mine_ref[row, :], (8, 640))
+
+
+def base_project(place, plan, bands, wq, wkt, wvt, after):
     return pl.pallas_call(
         base_kernel,
         out_shape=[
-            jax.ShapeDtypeStruct((32, 640), F32),
-            jax.ShapeDtypeStruct((32, 640), F32),
-            jax.ShapeDtypeStruct(keys.shape[1:], BF16),
-            jax.ShapeDtypeStruct(values.shape[1:], BF16),
-        ],
-        in_specs=[SMEM] * 2 + [VMEM] * 5 + [ANY] * 6,
-        out_specs=[VMEM] * 4,
+            jax.ShapeDtypeStruct((40, 640), F32),
+            jax.ShapeDtypeStruct((40, 640), F32),
+        ],
+        in_specs=[SMEM] * 2 + [VMEM] * 5 + [ANY] * 4,
+        out_specs=[VMEM] * 2,
         scratch_shapes=[
             pltpu.VMEM((16, 512, 512), BF16),
             pltpu.VMEM((16, 128, 512), BF16),
             pltpu.VMEM((64, 128), F32),
             pltpu.SemaphoreType.DMA((3, 16)),
-            pltpu.SemaphoreType.DMA((2,)),
         ],
         cost_estimate=pl.CostEstimate(flops=671_000_000, bytes_accessed=11_700_000, transcendentals=0),
         compiler_params=pltpu.CompilerParams(vmem_limit_bytes=16 * 2**20),
         name="base_project",
-    )(place, plan, *bands, *in_hbm(wq, wkt, wvt, keys, values), after)
+    )(place, plan, *bands, *in_hbm(wq, wkt, wvt), after)
 
 
 def rotate(part, cos, sin):
     return part * cos + pltpu.roll(part, 64, 1) * sin
-
-
-def attend(query, key_new, value_new, keys, values, used):
-    scale = 1.0 / math.sqrt(HEAD)
-    scores = dot_nt(query.astype(BF16), keys) * scale
-    own = jnp.sum(query * key_new, axis=1, keepdims=True) * scale
-    valid = lax.broadcasted_iota(jnp.int32, scores.shape, 1) < used
-    top = jnp.max(jnp.where(valid, scores, -jnp.inf), axis=1, keepdims=True)
-    top = jnp.maximum(top, own)
-    weights = jnp.where(valid, jnp.exp(scores - top), 0.0)
-    own_weight = jnp.exp(own - top)
-    total = jnp.sum(weights, axis=1, keepdims=True) + own_weight
-    out = dot(weights.astype(BF16), values) + own_weight.astype(BF16).astype(F32) * value_new
-    return out / total
 
 
 def sides(parity, mine, other):
@@ -332,7 +318,7 @@
 
 
 def attend_kernel(
-    plan_ref, parity_ref, used_ref, low_ref, mine_ref, other_ref, cos_ref, sin_ref, key_hbm, value_hbm,
+    plan_ref, parity_ref, filled_ref, low_ref, mine_ref, other_ref, cos_ref, sin_ref, pair_ref, key_hbm, value_hbm,
     keep_ref, give_ref, rows_ref, query_ref, near_ref, fresh_ref, out_ref, key_ref, value_ref, sems,
 ):
     copies = []
@@ -344,24 +330,42 @@
     parity = parity_ref[0]
     for i in range(32):
         rows_ref[i : i + 1, :] = low_ref[plan_ref[2 * i + parity]]
+    rows_ref[32:40, :] = jnp.broadcast_to(low_ref[plan_ref[plan_ref[64]]], (8, 1280))
+    last = plan_ref[65]
+
+    def table(ref):
+        mine = jnp.where(parity == 0, ref[pl.ds(0, 32, 2), :], ref[pl.ds(1, 32, 2), :])
+        more = jnp.broadcast_to(ref[pl.ds(last, 1), :], (8, 128))
+        return jnp.concatenate([mine, more], axis=0)
+
     heads, key, value = project(
-        parity, mine_ref[...], other_ref[...], rows_ref[...], cos_ref[...], sin_ref[...]
+        parity, mine_ref[...], other_ref[...], rows_ref[...], table(cos_ref), table(sin_ref)
     )
     for h in range(8):
-        query_ref[pl.ds(h, 32, 8), :] = heads[h]
-        near_ref[pl.ds(h, 32, 8), :] = key
-        fresh_ref[pl.ds(h, 32, 8), :] = value
+        query_ref[pl.ds(h, 40, 8), :] = heads[h]
+        near_ref[pl.ds(h, 40, 8), :] = key
+        fresh_ref[pl.ds(h, 40, 8), :] = value
     scale = 1.0 / math.sqrt(HEAD)
+    def caches(half, ref, which):
+        return [ref[half * 16 + s] for s in range(16)] + ([pair_ref[which]] if half else [])
+
     halves = []
     for half in range(2):
-        rows = slice(half * 128, (half + 1) * 128)
+        rows = slice(half * 128, half * 136 + 128)
         query = query_ref[rows, :]
         own = jnp.sum(query * near_ref[rows, :], axis=1, keepdims=True) * scale
         copies[half].wait()
         scores = jnp.concatenate(
-            [dot_nt(query[s * 8 : s * 8 + 8].astype(BF16), key_ref[half * 16 + s]) for s in range(16)], axis=0
+            [
+                dot_nt(query[s * 8 : s * 8 + 8].astype(BF16), block)
+                for s, block in enumerate(caches(half, key_ref, 0))
+            ],
+            axis=0,
         ) * scale
-        valid = lax.broadcasted_iota(jnp.int32, (128, 512), 1) < used_ref[rows, :]
+        used = [filled_ref[2 * (half * 16 + s) + parity] for s in range(16)] + [filled_ref[last]] * half
+        slot = lax.broadcasted_iota(jnp.int32, (8, 512), 1)
+        left = jnp.concatenate([n - slot for n in used], axis=0)
+        valid = left > 0
         top = jnp.max(jnp.where(valid, scores, -jnp.inf), axis=1, keepdims=True)
         top = jnp.maximum(top, own)
         weights = jnp.where(valid, jnp.exp(scores - top), 0.0)
@@ -371,30 +375,34 @@
     for half in range(2):
         copies[2 + half].wait()
         weights, own_weight, total = halves[half]
-        rows = slice(half * 128, (half + 1) * 128)
+        rows = slice(half * 128, half * 136 + 128)
         own = own_weight.astype(BF16).astype(F32) * fresh_ref[rows, :]
         out = jnp.concatenate(
-            [dot(weights[s * 8 : s * 8 + 8], value_ref[half * 16 + s]) for s in range(16)], axis=0
+            [
+                dot(weights[s * 8 : s * 8 + 8], block)
+                for s, block in enumerate(caches(half, value_ref, 1))
+            ],
+            axis=0,
         )
         out_ref[rows, :] = (out + own) / total
-    outs = [out_ref[pl.ds(h, 32, 8), :] for h in range(8)]
+    outs = [out_ref[pl.ds(h, 40, 8), :] for h in range(8)]
     keep, give = split(parity, outs, key, value)
     keep_ref[...] = keep.astype(BF16)
     give_ref[...] = give.astype(BF16)
 
 
-def attend_all(plan, parity, used, low, mine, other, cos, sin, keys, values):
+def attend_all(plan, parity, filled, low, mine, other, cos, sin, pair, keys, values):
     return pl.pallas_call(
         attend_kernel,
-        out_shape=[jax.ShapeDtypeStruct((32, 640), BF16)] * 2,
-        in_specs=[SMEM] * 2 + [VMEM] * 6 + [ANY] * 2,
+        out_shape=[jax.ShapeDtypeStruct((40, 640), BF16)] * 2,
+        in_specs=[SMEM] * 3 + [VMEM] * 6 + [ANY] * 2,
         out_specs=[VMEM] * 2,
         scratch_shapes=[
-            pltpu.VMEM((32, 1280), F32),
-            pltpu.VMEM((256, 128), F32),
-            pltpu.VMEM((256, 128), F32),
-            pltpu.VMEM((256, 128), F32),
-            pltpu.VMEM((256, 128), F32),
+            pltpu.VMEM((40, 1280), F32),
+            pltpu.VMEM((320, 128), F32),
+            pltpu.VMEM((320, 128), F32),
+            pltpu.VMEM((320, 128), F32),
+            pltpu.VMEM((320, 128), F32),
             pltpu.VMEM(keys.shape, BF16),
             pltpu.VMEM(values.shape, BF16),
             pltpu.SemaphoreType.DMA((4,)),
@@ -402,64 +410,24 @@
         cost_estimate=pl.CostEstimate(flops=70_000_000, bytes_accessed=1_000_000, transcendentals=131_072),
         compiler_params=pltpu.CompilerParams(vmem_limit_bytes=20 * 2**20),
         name="attend_all",
-    )(plan, parity, used, low, mine, other, cos, sin, keys, values)
-
-
-def amend_kernel(
-    plan_ref, parity_ref, used_ref, row_ref, mine_ref, other_ref, cos_ref, sin_ref, key_ref, value_ref,
-    keep_in, give_in, keep_ref, give_ref, query_ref,
-):
-    parity = parity_ref[0]
-    first, last = plan_ref[64], plan_ref[65]
-    here = ((first & 1) == parity) & ((last & 1) == parity)
-    i = last >> 1
-    one = pl.ds(i, 1)
-    heads, key, value = project(
-        parity, mine_ref[one, :], other_ref[one, :], row_ref[0:1, :], cos_ref[one, :], sin_ref[one, :]
-    )
-    for h in range(8):
-        query_ref[h : h + 1, :] = heads[h]
-    out = attend(query_ref[...], key, value, key_ref[...], value_ref[...], used_ref[last])
-    keep, give = split(parity, [out[h : h + 1] for h in range(8)], key, value)
-    hit = (lax.broadcasted_iota(jnp.int32, (32, 640), 0) == i) & here
-    keep_ref[...] = jnp.where(hit, keep, keep_in[...].astype(F32)).astype(BF16)
-    give_ref[...] = jnp.where(hit, give, give_in[...].astype(F32)).astype(BF16)
-
-
-def amend(plan, parity, used, row, mine, other, cos, sin, keys, values, keep, give):
-    return pl.pallas_call(
-        amend_kernel,
-        out_shape=[jax.ShapeDtypeStruct((32, 640), BF16)] * 2,
-        in_specs=[SMEM] * 3 + [VMEM] * 9,
-        out_specs=[VMEM] * 2,
-        scratch_shapes=[pltpu.VMEM((8, 128), F32)],
-        cost_estimate=pl.CostEstimate(flops=2_000_000, bytes_accessed=500_000, transcendentals=4096),
-        compiler_params=pltpu.CompilerParams(vmem_limit_bytes=4 * 2**20),
-        name="amend",
-    )(plan, parity, used, row, mine, other, cos, sin, keys, values, keep, give)
-
-
-def pick_kernel(plan_ref, low_ref, row_ref):
-    row_ref[...] = low_ref[plan_ref[plan_ref[64]]]
-
-
-def pick(plan, low):
-    return pl.pallas_call(
-        pick_kernel,
-        out_shape=jax.ShapeDtypeStruct((1, 1280), F32),
-        in_specs=[SMEM, VMEM],
-        out_specs=VMEM,
-        compiler_params=pltpu.CompilerParams(vmem_limit_bytes=2 * 2**20),
-        name="pick",
-    )(plan, low)
-
-
-def weave_kernel(parity_ref, keep_ref, back_ref, out_ref, key_ref, value_ref, rows_ref):
-    even, odd = sides(parity_ref[0], keep_ref[...].astype(F32), back_ref[...].astype(F32))
+    )(plan, parity, filled, low, mine, other, cos, sin, pair, keys, values)
+
+
+def weave_kernel(plan_ref, parity_ref, keep_ref, back_ref, out_ref, key_ref, value_ref, rows_ref, extra_ref):
+    parity, first, last = parity_ref[0], plan_ref[64], plan_ref[65]
+    keep, back = keep_ref[...].astype(F32), back_ref[...].astype(F32)
+    even, odd = sides(parity, keep[0:32], back[0:32])
+    extra_ref[...] = jnp.where(parity == (last & 1), back[32:40], keep[32:40])
+    same = (first & 1) == (last & 1)
     for c in range(5):
         cols = slice(c * 128, (c + 1) * 128)
         rows_ref[pl.ds(0, 32, 2), :] = even[:, cols]
         rows_ref[pl.ds(1, 32, 2), :] = odd[:, cols]
+
+        @pl.when(same)
+        def _():
+            rows_ref[pl.ds(last, 1), :] = extra_ref[0:1, cols]
+
         both = rows_ref[...].astype(BF16)
         if c < 4:
             out_ref[:, cols] = both
@@ -468,7 +436,7 @@
             value_ref[...] = both[:, 64:128]
 
 
-def weave(parity, keep, back):
+def weave(plan, parity, keep, back):
     return pl.pallas_call(
         weave_kernel,
         out_shape=[
@@ -476,12 +444,12 @@
             jax.ShapeDtypeStruct((64, 64), BF16),
             jax.ShapeDtypeStruct((64, 64), BF16),
         ],
-        in_specs=[SMEM, VMEM, VMEM],
+        in_specs=[SMEM, SMEM, VMEM, VMEM],
         out_specs=[VMEM] * 3,
-        scratch_shapes=[pltpu.VMEM((64, 128), F32)],
+        scratch_shapes=[pltpu.VMEM((64, 128), F32), pltpu.VMEM((8, 640), F32)],
         compiler_params=pltpu.CompilerParams(vmem_limit_bytes=2 * 2**20),
         name="weave",
-    )(parity, keep, back)
+    )(plan, parity, keep, back)
 
 
 def local(
@@ -498,8 +466,9 @@
     def y_turn(k):
         return [(4 * a + b, 4 * ((a + k) % 4) + b) for a in range(4) for b in range(4)]
 
-    plan, spread, code, down_near, up_near, hidden_near = make_plan(
-        z.reshape(1), requests, slots, hidden, down_maps.reshape(96, 8192), up_maps.reshape(32, 10240)
+    plan, spread, code, down_near, up_near, hidden_near, pair = make_plan(
+        z.reshape(1), requests, slots, hidden, down_maps.reshape(96, 8192), up_maps.reshape(32, 10240),
+        key_cache[0], value_cache[0],
     )
     around_z = [hidden_near] + [lax.ppermute(hidden, "tensor", z_turn(k)) for k in (1, 2, 3)]
     sent = send_rows(spread, code, around_z)
@@ -510,35 +479,27 @@
 
     halves = take_halves(up, down)
     halves = [lax.ppermute(half, "tensor", y_turn(k)) for half, k in zip(halves, (1, 3))]
+    pair = lax.ppermute(pair, "tensor", swap)
     recv, up, down = lax.optimization_barrier((recv, up, down))
     low_sent = owner_low(z.reshape(1), recv, down_near, up_near)
-    low_sent, *halves = lax.optimization_barrier((low_sent, *halves))
+    low_sent, pair, *halves = lax.optimization_barrier((low_sent, pair, *halves))
     low = lax.all_to_all(low_sent, ROUTE, 0, 0, tiled=True)
 
     place = jnp.stack([y, z]).astype(jnp.int32)
-    mine, give, key2, value2 = base_project(
-        place, plan, (band, up, *halves, down), wq, wk.T, wv.T, key_cache[0], value_cache[0], low_sent
-    )
+    mine, give = base_project(place, plan, (band, up, *halves, down), wq, wk.T, wv.T, low_sent)
     other = lax.ppermute(give, "tensor", swap)
 
-    positions, filled, mine = lax.optimization_barrier((positions, filled, mine))
-    pos = lax.dynamic_index_in_dim(positions.reshape(32, 2), parity, 1, keepdims=False)
+    pos, mine = lax.optimization_barrier((positions, mine))
     freq = THETA ** (-2.0 * jnp.arange(64, dtype=F32) / HEAD)
     angle = pos.astype(F32)[:, None] * freq[None, :]
     cos, sin = jnp.cos(angle), jnp.sin(angle)
     cos, sin = jnp.concatenate([cos, cos], 1), jnp.concatenate([-sin, sin], 1)
 
     which = parity.reshape(1)
-    row = lax.ppermute(pick(plan, low), "tensor", swap)
     keys, values = in_hbm(key_cache[0], value_cache[0])
-    used = lax.dynamic_index_in_dim(filled.reshape(32, 2), parity, 1, keepdims=False)
-    used = jnp.repeat(used, 8).reshape(256, 1)
-    keep, give = attend_all(plan, which, used, low, mine, other, cos, sin, keys, values)
-    keep, give = amend(
-        plan, which, filled, row, mine, other, cos, sin, key2, value2, keep, give
-    )
+    keep, give = attend_all(plan, which, filled, low, mine, other, cos, sin, pair, keys, values)
     back = lax.ppermute(give, "tensor", swap)
-    return tuple(weave(which, keep, back))
+    return tuple(weave(plan, which, keep, back))
 
 
 def solution(mesh):

time: 66 us -> 65.7 us (level)
    ppermute x1, waiting for transfers between devices: 0.01 us -> 4.54 us  [local(): other = lax.ppermute(give, 'tensor', swap)]
    all_to_all x1, waiting for transfers between devices: 6.48 us -> 2.17 us  [local(): low = lax.all_to_all(low_sent, ROUTE, 0, 0, tiled=True)]
    ppermute x1, waiting for transfers between devices: 2.4 us -> 3.69 us  [local(): back = lax.ppermute(give, 'tensor', swap)]
    ppermute x1, starting transfers between devices: 1.68 us -> 0.5 us  [local(): back = lax.ppermute(give, 'tensor', swap)]
    ppermute x3, waiting for transfers between devices: 1.13 us -> 0.01 us  [local(): lax.ppermute(hidden, 'tensor', z_turn(k))]
    all_to_all x1, waiting for transfers between devices: 5.12 us -> 4.05 us  [local(): lax.all_to_all(sent, ('dp', 'tensor'), 0, 0, tiled=True, axis_index_group...]
    pallas_call x4 -> x2, Pallas kernels: 11.7 us -> 10.7 us  [the longest x1 5.99 us: base_project(): pl.pallas_call(base_kernel, out_shape=[jax.ShapeDtypeStruct((40, 640), F3...]
    pallas_call x1, Pallas kernels: 2.31 us -> 3.29 us  [make_plan(): pl.pallas_call(plan_kernel, out_shape=[jax.ShapeDtypeStruct((66,), jnp.in...]
  transfers between devices with their start and end apart: 12 -> 12, of which waited for: 5 -> 4; matrix products, arithmetic and copies ran while one was open for 2% -> 1% of each run, Pallas kernels for 25% -> 20%
where the time goes in v5:
time: 65.7 us; the launch traced here: 65.4 us
  starting transfers between devices  28.8 us (44%)
  Pallas kernels  19.5 us (30%)
  waiting for transfers between devices  14.5 us (22%)
  local copies, waits for them, and re-layouts  1.38 us (2%)
  between operations  0.76 us (1%)
    all_to_all x1, starting transfers between devices, local(): low = lax.all_to_all(low_sent, ROUTE, 0, 0, tiled=True)  6.77 us
    ppermute x3, starting transfers between devices, local(): lax.ppermute(hidden, 'tensor', z_turn(k))  6.66 us
    all_to_all x1, starting transfers between devices, local(): lax.all_to_all(sent, ('dp', 'tensor'), 0, 0, tiled=True, axis_index_group...  6.11 us
    pallas_call x1, Pallas kernels, base_project(): pl.pallas_call(base_kernel, out_shape=[jax.ShapeDtypeStruct((40, 640), F3...  5.99 us
    pallas_call x1, Pallas kernels, attend_all(): pl.pallas_call(attend_kernel, out_shape=[jax.ShapeDtypeStruct((40, 640),...  4.76 us
    ppermute x1, waiting for transfers between devices, local(): other = lax.ppermute(give, 'tensor', swap)  4.54 us
    all_to_all x1, waiting for transfers between devices, local(): lax.all_to_all(sent, ('dp', 'tensor'), 0, 0, tiled=True, axis_index_group...  4.05 us
    ppermute x1, waiting for transfers between devices, local(): back = lax.ppermute(give, 'tensor', swap)  3.69 us
  transfers between devices with their start and end apart: 12, of which 4 were waited for; matrix products, arithmetic and copies ran while one was open for 1% of the time, Pallas kernels for 20%

profile of v5, /device:TPU:0, one launch (start us, length us, event | category | flops | bytes accessed | tf_op | source)
XLA Modules:
  0.0 65.4 jit_solution(12979823489925591394)
XLA Ops:
  0.6 2.1 %collective-permute-start = (bf16[64,512]{1,0:T(8,128)(2,1)}, bf16[64,512]{1,0:T(8,128)(2,1)S(1)}, u32[]{:S(2)}, u32[]{:S(2)}) collective-permute-start(bf16[64,512]{1,0:T(8,128)(2,1)} %hidden_hbm.1), channel_id=1, source_target_pairs={{0,1},{1,2},{2,3},{3,0},{4,5},{5,6},{6,7},{7,4},{8,9},{9,10},{10,1... | collective-permute-start | bytes 196616 | tf_op jit(solution)/shard_map/ppermute | solution.py:473
  2.7 3.6 %collective-permute-start.1 = (bf16[64,512]{1,0:T(8,128)(2,1)}, bf16[64,512]{1,0:T(8,128)(2,1)S(1)}, u32[]{:S(2)}, u32[]{:S(2)}) collective-permute-start(bf16[64,512]{1,0:T(8,128)(2,1)} %hidden_hbm.1), channel_id=1, source_target_pairs={{0,2},{1,3},{2,0},{3,1},{4,6},{5,7},{6,4},{7,5},{8,10},{9,11},{10,... | collective-permute-start | bytes 196616 | tf_op jit(solution)/shard_map/ppermute | solution.py:473
  6.3 1.0 %collective-permute-start.2 = (bf16[64,512]{1,0:T(8,128)(2,1)}, bf16[64,512]{1,0:T(8,128)(2,1)S(1)}, u32[]{:S(2)}, u32[]{:S(2)}) collective-permute-start(bf16[64,512]{1,0:T(8,128)(2,1)} %hidden_hbm.1), channel_id=1, source_target_pairs={{0,3},{1,0},{2,1},{3,2},{4,7},{5,4},{6,5},{7,6},{8,11},{9,8},{10,9... | collective-permute-start | bytes 196616 | tf_op jit(solution)/shard_map/ppermute | solution.py:473
  7.3 3.3 %make_plan.1 = (s32[66]{0:T(128)S(1)}, f32[64,128]{1,0:T(8,128)S(1)}, f32[64,128]{1,0:T(8,128)S(1)}, bf16[96,8192]{1,0:T(8,128)(2,1)S(1)}, bf16[32,10240]{1,0:T(...) custom-call(s32[1]{0:T(128)} %bitcast.z_ref, s32[1,63]{1,0:T(1,128)} %requests_hbm.1, ...), custom_call_target="tpu_custom_call" | custom-call | flops 1000000 | bytes 500000 | tf_op jit(solution)/shard_map/make_plan/pallas_call | solution.py:88
  10.6 0.7 %copy-done.4 = bf16[2,512,128]{2,1,0:T(8,128)(2,1)} copy-done((bf16[2,512,128]{2,1,0:T(8,128)(2,1)}, bf16[2,512,128]{2,1,0:T(8,128)(2,1)S(1)}, u32[]{:S(2)}) %copy-start.4) | copy-done | bytes 262168
  11.9 1.6 %collective-permute-start.3 = (bf16[4,64,512]{2,1,0:T(8,128)(2,1)S(1)}, bf16[4,64,512]{2,1,0:T(8,128)(2,1)S(1)}, u32[]{:S(2)}, u32[]{:S(2)}) collective-permute-start(bf16[4,64,512]{2,1,0:T(8,128)(2,1)S(1)} %stack_band.1.h0_ref), channel_id=1, source_target_pairs={{0,4},{1,5},{2,6},{3,7},{4,8},{5,9},{6,10},{7,11},{8,12},{9,13},{1... | collective-permute-start | bytes 786440 | tf_op jit(solution)/shard_map/ppermute | solution.py:478
  13.6 1.7 %collective-permute-start.4 = (bf16[4,64,512]{2,1,0:T(8,128)(2,1)S(1)}, bf16[4,64,512]{2,1,0:T(8,128)(2,1)S(1)}, u32[]{:S(2)}, u32[]{:S(2)}) collective-permute-start(bf16[4,64,512]{2,1,0:T(8,128)(2,1)S(1)} %stack_band.1.h0_ref), channel_id=1, source_target_pairs={{0,12},{1,13},{2,14},{3,15},{4,0},{5,1},{6,2},{7,3},{8,4},{9,5},{1... | collective-permute-start | bytes 786440 | tf_op jit(solution)/shard_map/ppermute | solution.py:478
  15.2 1.1 %send_rows.1 = bf16[32,2,2176]{2,1,0:T(2,128)(2,1)} custom-call(f32[64,128]{1,0:T(8,128)S(1)} %get-tuple-element.26.spread_ref, f32[64,128]{1,0:T(8,128)S(1)} %get-tuple-element.27.code_ref, bf16[64,512]{1,0:T(8,128)(2,1)S(1)} %get-tuple-element.28.h0_ref, bf16[64,512]{1,0:T(8,128)(2,1)S(1)} %collective-permute-done.h1_ref, ...), custom_call_target="tpu_custom_call" | custom-call | flops 1000000 | bytes 500000 | tf_op jit(solution)/shard_map/send_rows/pallas_call | solution.py:123
  16.3 6.1 %all-to-all-start = ((bf16[32,2,2176]{2,1,0:T(2,128)(2,1)}), bf16[32,2,2176]{2,1,0:T(2,128)(2,1)S(1)}, u32[]{:S(2)}, u32[]{:S(2)}) async-start(bf16[32,2,2176]{2,1,0:T(2,128)(2,1)} %send_rows.1), calls=%async_computation | async-start | bytes 557056 | tf_op jit(solution)/shard_map/all_to_all | solution.py:476
  22.4 1.1 %collective-permute-start.5 = (bf16[2,512,128]{2,1,0:T(8,128)(2,1)}, bf16[2,512,128]{2,1,0:T(8,128)(2,1)S(1)}, u32[]{:S(2)}, u32[]{:S(2)}) collective-permute-start(bf16[2,512,128]{2,1,0:T(8,128)(2,1)} %copy-done.4), channel_id=1, source_target_pairs={{0,1},{1,0},{2,3},{3,2},{4,5},{5,4},{6,7},{7,6},{8,9},{9,8},{10,11... | collective-permute-start | bytes 786440 | tf_op jit(solution)/shard_map/ppermute | solution.py:482
  23.5 0.7 %take_halves.1 = (bf16[2,64,512]{2,1,0:T(8,128)(2,1)}, bf16[2,64,512]{2,1,0:T(8,128)(2,1)}) custom-call(bf16[4,64,512]{2,1,0:T(8,128)(2,1)S(1)} %collective-permute-done.3.up_ref.h1_ref, bf16[4,64,512]{2,1,0:T(8,128)(2,1)S(1)} %collective-permute-done.4.down_ref.h3_ref), custom_call_target="tpu_custom_call" | custom-call | flops 1000 | bytes 500000 | tf_op jit(solution)/shard_map/take_halves/pallas_call | solution.py:157
  24.2 1.8 %collective-permute-start.6 = (bf16[2,64,512]{2,1,0:T(8,128)(2,1)}, bf16[2,64,512]{2,1,0:T(8,128)(2,1)}, u32[]{:S(2)}, u32[]{:S(2)}) collective-permute-start(bf16[2,64,512]{2,1,0:T(8,128)(2,1)} %get-tuple-element.33), channel_id=1, source_target_pairs={{0,4},{1,5},{2,6},{3,7},{4,8},{5,9},{6,10},{7,11},{8,12},{9,13},{1... | collective-permute-start | bytes 393224 | tf_op jit(solution)/shard_map/ppermute | solution.py:481
  26.0 1.4 %collective-permute-start.7 = (bf16[2,64,512]{2,1,0:T(8,128)(2,1)}, bf16[2,64,512]{2,1,0:T(8,128)(2,1)}, u32[]{:S(2)}, u32[]{:S(2)}) collective-permute-start(bf16[2,64,512]{2,1,0:T(8,128)(2,1)} %get-tuple-element.34), channel_id=1, source_target_pairs={{0,12},{1,13},{2,14},{3,15},{4,0},{5,1},{6,2},{7,3},{8,4},{9,5},{1... | collective-permute-start | bytes 393224 | tf_op jit(solution)/shard_map/ppermute | solution.py:481
  27.5 4.0 %all-to-all-done.recv_ref = bf16[32,2,2176]{2,1,0:T(2,128)(2,1)S(1)} async-done(((bf16[32,2,2176]{2,1,0:T(2,128)(2,1)}), bf16[32,2,2176]{2,1,0:T(2,128)(2,1)S(1)}, u32[]{:S(2)}, u32[]{:S(2)}) %all-to-all-start) | async-done | bytes 278560 | tf_op jit(solution)/shard_map/all_to_all | solution.py:476
  31.5 1.9 %owner_low.1._ = f32[128,1,1280]{2,1,0:T(1,128)} custom-call(s32[1]{0:T(128)} %bitcast.z_ref, bf16[32,2,2176]{2,1,0:T(2,128)(2,1)S(1)} %all-to-all-done.recv_ref, bf16[96,8192]{1,0:T(8,128)(2,1)S(1)} %get-tuple-element.30.down_ref, bf16[32,10240]{1,0:T(8,128)(2,1)S(1)} %get-tuple-element.31.up_ref), custom_call_target="tpu_custom_call" | custom-call | flops 40000000 | bytes 3400000 | tf_op jit(solution)/shard_map/owner_low/pallas_call | solution.py:203
  33.4 6.8 %all-to-all-start.1 = ((f32[128,1,1280]{2,1,0:T(1,128)}), f32[128,1,1280]{2,1,0:T(1,128)S(1)}, u32[]{:S(2)}, u32[]{:S(2)}) async-start(f32[128,1,1280]{2,1,0:T(1,128)} %owner_low.1._), calls=%async_computation.1 | async-start | bytes 1310720 | tf_op jit(solution)/shard_map/all_to_all | solution.py:486
  40.3 0.7 copy-done.1
  40.9 6.0 %base_project.1 = (f32[40,640]{1,0:T(8,128)S(1)}, f32[40,640]{1,0:T(8,128)S(1)}) custom-call(s32[2]{0:T(128)S(1)} %pad_add_fusion.place_ref, s32[66]{0:T(128)S(1)} %copy-done.1, bf16[4,64,512]{2,1,0:T(8,128)(2,1)S(1)} %stack_band.1.h0_ref, bf16[4,64,512]{2,1,0:T(8,128)(2,1)S(1)} %collective-permute-done.3.up_ref.h1_ref, ...), custom_call_target="tpu_custom_call" | custom-call | flops 671000000 | bytes 11700000 | tf_op jit(solution)/shard_map/base_project/pallas_call | solution.py:271
  47.0 1.2 %collective-permute-start.8 = (f32[40,640]{1,0:T(8,128)S(1)}, f32[40,640]{1,0:T(8,128)S(1)}, u32[]{:S(2)}, u32[]{:S(2)}) collective-permute-start(f32[40,640]{1,0:T(8,128)S(1)} %get-tuple-element.42), channel_id=1, source_target_pairs={{0,1},{1,0},{2,3},{3,2},{4,5},{5,4},{6,7},{7,6},{8,9},{9,8},{10,11... | collective-permute-start | bytes 307208 | tf_op jit(solution)/shard_map/ppermute | solution.py:490
  48.4 4.5 %collective-permute-done.8.other_ref = f32[40,640]{1,0:T(8,128)S(1)} collective-permute-done((f32[40,640]{1,0:T(8,128)S(1)}, f32[40,640]{1,0:T(8,128)S(1)}, u32[]{:S(2)}, u32[]{:S(2)}) %collective-permute-start.8) | collective-permute-done | bytes 102432 | tf_op jit(solution)/shard_map/ppermute | solution.py:490
  53.0 2.2 %all-to-all-done.1.low_ref = f32[128,1,1280]{2,1,0:T(1,128)S(1)} async-done(((f32[128,1,1280]{2,1,0:T(1,128)}), f32[128,1,1280]{2,1,0:T(1,128)S(1)}, u32[]{:S(2)}, u32[]{:S(2)}) %all-to-all-start.1) | async-done | bytes 655392 | tf_op jit(solution)/shard_map/all_to_all | solution.py:486
  55.1 4.8 %attend_all.1 = (bf16[40,640]{1,0:T(8,128)(2,1)S(1)}, bf16[40,640]{1,0:T(8,128)(2,1)S(1)}) custom-call(s32[66]{0:T(128)S(1)} %copy-done.2, s32[1]{0:T(128)} %bitcast.5.parity_ref, s32[64]{0:T(128)S(1)} %copy-done.3, f32[128,1,1280]{2,1,0:T(1,128)S(1)} %all-to-all-done.1.low_ref, f32[40,640]{1,0:T(8,128)S(1)} %get-tuple-element.41.mine_ref, ...), custom_call_target="tpu_custom_call" | custom-call | flops 70000000 | bytes 1000000 | tf_op jit(solution)/shard_map/attend_all/pallas_call | solution.py:395
  60.4 3.7 %collective-permute-done.9.back_ref = bf16[40,640]{1,0:T(8,128)(2,1)S(1)} collective-permute-done((bf16[40,640]{1,0:T(8,128)(2,1)S(1)}, bf16[40,640]{1,0:T(8,128)(2,1)S(1)}, u32[]{:S(2)}, u32[]{:S(2)}) %collective-permute-start.9) | collective-permute-done | bytes 51232 | tf_op jit(solution)/shard_map/ppermute | solution.py:501
  64.1 1.3 %weave.1 = (bf16[64,512]{1,0:T(8,128)(2,1)}, bf16[64,64]{1,0:T(8,128)(2,1)}, bf16[64,64]{1,0:T(8,128)(2,1)}) custom-call(s32[66]{0:T(128)S(1)} %copy-done.2, s32[1]{0:T(128)} %bitcast.5.parity_ref, bf16[40,640]{1,0:T(8,128)(2,1)S(1)} %get-tuple-element.45.keep_ref, bf16[40,640]{1,0:T(8,128)(2,1)S(1)} %collective-permute-done.9.back_ref), custom_call_target="tpu_custom_call" | custom-call | tf_op jit(solution)/shard_map/weave/pallas_call | solution.py:440
  (25 shorter events, 1.5 us)
Async XLA Ops:
  0.6 10.7 %collective-permute-start = (bf16[64,512]{1,0:T(8,128)(2,1)}, bf16[64,512]{1,0:T(8,128)(2,1)S(1)}, u32[]{:S(2)}, u32[]{:S(2)}) collective-permute-start(bf16[64,512]{1,0:T(8,128)(2,1)} %hidden_hbm.1), channel_id=1, source_target_pairs={{0,1},{1,2},{2,3},{3,0},{4,5},{5,6},{6,7},{7,4},{8,9},{9,10},{10,1... | collective-permute-start | bytes 196616 | tf_op jit(solution)/shard_map/ppermute | solution.py:473
  2.7 8.6 %collective-permute-start.1 = (bf16[64,512]{1,0:T(8,128)(2,1)}, bf16[64,512]{1,0:T(8,128)(2,1)S(1)}, u32[]{:S(2)}, u32[]{:S(2)}) collective-permute-start(bf16[64,512]{1,0:T(8,128)(2,1)} %hidden_hbm.1), channel_id=1, source_target_pairs={{0,2},{1,3},{2,0},{3,1},{4,6},{5,7},{6,4},{7,5},{8,10},{9,11},{10,... | collective-permute-start | bytes 196616 | tf_op jit(solution)/shard_map/ppermute | solution.py:473
  6.3 5.0 %collective-permute-start.2 = (bf16[64,512]{1,0:T(8,128)(2,1)}, bf16[64,512]{1,0:T(8,128)(2,1)S(1)}, u32[]{:S(2)}, u32[]{:S(2)}) collective-permute-start(bf16[64,512]{1,0:T(8,128)(2,1)} %hidden_hbm.1), channel_id=1, source_target_pairs={{0,3},{1,0},{2,1},{3,2},{4,7},{5,4},{6,5},{7,6},{8,11},{9,8},{10,9... | collective-permute-start | bytes 196616 | tf_op jit(solution)/shard_map/ppermute | solution.py:473
  10.6 0.7 %copy-start.4 = (bf16[2,512,128]{2,1,0:T(8,128)(2,1)}, bf16[2,512,128]{2,1,0:T(8,128)(2,1)S(1)}, u32[]{:S(2)}) copy-start(bf16[2,512,128]{2,1,0:T(8,128)(2,1)S(1)} %get-tuple-element.32) | copy-start | bytes 786436
  11.3 0.6 copy-start
  11.9 11.6 %collective-permute-start.3 = (bf16[4,64,512]{2,1,0:T(8,128)(2,1)S(1)}, bf16[4,64,512]{2,1,0:T(8,128)(2,1)S(1)}, u32[]{:S(2)}, u32[]{:S(2)}) collective-permute-start(bf16[4,64,512]{2,1,0:T(8,128)(2,1)S(1)} %stack_band.1.h0_ref), channel_id=1, source_target_pairs={{0,4},{1,5},{2,6},{3,7},{4,8},{5,9},{6,10},{7,11},{8,12},{9,13},{1... | collective-permute-start | bytes 786440 | tf_op jit(solution)/shard_map/ppermute | solution.py:478
  13.6 10.0 %collective-permute-start.4 = (bf16[4,64,512]{2,1,0:T(8,128)(2,1)S(1)}, bf16[4,64,512]{2,1,0:T(8,128)(2,1)S(1)}, u32[]{:S(2)}, u32[]{:S(2)}) collective-permute-start(bf16[4,64,512]{2,1,0:T(8,128)(2,1)S(1)} %stack_band.1.h0_ref), channel_id=1, source_target_pairs={{0,12},{1,13},{2,14},{3,15},{4,0},{5,1},{6,2},{7,3},{8,4},{9,5},{1... | collective-permute-start | bytes 786440 | tf_op jit(solution)/shard_map/ppermute | solution.py:478
  16.3 15.2 %all-to-all-start = ((bf16[32,2,2176]{2,1,0:T(2,128)(2,1)}), bf16[32,2,2176]{2,1,0:T(2,128)(2,1)S(1)}, u32[]{:S(2)}, u32[]{:S(2)}) async-start(bf16[32,2,2176]{2,1,0:T(2,128)(2,1)} %send_rows.1), calls=%async_computation | async-start | bytes 557056 | tf_op jit(solution)/shard_map/all_to_all | solution.py:476
  22.4 11.0 %collective-permute-start.5 = (bf16[2,512,128]{2,1,0:T(8,128)(2,1)}, bf16[2,512,128]{2,1,0:T(8,128)(2,1)S(1)}, u32[]{:S(2)}, u32[]{:S(2)}) collective-permute-start(bf16[2,512,128]{2,1,0:T(8,128)(2,1)} %copy-done.4), channel_id=1, source_target_pairs={{0,1},{1,0},{2,3},{3,2},{4,5},{5,4},{6,7},{7,6},{8,9},{9,8},{10,11... | collective-permute-start | bytes 786440 | tf_op jit(solution)/shard_map/ppermute | solution.py:482
  24.2 9.2 %collective-permute-start.6 = (bf16[2,64,512]{2,1,0:T(8,128)(2,1)}, bf16[2,64,512]{2,1,0:T(8,128)(2,1)}, u32[]{:S(2)}, u32[]{:S(2)}) collective-permute-start(bf16[2,64,512]{2,1,0:T(8,128)(2,1)} %get-tuple-element.33), channel_id=1, source_target_pairs={{0,4},{1,5},{2,6},{3,7},{4,8},{5,9},{6,10},{7,11},{8,12},{9,13},{1... | collective-permute-start | bytes 393224 | tf_op jit(solution)/shard_map/ppermute | solution.py:481
  26.0 7.4 %collective-permute-start.7 = (bf16[2,64,512]{2,1,0:T(8,128)(2,1)}, bf16[2,64,512]{2,1,0:T(8,128)(2,1)}, u32[]{:S(2)}, u32[]{:S(2)}) collective-permute-start(bf16[2,64,512]{2,1,0:T(8,128)(2,1)} %get-tuple-element.34), channel_id=1, source_target_pairs={{0,12},{1,13},{2,14},{3,15},{4,0},{5,1},{6,2},{7,3},{8,4},{9,5},{1... | collective-permute-start | bytes 393224 | tf_op jit(solution)/shard_map/ppermute | solution.py:481
  33.4 21.7 %all-to-all-start.1 = ((f32[128,1,1280]{2,1,0:T(1,128)}), f32[128,1,1280]{2,1,0:T(1,128)S(1)}, u32[]{:S(2)}, u32[]{:S(2)}) async-start(f32[128,1,1280]{2,1,0:T(1,128)} %owner_low.1._), calls=%async_computation.1 | async-start | bytes 1310720 | tf_op jit(solution)/shard_map/all_to_all | solution.py:486
  40.3 0.7 %copy-start.1 = (s32[66]{0:T(128)S(1)}, s32[66]{0:T(128)}, u32[]{:S(2)}) copy-start(s32[66]{0:T(128)} %copy-done) | copy-start | bytes 796
  40.9 6.0 %copy-start.5 = (s32[64]{0:T(128)S(1)}, s32[64]{0:T(128)}, u32[]{:S(2)}) copy-start(s32[64]{0:T(128)} %param.21) | copy-start | bytes 772
  40.9 14.2 %copy-start.2 = (s32[66]{0:T(128)S(1)}, s32[66]{0:T(128)}, u32[]{:S(2)}) copy-start(s32[66]{0:T(128)} %copy-done) | copy-start | bytes 796
  40.9 14.2 %copy-start.3 = (s32[64]{0:T(128)S(1)}, s32[64]{0:T(128)}, u32[]{:S(2)}) copy-start(s32[64]{0:T(128)} %filled_ref.1) | copy-start | bytes 772
  47.0 6.0 %collective-permute-start.8 = (f32[40,640]{1,0:T(8,128)S(1)}, f32[40,640]{1,0:T(8,128)S(1)}, u32[]{:S(2)}, u32[]{:S(2)}) collective-permute-start(f32[40,640]{1,0:T(8,128)S(1)} %get-tuple-element.42), channel_id=1, source_target_pairs={{0,1},{1,0},{2,3},{3,2},{4,5},{5,4},{6,7},{7,6},{8,9},{9,8},{10,11... | collective-permute-start | bytes 307208 | tf_op jit(solution)/shard_map/ppermute | solution.py:490
  59.9 4.2 %collective-permute-start.9 = (bf16[40,640]{1,0:T(8,128)(2,1)S(1)}, bf16[40,640]{1,0:T(8,128)(2,1)S(1)}, u32[]{:S(2)}, u32[]{:S(2)}) collective-permute-start(bf16[40,640]{1,0:T(8,128)(2,1)S(1)} %get-tuple-element.46), channel_id=1, source_target_pairs={{0,1},{1,0},{2,3},{3,2},{4,5},{5,4},{6,7},{7,6},{8,9},{9,8},{10,11... | collective-permute-start | bytes 153608 | tf_op jit(solution)/shard_map/ppermute | solution.py:501

commit v6 on v5

--- a/solution.py
+++ b/solution.py
@@ -242,12 +242,14 @@
 
 
 def base_kernel(
-    place_ref, plan_ref, h0_ref, h1_ref, ha_ref, hb_ref, h3_ref, wq_hbm, wk_hbm, wv_hbm, _,
-    mine_ref, give_ref, wq_ref, wkv_ref, acc_ref, sems,
+    place_ref, plan_hbm, h0_ref, h1_ref, ha_ref, hb_ref, h3_ref, wq_hbm, wk_hbm, wv_hbm, _,
+    mine_ref, give_ref, wq_ref, wkv_ref, acc_ref, plan_ref, sems, plan_sem,
 ):
     y, z = place_ref[0], place_ref[1]
     rows = [(((y - a) & 3) * 4 + ((z - b) & 3)) * 512 for a in range(4) for b in range(4)]
     copies = weight_copies(rows, wq_hbm, wk_hbm, wv_hbm, wq_ref, wkv_ref, sems)
+    plan_copy = pltpu.make_async_copy(plan_hbm, plan_ref, plan_sem)
+    plan_copy.start()
     hiddens = [ref[b] for ref in (h0_ref, h1_ref) for b in range(4)]
     hiddens += [ha_ref[0], ha_ref[1], hb_ref[0], hb_ref[1]] + [h3_ref[b] for b in range(4)]
     q, kv = jnp.zeros((64, 512), F32), jnp.zeros((64, 128), F32)
@@ -262,6 +264,7 @@
         acc_ref[...] = q[:, cols] if c < 4 else kv
         even, odd = acc_ref[pl.ds(0, 32, 2), :], acc_ref[pl.ds(1, 32, 2), :]
         mine_ref[0:32, cols], give_ref[0:32, cols] = sides(parity, even, odd)
+    plan_copy.wait()
     row = pl.ds(plan_ref[65] >> 1, 1)
     mine_ref[32:40, :] = jnp.broadcast_to(give_ref[row, :], (8, 640))
     give_ref[32:40, :] = jnp.broadcast_to(mine_ref[row, :], (8, 640))
@@ -274,13 +277,15 @@
             jax.ShapeDtypeStruct((40, 640), F32),
             jax.ShapeDtypeStruct((40, 640), F32),
         ],
-        in_specs=[SMEM] * 2 + [VMEM] * 5 + [ANY] * 4,
+        in_specs=[SMEM, ANY] + [VMEM] * 5 + [ANY] * 4,
         out_specs=[VMEM] * 2,
         scratch_shapes=[
             pltpu.VMEM((16, 512, 512), BF16),
             pltpu.VMEM((16, 128, 512), BF16),
             pltpu.VMEM((64, 128), F32),
+            pltpu.SMEM((66,), jnp.int32),
             pltpu.SemaphoreType.DMA((3, 16)),
+            pltpu.SemaphoreType.DMA,
         ],
         cost_estimate=pl.CostEstimate(flops=671_000_000, bytes_accessed=11_700_000, transcendentals=0),
         compiler_params=pltpu.CompilerParams(vmem_limit_bytes=16 * 2**20),

time: 65.7 us -> 65.7 us (level)
  no operation moved by 1% of the time
where the time goes in v6:
time: 65.7 us; the launch traced here: 65.4 us
  starting transfers between devices  28.8 us (44%)
  Pallas kernels  19.6 us (30%)
  waiting for transfers between devices  14.5 us (22%)
  local copies, waits for them, and re-layouts  1.38 us (2%)
  between operations  0.76 us (1%)
    all_to_all x1, starting transfers between devices, local(): low = lax.all_to_all(low_sent, ROUTE, 0, 0, tiled=True)  6.76 us
    ppermute x3, starting transfers between devices, local(): lax.ppermute(hidden, 'tensor', z_turn(k))  6.66 us
    all_to_all x1, starting transfers between devices, local(): lax.all_to_all(sent, ('dp', 'tensor'), 0, 0, tiled=True, axis_index_group...  6.11 us
    pallas_call x1, Pallas kernels, base_project(): pl.pallas_call(base_kernel, out_shape=[jax.ShapeDtypeStruct((40, 640), F3...  6 us
    pallas_call x1, Pallas kernels, attend_all(): pl.pallas_call(attend_kernel, out_shape=[jax.ShapeDtypeStruct((40, 640),...  4.76 us
    ppermute x1, waiting for transfers between devices, local(): other = lax.ppermute(give, 'tensor', swap)  4.52 us
    all_to_all x1, waiting for transfers between devices, local(): lax.all_to_all(sent, ('dp', 'tensor'), 0, 0, tiled=True, axis_index_group...  4.05 us
    ppermute x1, waiting for transfers between devices, local(): back = lax.ppermute(give, 'tensor', swap)  3.69 us
  transfers between devices with their start and end apart: 12, of which 4 were waited for; matrix products, arithmetic and copies ran while one was open for 1% of the time, Pallas kernels for 20%

profile of v6, /device:TPU:0, one launch (start us, length us, event | category | flops | bytes accessed | tf_op | source)
XLA Modules:
  0.0 65.4 jit_solution(14734245649950837028)
XLA Ops:
  0.6 2.1 %collective-permute-start = (bf16[64,512]{1,0:T(8,128)(2,1)}, bf16[64,512]{1,0:T(8,128)(2,1)S(1)}, u32[]{:S(2)}, u32[]{:S(2)}) collective-permute-start(bf16[64,512]{1,0:T(8,128)(2,1)} %hidden_hbm.1), channel_id=1, source_target_pairs={{0,1},{1,2},{2,3},{3,0},{4,5},{5,6},{6,7},{7,4},{8,9},{9,10},{10,1... | collective-permute-start | bytes 196616 | tf_op jit(solution)/shard_map/ppermute | solution.py:478
  2.7 3.6 %collective-permute-start.1 = (bf16[64,512]{1,0:T(8,128)(2,1)}, bf16[64,512]{1,0:T(8,128)(2,1)S(1)}, u32[]{:S(2)}, u32[]{:S(2)}) collective-permute-start(bf16[64,512]{1,0:T(8,128)(2,1)} %hidden_hbm.1), channel_id=1, source_target_pairs={{0,2},{1,3},{2,0},{3,1},{4,6},{5,7},{6,4},{7,5},{8,10},{9,11},{10,... | collective-permute-start | bytes 196616 | tf_op jit(solution)/shard_map/ppermute | solution.py:478
  6.3 1.0 %collective-permute-start.2 = (bf16[64,512]{1,0:T(8,128)(2,1)}, bf16[64,512]{1,0:T(8,128)(2,1)S(1)}, u32[]{:S(2)}, u32[]{:S(2)}) collective-permute-start(bf16[64,512]{1,0:T(8,128)(2,1)} %hidden_hbm.1), channel_id=1, source_target_pairs={{0,3},{1,0},{2,1},{3,2},{4,7},{5,4},{6,5},{7,6},{8,11},{9,8},{10,9... | collective-permute-start | bytes 196616 | tf_op jit(solution)/shard_map/ppermute | solution.py:478
  7.3 3.3 %make_plan.1 = (s32[66]{0:T(128)S(1)}, f32[64,128]{1,0:T(8,128)S(1)}, f32[64,128]{1,0:T(8,128)S(1)}, bf16[96,8192]{1,0:T(8,128)(2,1)S(1)}, bf16[32,10240]{1,0:T(...) custom-call(s32[1]{0:T(128)} %bitcast.z_ref, s32[1,63]{1,0:T(1,128)} %requests_hbm.1, ...), custom_call_target="tpu_custom_call" | custom-call | flops 1000000 | bytes 500000 | tf_op jit(solution)/shard_map/make_plan/pallas_call | solution.py:88
  10.6 0.7 %copy-done.4 = bf16[2,512,128]{2,1,0:T(8,128)(2,1)} copy-done((bf16[2,512,128]{2,1,0:T(8,128)(2,1)}, bf16[2,512,128]{2,1,0:T(8,128)(2,1)S(1)}, u32[]{:S(2)}) %copy-start.4) | copy-done | bytes 262168
  11.9 1.6 %collective-permute-start.3 = (bf16[4,64,512]{2,1,0:T(8,128)(2,1)S(1)}, bf16[4,64,512]{2,1,0:T(8,128)(2,1)S(1)}, u32[]{:S(2)}, u32[]{:S(2)}) collective-permute-start(bf16[4,64,512]{2,1,0:T(8,128)(2,1)S(1)} %stack_band.1.h0_ref), channel_id=1, source_target_pairs={{0,4},{1,5},{2,6},{3,7},{4,8},{5,9},{6,10},{7,11},{8,12},{9,13},{1... | collective-permute-start | bytes 786440 | tf_op jit(solution)/shard_map/ppermute | solution.py:483
  13.6 1.7 %collective-permute-start.4 = (bf16[4,64,512]{2,1,0:T(8,128)(2,1)S(1)}, bf16[4,64,512]{2,1,0:T(8,128)(2,1)S(1)}, u32[]{:S(2)}, u32[]{:S(2)}) collective-permute-start(bf16[4,64,512]{2,1,0:T(8,128)(2,1)S(1)} %stack_band.1.h0_ref), channel_id=1, source_target_pairs={{0,12},{1,13},{2,14},{3,15},{4,0},{5,1},{6,2},{7,3},{8,4},{9,5},{1... | collective-permute-start | bytes 786440 | tf_op jit(solution)/shard_map/ppermute | solution.py:483
  15.2 1.1 %send_rows.1 = bf16[32,2,2176]{2,1,0:T(2,128)(2,1)} custom-call(f32[64,128]{1,0:T(8,128)S(1)} %get-tuple-element.26.spread_ref, f32[64,128]{1,0:T(8,128)S(1)} %get-tuple-element.27.code_ref, bf16[64,512]{1,0:T(8,128)(2,1)S(1)} %get-tuple-element.28.h0_ref, bf16[64,512]{1,0:T(8,128)(2,1)S(1)} %collective-permute-done.h1_ref, ...), custom_call_target="tpu_custom_call" | custom-call | flops 1000000 | bytes 500000 | tf_op jit(solution)/shard_map/send_rows/pallas_call | solution.py:123
  16.3 6.1 %all-to-all-start = ((bf16[32,2,2176]{2,1,0:T(2,128)(2,1)}), bf16[32,2,2176]{2,1,0:T(2,128)(2,1)S(1)}, u32[]{:S(2)}, u32[]{:S(2)}) async-start(bf16[32,2,2176]{2,1,0:T(2,128)(2,1)} %send_rows.1), calls=%async_computation | async-start | bytes 557056 | tf_op jit(solution)/shard_map/all_to_all | solution.py:481
  22.4 1.1 %collective-permute-start.5 = (bf16[2,512,128]{2,1,0:T(8,128)(2,1)}, bf16[2,512,128]{2,1,0:T(8,128)(2,1)S(1)}, u32[]{:S(2)}, u32[]{:S(2)}) collective-permute-start(bf16[2,512,128]{2,1,0:T(8,128)(2,1)} %copy-done.4), channel_id=1, source_target_pairs={{0,1},{1,0},{2,3},{3,2},{4,5},{5,4},{6,7},{7,6},{8,9},{9,8},{10,11... | collective-permute-start | bytes 786440 | tf_op jit(solution)/shard_map/ppermute | solution.py:487
  23.5 0.7 %take_halves.1 = (bf16[2,64,512]{2,1,0:T(8,128)(2,1)}, bf16[2,64,512]{2,1,0:T(8,128)(2,1)}) custom-call(bf16[4,64,512]{2,1,0:T(8,128)(2,1)S(1)} %collective-permute-done.3.up_ref.h1_ref, bf16[4,64,512]{2,1,0:T(8,128)(2,1)S(1)} %collective-permute-done.4.down_ref.h3_ref), custom_call_target="tpu_custom_call" | custom-call | flops 1000 | bytes 500000 | tf_op jit(solution)/shard_map/take_halves/pallas_call | solution.py:157
  24.2 1.8 %collective-permute-start.6 = (bf16[2,64,512]{2,1,0:T(8,128)(2,1)}, bf16[2,64,512]{2,1,0:T(8,128)(2,1)}, u32[]{:S(2)}, u32[]{:S(2)}) collective-permute-start(bf16[2,64,512]{2,1,0:T(8,128)(2,1)} %get-tuple-element.33), channel_id=1, source_target_pairs={{0,4},{1,5},{2,6},{3,7},{4,8},{5,9},{6,10},{7,11},{8,12},{9,13},{1... | collective-permute-start | bytes 393224 | tf_op jit(solution)/shard_map/ppermute | solution.py:486
  26.0 1.4 %collective-permute-start.7 = (bf16[2,64,512]{2,1,0:T(8,128)(2,1)}, bf16[2,64,512]{2,1,0:T(8,128)(2,1)}, u32[]{:S(2)}, u32[]{:S(2)}) collective-permute-start(bf16[2,64,512]{2,1,0:T(8,128)(2,1)} %get-tuple-element.34), channel_id=1, source_target_pairs={{0,12},{1,13},{2,14},{3,15},{4,0},{5,1},{6,2},{7,3},{8,4},{9,5},{1... | collective-permute-start | bytes 393224 | tf_op jit(solution)/shard_map/ppermute | solution.py:486
  27.5 4.1 %all-to-all-done.recv_ref = bf16[32,2,2176]{2,1,0:T(2,128)(2,1)S(1)} async-done(((bf16[32,2,2176]{2,1,0:T(2,128)(2,1)}), bf16[32,2,2176]{2,1,0:T(2,128)(2,1)S(1)}, u32[]{:S(2)}, u32[]{:S(2)}) %all-to-all-start) | async-done | bytes 278560 | tf_op jit(solution)/shard_map/all_to_all | solution.py:481
  31.5 1.9 %owner_low.1._ = f32[128,1,1280]{2,1,0:T(1,128)} custom-call(s32[1]{0:T(128)} %bitcast.z_ref, bf16[32,2,2176]{2,1,0:T(2,128)(2,1)S(1)} %all-to-all-done.recv_ref, bf16[96,8192]{1,0:T(8,128)(2,1)S(1)} %get-tuple-element.30.down_ref, bf16[32,10240]{1,0:T(8,128)(2,1)S(1)} %get-tuple-element.31.up_ref), custom_call_target="tpu_custom_call" | custom-call | flops 40000000 | bytes 3400000 | tf_op jit(solution)/shard_map/owner_low/pallas_call | solution.py:203
  33.4 6.8 %all-to-all-start.1 = ((f32[128,1,1280]{2,1,0:T(1,128)}), f32[128,1,1280]{2,1,0:T(1,128)S(1)}, u32[]{:S(2)}, u32[]{:S(2)}) async-start(f32[128,1,1280]{2,1,0:T(1,128)} %owner_low.1._), calls=%async_computation.1 | async-start | bytes 1310720 | tf_op jit(solution)/shard_map/all_to_all | solution.py:491
  40.3 0.7 copy-done.1
  40.9 6.0 %base_project.1 = (f32[40,640]{1,0:T(8,128)S(1)}, f32[40,640]{1,0:T(8,128)S(1)}) custom-call(s32[2]{0:T(128)S(1)} %pad_add_fusion.place_ref, s32[66]{0:T(128)S(1)} %copy-done.1, bf16[4,64,512]{2,1,0:T(8,128)(2,1)S(1)} %stack_band.1.h0_ref, bf16[4,64,512]{2,1,0:T(8,128)(2,1)S(1)} %collective-permute-done.3.up_ref.h1_ref, ...), custom_call_target="tpu_custom_call" | custom-call | flops 671000000 | bytes 11700000 | tf_op jit(solution)/shard_map/base_project/pallas_call | solution.py:274
  47.0 1.2 %collective-permute-start.8 = (f32[40,640]{1,0:T(8,128)S(1)}, f32[40,640]{1,0:T(8,128)S(1)}, u32[]{:S(2)}, u32[]{:S(2)}) collective-permute-start(f32[40,640]{1,0:T(8,128)S(1)} %get-tuple-element.42), channel_id=1, source_target_pairs={{0,1},{1,0},{2,3},{3,2},{4,5},{5,4},{6,7},{7,6},{8,9},{9,8},{10,11... | collective-permute-start | bytes 307208 | tf_op jit(solution)/shard_map/ppermute | solution.py:495
  48.4 4.5 %collective-permute-done.8.other_ref = f32[40,640]{1,0:T(8,128)S(1)} collective-permute-done((f32[40,640]{1,0:T(8,128)S(1)}, f32[40,640]{1,0:T(8,128)S(1)}, u32[]{:S(2)}, u32[]{:S(2)}) %collective-permute-start.8) | collective-permute-done | bytes 102432 | tf_op jit(solution)/shard_map/ppermute | solution.py:495
  53.0 2.2 %all-to-all-done.1.low_ref = f32[128,1,1280]{2,1,0:T(1,128)S(1)} async-done(((f32[128,1,1280]{2,1,0:T(1,128)}), f32[128,1,1280]{2,1,0:T(1,128)S(1)}, u32[]{:S(2)}, u32[]{:S(2)}) %all-to-all-start.1) | async-done | bytes 655392 | tf_op jit(solution)/shard_map/all_to_all | solution.py:491
  55.1 4.8 %attend_all.1 = (bf16[40,640]{1,0:T(8,128)(2,1)S(1)}, bf16[40,640]{1,0:T(8,128)(2,1)S(1)}) custom-call(s32[66]{0:T(128)S(1)} %copy-done.2, s32[1]{0:T(128)} %bitcast.5.parity_ref, s32[64]{0:T(128)S(1)} %copy-done.3, f32[128,1,1280]{2,1,0:T(1,128)S(1)} %all-to-all-done.1.low_ref, f32[40,640]{1,0:T(8,128)S(1)} %get-tuple-element.41.mine_ref, ...), custom_call_target="tpu_custom_call" | custom-call | flops 70000000 | bytes 1000000 | tf_op jit(solution)/shard_map/attend_all/pallas_call | solution.py:400
  60.4 3.7 %collective-permute-done.9.back_ref = bf16[40,640]{1,0:T(8,128)(2,1)S(1)} collective-permute-done((bf16[40,640]{1,0:T(8,128)(2,1)S(1)}, bf16[40,640]{1,0:T(8,128)(2,1)S(1)}, u32[]{:S(2)}, u32[]{:S(2)}) %collective-permute-start.9) | collective-permute-done | bytes 51232 | tf_op jit(solution)/shard_map/ppermute | solution.py:506
  64.1 1.3 %weave.1 = (bf16[64,512]{1,0:T(8,128)(2,1)}, bf16[64,64]{1,0:T(8,128)(2,1)}, bf16[64,64]{1,0:T(8,128)(2,1)}) custom-call(s32[66]{0:T(128)S(1)} %copy-done.2, s32[1]{0:T(128)} %bitcast.5.parity_ref, bf16[40,640]{1,0:T(8,128)(2,1)S(1)} %get-tuple-element.45.keep_ref, bf16[40,640]{1,0:T(8,128)(2,1)S(1)} %collective-permute-done.9.back_ref), custom_call_target="tpu_custom_call" | custom-call | tf_op jit(solution)/shard_map/weave/pallas_call | solution.py:445
  (25 shorter events, 1.5 us)
Async XLA Ops:
  0.6 10.7 %collective-permute-start = (bf16[64,512]{1,0:T(8,128)(2,1)}, bf16[64,512]{1,0:T(8,128)(2,1)S(1)}, u32[]{:S(2)}, u32[]{:S(2)}) collective-permute-start(bf16[64,512]{1,0:T(8,128)(2,1)} %hidden_hbm.1), channel_id=1, source_target_pairs={{0,1},{1,2},{2,3},{3,0},{4,5},{5,6},{6,7},{7,4},{8,9},{9,10},{10,1... | collective-permute-start | bytes 196616 | tf_op jit(solution)/shard_map/ppermute | solution.py:478
  2.7 8.6 %collective-permute-start.1 = (bf16[64,512]{1,0:T(8,128)(2,1)}, bf16[64,512]{1,0:T(8,128)(2,1)S(1)}, u32[]{:S(2)}, u32[]{:S(2)}) collective-permute-start(bf16[64,512]{1,0:T(8,128)(2,1)} %hidden_hbm.1), channel_id=1, source_target_pairs={{0,2},{1,3},{2,0},{3,1},{4,6},{5,7},{6,4},{7,5},{8,10},{9,11},{10,... | collective-permute-start | bytes 196616 | tf_op jit(solution)/shard_map/ppermute | solution.py:478
  6.3 5.0 %collective-permute-start.2 = (bf16[64,512]{1,0:T(8,128)(2,1)}, bf16[64,512]{1,0:T(8,128)(2,1)S(1)}, u32[]{:S(2)}, u32[]{:S(2)}) collective-permute-start(bf16[64,512]{1,0:T(8,128)(2,1)} %hidden_hbm.1), channel_id=1, source_target_pairs={{0,3},{1,0},{2,1},{3,2},{4,7},{5,4},{6,5},{7,6},{8,11},{9,8},{10,9... | collective-permute-start | bytes 196616 | tf_op jit(solution)/shard_map/ppermute | solution.py:478
  10.6 0.7 %copy-start.4 = (bf16[2,512,128]{2,1,0:T(8,128)(2,1)}, bf16[2,512,128]{2,1,0:T(8,128)(2,1)S(1)}, u32[]{:S(2)}) copy-start(bf16[2,512,128]{2,1,0:T(8,128)(2,1)S(1)} %get-tuple-element.32) | copy-start | bytes 786436
  11.3 0.6 copy-start
  11.9 11.6 %collective-permute-start.3 = (bf16[4,64,512]{2,1,0:T(8,128)(2,1)S(1)}, bf16[4,64,512]{2,1,0:T(8,128)(2,1)S(1)}, u32[]{:S(2)}, u32[]{:S(2)}) collective-permute-start(bf16[4,64,512]{2,1,0:T(8,128)(2,1)S(1)} %stack_band.1.h0_ref), channel_id=1, source_target_pairs={{0,4},{1,5},{2,6},{3,7},{4,8},{5,9},{6,10},{7,11},{8,12},{9,13},{1... | collective-permute-start | bytes 786440 | tf_op jit(solution)/shard_map/ppermute | solution.py:483
  13.6 10.0 %collective-permute-start.4 = (bf16[4,64,512]{2,1,0:T(8,128)(2,1)S(1)}, bf16[4,64,512]{2,1,0:T(8,128)(2,1)S(1)}, u32[]{:S(2)}, u32[]{:S(2)}) collective-permute-start(bf16[4,64,512]{2,1,0:T(8,128)(2,1)S(1)} %stack_band.1.h0_ref), channel_id=1, source_target_pairs={{0,12},{1,13},{2,14},{3,15},{4,0},{5,1},{6,2},{7,3},{8,4},{9,5},{1... | collective-permute-start | bytes 786440 | tf_op jit(solution)/shard_map/ppermute | solution.py:483
  16.3 15.2 %all-to-all-start = ((bf16[32,2,2176]{2,1,0:T(2,128)(2,1)}), bf16[32,2,2176]{2,1,0:T(2,128)(2,1)S(1)}, u32[]{:S(2)}, u32[]{:S(2)}) async-start(bf16[32,2,2176]{2,1,0:T(2,128)(2,1)} %send_rows.1), calls=%async_computation | async-start | bytes 557056 | tf_op jit(solution)/shard_map/all_to_all | solution.py:481
  22.4 11.0 %collective-permute-start.5 = (bf16[2,512,128]{2,1,0:T(8,128)(2,1)}, bf16[2,512,128]{2,1,0:T(8,128)(2,1)S(1)}, u32[]{:S(2)}, u32[]{:S(2)}) collective-permute-start(bf16[2,512,128]{2,1,0:T(8,128)(2,1)} %copy-done.4), channel_id=1, source_target_pairs={{0,1},{1,0},{2,3},{3,2},{4,5},{5,4},{6,7},{7,6},{8,9},{9,8},{10,11... | collective-permute-start | bytes 786440 | tf_op jit(solution)/shard_map/ppermute | solution.py:487
  24.2 9.2 %collective-permute-start.6 = (bf16[2,64,512]{2,1,0:T(8,128)(2,1)}, bf16[2,64,512]{2,1,0:T(8,128)(2,1)}, u32[]{:S(2)}, u32[]{:S(2)}) collective-permute-start(bf16[2,64,512]{2,1,0:T(8,128)(2,1)} %get-tuple-element.33), channel_id=1, source_target_pairs={{0,4},{1,5},{2,6},{3,7},{4,8},{5,9},{6,10},{7,11},{8,12},{9,13},{1... | collective-permute-start | bytes 393224 | tf_op jit(solution)/shard_map/ppermute | solution.py:486
  26.0 7.4 %collective-permute-start.7 = (bf16[2,64,512]{2,1,0:T(8,128)(2,1)}, bf16[2,64,512]{2,1,0:T(8,128)(2,1)}, u32[]{:S(2)}, u32[]{:S(2)}) collective-permute-start(bf16[2,64,512]{2,1,0:T(8,128)(2,1)} %get-tuple-element.34), channel_id=1, source_target_pairs={{0,12},{1,13},{2,14},{3,15},{4,0},{5,1},{6,2},{7,3},{8,4},{9,5},{1... | collective-permute-start | bytes 393224 | tf_op jit(solution)/shard_map/ppermute | solution.py:486
  33.4 21.7 %all-to-all-start.1 = ((f32[128,1,1280]{2,1,0:T(1,128)}), f32[128,1,1280]{2,1,0:T(1,128)S(1)}, u32[]{:S(2)}, u32[]{:S(2)}) async-start(f32[128,1,1280]{2,1,0:T(1,128)} %owner_low.1._), calls=%async_computation.1 | async-start | bytes 1310720 | tf_op jit(solution)/shard_map/all_to_all | solution.py:491
  40.3 0.7 %copy-start.1 = (s32[66]{0:T(128)S(1)}, s32[66]{0:T(128)}, u32[]{:S(2)}) copy-start(s32[66]{0:T(128)} %copy-done) | copy-start | bytes 796
  40.9 6.0 %copy-start.5 = (s32[64]{0:T(128)S(1)}, s32[64]{0:T(128)}, u32[]{:S(2)}) copy-start(s32[64]{0:T(128)} %param.21) | copy-start | bytes 772
  40.9 14.2 %copy-start.2 = (s32[66]{0:T(128)S(1)}, s32[66]{0:T(128)}, u32[]{:S(2)}) copy-start(s32[66]{0:T(128)} %copy-done) | copy-start | bytes 796
  40.9 14.2 %copy-start.3 = (s32[64]{0:T(128)S(1)}, s32[64]{0:T(128)}, u32[]{:S(2)}) copy-start(s32[64]{0:T(128)} %filled_ref.1) | copy-start | bytes 772
  47.0 6.0 %collective-permute-start.8 = (f32[40,640]{1,0:T(8,128)S(1)}, f32[40,640]{1,0:T(8,128)S(1)}, u32[]{:S(2)}, u32[]{:S(2)}) collective-permute-start(f32[40,640]{1,0:T(8,128)S(1)} %get-tuple-element.42), channel_id=1, source_target_pairs={{0,1},{1,0},{2,3},{3,2},{4,5},{5,4},{6,7},{7,6},{8,9},{9,8},{10,11... | collective-permute-start | bytes 307208 | tf_op jit(solution)/shard_map/ppermute | solution.py:495
  59.9 4.2 %collective-permute-start.9 = (bf16[40,640]{1,0:T(8,128)(2,1)S(1)}, bf16[40,640]{1,0:T(8,128)(2,1)S(1)}, u32[]{:S(2)}, u32[]{:S(2)}) collective-permute-start(bf16[40,640]{1,0:T(8,128)(2,1)S(1)} %get-tuple-element.46), channel_id=1, source_target_pairs={{0,1},{1,0},{2,3},{3,2},{4,5},{5,4},{6,7},{7,6},{8,9},{9,8},{10,11... | collective-permute-start | bytes 153608 | tf_op jit(solution)/shard_map/ppermute | solution.py:506
